TPU v7x, 32 devices: a whole 2x2x4 slice. The times are simulated.
32 devices in a mesh: section: 4 (over x, core), tensor: 2 (over y), dp: 4 (over z).
Axes of the slice: x: 2, y: 2, z: 4, core: 2. Of those that a mesh axis runs over, the one named last changes fastest.
Arguments:
- hidden_in: bfloat16 [1, 512, 16384], P(None, 'dp', 'tensor'), may hold values from -6 to 6
- norm_gain: bfloat16 [4, 16384], P('section', 'tensor'), may hold values from 0.099609375 to 1.8984375
- trainer_kv: bfloat16 [4, 16384, 2048], P('section', ('tensor', 'dp')), may hold values from -0.046875 to 0.046875
- queries: bfloat16 [4, 1, 512, 16384], P('section', None, 'dp', 'tensor'), may hold values from -120 to 120
- kv_cache: bfloat16 [4, 1, 512, 16, 4096], P('section', None, 'dp', None, 'tensor'), may hold values from -4 to 4, as said below
- cache_lengths: int32 [1, 512], P(None, 'dp'), may hold values from 1 to 16, as said below
Outputs:
- rollout_kv: bfloat16 [4, 16384, 2048], P('section', None, 'tensor')
- section_out: bfloat16 [4, 1, 512, 16384], P('section', None, 'dp', 'tensor')
Inputs may be any that keep to these rules, and one draw needn't show every extreme that they name: `kv_cache`: the two copies c = 0 and c = 1 of each head's keys and values are equal. `cache_lengths`: valid cache positions of each row; in every aligned block of 128 rows one row has 16 and one has 1.
All inputs are finite; a program needn't handle non-finite values.
Results may differ from a plain program's by a relative error of at most 0.0035.
The roundings to bfloat16 on the way count: a program that leaves them out, or rounds other values in their place, can miss the bound.
Values may be sent and summed in bfloat16 or wider, within the bound.
No kernel may reach another device: no remote copies, remote signals or barrier semaphores. Data moves between devices by JAX's collectives and lax.ppermute only.
A program may use at most 384 MiB of HBM per device.

v0:
```python
import functools

import jax
import jax.numpy as jnp
from jax import lax
from jax.experimental import pallas as pl
from jax.experimental.pallas import tpu as pltpu
from jax.sharding import PartitionSpec as P

D = 16384
KVH = 8
HD = 128
GQ = 16
GROUP = 128
LMAX = 16
HALF = GQ // 2
PAIR = 2 * HD
ROW_TILE = 16

epsilon = 1e-05
clip_ratio = 2.0
FAR, RELAYED = 4, 5
FIXED = 4
VMEM = 60 << 20
SHORT = pl.CostEstimate(flops=0, bytes_accessed=0, transcendentals=0)


def requantize_kernel(column_ref, w_ref, o_ref):
    ones = jnp.ones((ROW_TILE, GROUP), jnp.bfloat16)
    for start in range(0, w_ref.shape[0], GROUP):
        block = w_ref[start : start + GROUP, :]
        total = jnp.dot(ones, jnp.abs(block), preferred_element_type=jnp.float32)[:1]
        limit = (total * (clip_ratio / GROUP)).astype(jnp.bfloat16)
        o_ref[start : start + GROUP, :] = jnp.minimum(jnp.maximum(block, -limit), limit)


def requantize(weight, indices, own_width, width):
    rows = weight.shape[0]
    tile = min(rows, 4 * GROUP)
    return [
        pl.pallas_call(
            requantize_kernel,
            out_shape=jax.ShapeDtypeStruct((rows, width), jnp.bfloat16),
            grid_spec=pltpu.PrefetchScalarGridSpec(
                num_scalar_prefetch=1,
                grid=(rows // tile,),
                in_specs=[pl.BlockSpec((tile, width), lambda i, column: (i, column[0]))],
                out_specs=pl.BlockSpec((tile, width), lambda i, column: (i, 0)),
            ),
            compiler_params=pltpu.CompilerParams(vmem_limit_bytes=VMEM),
            cost_estimate=SHORT,
        )((index * own_width // width).reshape(1), weight)
        for index in indices
    ]


def project_kernel(layout, lhs_count, has_total, has_held, placed, where_ref, *refs):
    lhs = refs[:lhs_count]
    blocks = refs[lhs_count : lhs_count + len(layout)]
    rest = list(refs[lhs_count + len(layout) :])
    total_ref = rest.pop(0) if has_total else None
    if has_held:
        rest.pop(0)
    o_ref = rest.pop(0)
    segments = [(n, *segment) for n, (_, of_block) in enumerate(layout) for segment in of_block]

    def copy(i):
        n, _, start, depth = segments[i]
        out, sems = rest
        width = min(out.shape[1], o_ref.shape[1])
        rows = pl.ds(pl.multiple_of(where_ref[FIXED + len(layout) + 2 * i + 1], GROUP), depth)
        columns = pl.ds(pl.multiple_of(pl.program_id(0) * width, HD), width)
        source = blocks[n].at[pl.ds(start, depth)]
        if width < blocks[n].shape[1]:
            source = blocks[n].at[pl.ds(start, depth), pl.ds(pl.multiple_of(where_ref[2], HD), width)]
        return pltpu.make_async_copy(source, out.at[rows, columns], sems.at[i])

    def add(which):
        total = o_ref[...]
        for i in which:
            n, j, start, depth = segments[i]
            columns = pl.ds(pl.multiple_of(where_ref[FIXED + len(layout) + 2 * i], GROUP), depth)
            rows = blocks[n][start : start + depth, :]
            total += jnp.dot(lhs[j][:, columns], rows, preferred_element_type=jnp.float32)
        o_ref[...] = total

    def start(which):
        for i in which:
            copy(i).start()

    def wait(which):
        for i in which:
            copy(i).wait()

    groups = [(None, [i for i, segment in enumerate(segments) if not layout[segment[0]][0]])]
    for n, (gated, _) in enumerate(layout):
        if gated:
            groups.append((n, [i for i, segment in enumerate(segments) if segment[0] == n]))

    for n, which in groups:
        has = 1 if n is None else where_ref[FIXED + n]

        if placed and which:
            pl.when(where_ref[1] * has == 1)(functools.partial(start, which))

    o_ref[...] = total_ref[...] if has_total else jnp.zeros(o_ref.shape, jnp.float32)
    for n, which in groups:
        if which:
            has = 1 if n is None else where_ref[FIXED + n]
            pl.when(where_ref[0] * has == 1)(functools.partial(add, which))

    for n, which in groups:
        has = 1 if n is None else where_ref[FIXED + n]

        if placed and which:
            pl.when(where_ref[1] * has == 1)(functools.partial(wait, which))


def project(active, lhs, terms, total=None, placing=None, rollout=None):
    used = sorted({segment[0] for _, _, segments in terms for segment in segments})
    lhs = [lhs[j] for j in used]
    rows = lhs[0].shape[0]
    served = terms[0][0].shape[1]
    tile = min(served, 256)
    places, first_column, width = placing or (0, 0, 0)
    where = [active, places, first_column, active | places]
    where += [1 if has is None else has for _, has, _ in terms]
    for _, _, segments in terms:
        for _, offset, row, _, _ in segments:
            where += [offset, row]
    layout = [
        (has is not None, [(used.index(j), start, depth) for j, _, _, start, depth in segments])
        for _, has, segments in terms
    ]
    count = sum(len(segments) for _, segments in layout)
    added = () if total is None else (total,)
    held = () if rollout is None else (rollout,)
    column = lambda i, where: (0, i)

    def read(n):
        return lambda i, where: (0, i * where[3] * where[FIXED + n])

    anywhere = pl.BlockSpec(memory_space=pl.ANY)
    fresh_shape, fresh_spec = jax.ShapeDtypeStruct((rows, served), jnp.float32), pl.BlockSpec((rows, tile), column)
    placed = int(placing is not None)
    return pl.pallas_call(
        functools.partial(project_kernel, layout, len(lhs), bool(added), bool(held), placed),
        out_shape=[fresh_shape, jax.ShapeDtypeStruct((D, width), jnp.bfloat16)] if placing else fresh_shape,
        grid_spec=pltpu.PrefetchScalarGridSpec(
            num_scalar_prefetch=1,
            grid=(served // tile,),
            in_specs=[pl.BlockSpec(part.shape, lambda i, where: (0, 0)) for part in lhs]
            + [pl.BlockSpec((term[0].shape[0], tile), read(n)) for n, term in enumerate(terms)]
            + [fresh_spec for _ in added]
            + [anywhere for _ in held],
            out_specs=[fresh_spec, anywhere] if placing else fresh_spec,
            scratch_shapes=[pltpu.SemaphoreType.DMA((count,))] if placing else [],
        ),
        input_output_aliases={1 + len(lhs) + len(terms) + len(added): 1} if held else {},
        compiler_params=pltpu.CompilerParams(vmem_limit_bytes=VMEM),
        cost_estimate=SHORT,
    )(jnp.stack([jnp.asarray(v, jnp.int32) for v in where]), *lhs, *[term[0] for term in terms], *added, *held)


def attend_kernel(share, active_ref, bias_ref, x_ref, q_ref, c_ref, f_ref, held_ref, o_ref):
    heads = share * HALF
    scale = HD ** (-0.5)

    @pl.when((active_ref[0] == 0) & (pl.program_id(0) == 0))
    def _():
        o_ref[...] = held_ref[...]

    @pl.when(active_ref[0] == 1)
    def _():
        bias = jnp.concatenate([bias_ref[0]] * heads, axis=0)
        for g in range(q_ref.shape[1] // (heads * HD)):
            lanes = [slice((g * heads + i) * HD, (g * heads + i + 1) * HD) for i in range(heads)]
            query = jnp.concatenate([q_ref[:, lane] for lane in lanes], axis=0)
            at = g * share * PAIR
            keys = c_ref[:, :, at : at + HD].reshape(ROW_TILE * LMAX, HD)
            values = c_ref[:, :, at + HD : at + PAIR].reshape(ROW_TILE * LMAX, HD)
            fresh = f_ref[:, g * PAIR : (g + 1) * PAIR].astype(jnp.bfloat16).astype(jnp.float32)
            new_key = jnp.concatenate([fresh[:, :HD]] * heads, axis=0)
            new_value = jnp.concatenate([fresh[:, HD:]] * heads, axis=0)
            old = lax.dot_general(query, keys, (((1,), (1,)), ((), ())), preferred_element_type=jnp.float32)
            old = old * scale + bias
            new = jnp.sum(query.astype(jnp.float32) * new_key, axis=1, keepdims=True) * scale
            highest = jnp.maximum(jnp.max(old, axis=1, keepdims=True), new)
            old = jnp.exp(old - highest)
            new = jnp.exp(new - highest)
            inverse = 1.0 / (jnp.sum(old, axis=1, keepdims=True) + new)
            old = (old * inverse).astype(jnp.bfloat16)
            new = (new * inverse).astype(jnp.bfloat16).astype(jnp.float32)
            mixed = jnp.dot(old, values, preferred_element_type=jnp.float32) + new * new_value
            for i, lane in enumerate(lanes):
                total = x_ref[:, lane].astype(jnp.float32) + mixed[i * ROW_TILE : (i + 1) * ROW_TILE, :]
                o_ref[:, lane] = total.astype(jnp.bfloat16)


def seen_bias(lengths):
    column = jnp.arange(ROW_TILE * LMAX)
    own = jnp.arange(ROW_TILE)[:, None] == column[None, :] // LMAX
    seen = own[None] & ((column % LMAX)[None, None, :] < lengths.reshape(-1, ROW_TILE, 1))
    return jnp.where(seen, 0.0, -jnp.inf).astype(jnp.float32)


def attend(active, current, query, cache, bias, fresh, held):
    rows, width = query.shape
    share = min(2, width // (HALF * HD))
    wide = pl.BlockSpec((ROW_TILE, width), lambda i, active: (i * active[0], 0))
    return pl.pallas_call(
        functools.partial(attend_kernel, share),
        out_shape=jax.ShapeDtypeStruct((rows, width), jnp.bfloat16),
        grid_spec=pltpu.PrefetchScalarGridSpec(
            num_scalar_prefetch=1,
            grid=(rows // ROW_TILE,),
            in_specs=[
                pl.BlockSpec((1, *bias.shape[1:]), lambda i, active: (i * active[0], 0, 0)),
                wide,
                wide,
                pl.BlockSpec((ROW_TILE, LMAX, cache.shape[2]), lambda i, active: (i * active[0], 0, 0)),
                pl.BlockSpec((ROW_TILE, fresh.shape[1]), lambda i, active: (i * active[0], 0)),
                pl.BlockSpec((ROW_TILE, width), lambda i, active: (0, 0)),
            ],
            out_specs=wide,
        ),
        input_output_aliases={6: 0},
        compiler_params=pltpu.CompilerParams(vmem_limit_bytes=VMEM),
        cost_estimate=SHORT,
    )(active.reshape(1), bias, current, query, cache, fresh, held)


def together(*values):
    return lax.optimization_barrier(values)


def body(hidden_in, norm_gain, trainer_kv, queries, kv_cache, cache_lengths):
    sections, tensors, dps = (lax.axis_size(axis) for axis in ("section", "tensor", "dp"))
    section, tensor, dp = (lax.axis_index(axis) for axis in ("section", "tensor", "dp"))
    rows = hidden_in.shape[1]
    depth = trainer_kv.shape[1]
    own_width = 2 * KVH * HD // tensors
    served = max(own_width, PAIR)
    early, late = (1, 2), (0, 3)
    everyone = tuple(range(sections))
    is_early = ((section == 1) | (section == 2)).astype(jnp.int32)
    inner = ((dp == 1) | (dp == 2)).astype(jnp.int32)

    def over(axis, count, value, routes):
        pairs = [(a * count + i, b * count + j) for a, b, i, j in routes]
        return lax.ppermute(value, ("section", axis), pairs)

    def over_dp(value, at, target):
        return over("dp", dps, value, [(s, s, z, target[z]) for s in at for z in range(dps)])

    def over_tensor(value, at, flip, step=0):
        return over("tensor", tensors, value, [(s, s + step, t, t ^ flip) for s in at for t in range(tensors)])

    def flipped(b):
        return [z ^ b for z in range(dps)]

    def feature_block(value, b):
        return lax.dynamic_slice_in_dim(value, (dp ^ b) * depth, depth, 1)

    def normed_of(parts, inverse, gains):
        return [
            (part.astype(jnp.float32) * inverse[:, None] * gain.astype(jnp.float32)).astype(jnp.bfloat16)
            for part, gain in zip(parts, gains)
        ]

    def square_sum(part):
        wide = part.astype(jnp.float32)
        return jnp.sum(wide * wide, axis=1)

    bias = seen_bias(cache_lengths[0])
    turn = [(section == tick).astype(jnp.int32) for tick in range(sections)]

    def attended(tick, current, fresh, held):
        return attend(turn[tick], current, queries[0, 0], kv_cache[0, 0], bias, fresh, held)

    def hop(value, tick):
        return over_tensor(value, (tick - 1,), 0, 1)

    def both(part, tick):
        return [part] + [over_tensor(part, (tick,), j) for j in range(1, tensors)]

    def prepared(parts):
        inverse = lax.rsqrt(sum(square_sum(part) for part in parts) / D + epsilon)
        return normed_of(parts, inverse, gains)

    halves = [[(0, 0)], [(j, (j - 1) * depth) for j in range(1, tensors)], [(j, j * depth) for j in range(tensors)]]

    def far(at, blocks):
        return over("dp", dps, blocks[0], [(s, s, a, b) for s in at for a, b in ((0, 2), (3, 1))])

    def relayed(at, blocks):
        return over("dp", dps, blocks[3], [(s, s, a, b) for s in at for a, b in ((2, 3), (1, 0))])

    def around(at, blocks):
        return over_dp(jnp.where(inner == 1, blocks[3], blocks[0]), at, (2, 0, 3, 1))

    def terms_of(half, blocks, which, shift=0):
        terms = []
        for name in which:
            b, has = {FAR: (2, inner), RELAYED: (2, 1 - inner)}.get(name, (name, None))
            source = dp ^ b
            terms.append((blocks[name], has, [
                (j, source * depth + shift, ((tensor ^ j) * dps + source) * depth, start, depth)
                for j, start in halves[half]
            ]))
        return terms

    everything = (0, 1, 3, FAR, RELAYED)

    def placing(active):
        return (active, tensor * own_width % served, own_width)

    weight, hidden, first_kept = together(trainer_kv[0], hidden_in[0], requantize(trainer_kv[0], [tensor], own_width, served))

    squares = square_sum(hidden)
    for j in (2**i for i in range(tensors.bit_length() - 1)):
        squares = squares + over_tensor(squares, (0,), j)
    (normed,) = normed_of([hidden], lax.rsqrt(squares / D + epsilon), [norm_gain])
    first = [feature_block(normed, b) for b in range(dps)]
    weight, first = together(weight, first)
    kept = first_kept + requantize(weight, [tensor ^ j for j in range(1, tensors)], own_width, served)
    first[1:] = [over_dp(first[b], (0,), flipped(b)) for b in range(1, dps)]
    first, gain = together(first, norm_gain)
    gains = [gain] + [over_tensor(gain, everyone, j) for j in range(1, tensors)]

    def others(at, kept):
        received = [over_tensor(kept[j], at, j) for j in range(1, tensors)]
        return received[0] if len(received) == 1 else jnp.concatenate(received, axis=0)

    own = {0: kept[0], 3: over_dp(kept[0], early, flipped(3)), 1: over_dp(kept[0], early, flipped(1))}

    lhs = [jnp.concatenate(first, axis=0)]
    partial = [project(turn[0], lhs, [(kept[j], None, [(0, 0, 0, 0, depth)])]) for j in range(tensors)]
    partial, kept, gains = together(partial, kept, gains)
    rest = {0: others(early, kept)}
    total = partial[0]
    for j in range(1, tensors):
        total = total + over_tensor(partial[j].astype(jnp.bfloat16), (0,), j).astype(jnp.float32)
    total = total.reshape(dps, rows, served)
    returned = [over_dp(total[b].astype(jnp.bfloat16), (0,), flipped(b)) for b in range(1, dps)]
    fresh = total[0]
    for part in returned:
        fresh = fresh + part.astype(jnp.float32)
    result = attended(0, hidden, fresh, hidden)

    rest[3], rest[1] = over_dp(rest[0], early, flipped(3)), over_dp(rest[0], early, flipped(1))
    own, result, kept = together(own, result, kept)
    late_rest = others(late, kept)
    kept_back, rest[0] = together(own, rest[0])
    own[RELAYED], own[FAR] = relayed(early, kept_back), far(early, kept_back)
    own, rest = together(own, rest)
    rest[RELAYED], rest[FAR] = relayed(early, rest), far(early, rest)
    token = over("dp", dps, rest[3][:ROW_TILE, :HD], [(a, b, z, z) for a, b in ((1, 0), (2, 3)) for z in range(dps)])
    token, late_own, result = together(token, kept[0], result)
    whole = jnp.concatenate([late_own, late_rest], axis=0)
    shift = jnp.isnan(token[0, 0]).astype(jnp.int32)
    last = {0: whole, 3: over_dp(whole, late, flipped(3)), 1: over_dp(whole, late, flipped(1))}

    moved = both(hop(result, 1), 1)
    normed = prepared(moved)
    terms = terms_of(0, own, everything) + terms_of(1, rest, (0, 1, 3))
    fresh, rollout = project(turn[1], normed, terms, None, placing(is_early))
    fresh, rollout, rest = together(fresh, rollout, rest)
    fresh, rollout = project(turn[1], normed, terms_of(1, rest, (FAR, RELAYED)), fresh, placing(is_early), rollout)
    result = attended(1, moved[0], fresh, result)

    terms = terms_of(0, own, everything) + terms_of(1, rest, everything)
    moved, last = together(both(hop(result, 2), 2), last)
    last[RELAYED], last[FAR] = relayed(late, last), far(late, last)
    result = attended(2, moved[0], project(turn[2], prepared(moved), terms), result)
    moved = both(hop(result, 3), 3)
    normed = prepared(moved)
    fresh, rollout = project(turn[3], normed, terms_of(2, last, (0, 1, 3), shift), None, placing(1 - is_early), rollout)
    fresh, rollout, last = together(fresh, rollout, last)
    fresh, rollout = project(turn[3], normed, terms_of(2, last, (FAR, RELAYED)), fresh, placing(1 - is_early), rollout)
    result = attended(3, moved[0], fresh, result)
    return (rollout[None], result[None, None])


def solution(mesh):
    placed = (
        P(None, "dp", "tensor"),
        P("section", "tensor"),
        P("section", ("tensor", "dp"), None),
        P("section", None, "dp", "tensor"),
        P("section", None, "dp", None, "tensor"),
        P(None, "dp"),
    )
    return jax.shard_map(
        body,
        mesh=mesh,
        in_specs=placed,
        out_specs=(P("section", None, "tensor"), P("section", None, "dp", "tensor")),
        check_vma=False,
    )
```

profile of v0, /device:TPU:0, one launch (start us, length us, event | category | flops | bytes accessed | tf_op | source)
XLA Modules:
  0.0 646.3 jit_solution(11877539925178095078)
XLA Ops:
  0.7 5.3 shard_map.77.refs_1_.refs_2_
  6.5 4.9 collective-permute-start.2
  11.5 1.4 collective-permute-done.2
  14.7 4.0 collective-permute-start.3
  18.7 4.5 collective-permute-start.4
  23.2 1.9 collective-permute-start.5
  25.2 2.6 collective-permute-start
  27.8 2.7 collective-permute-start.1
  31.1 5.2 shard_map.79.refs_1_
  36.8 5.8 collective-permute-done.4
  42.6 14.2 %collective-permute-done.5 = bf16[128,2048]{1,0:T(8,128)(2,1)} collective-permute-done((bf16[128,2048]{1,0:T(8,128)(2,1)}, bf16[128,2048]{1,0:T(8,128)(2,1)}, u32[]{:S(2)}, u32[]{:S(2)}) %collective-permute-start.5) | collective-permute-done | bytes 524320 | tf_op jit(solution)/shard_map/ppermute | solution.py:251
  57.6 1.5 collective-permute-start.6
  60.0 1.9 constant_dynamic-update-slice_fusion.1
  61.9 1.9 constant_dynamic-update-slice_fusion.refs_0_
  63.7 7.1 %shard_map.78 = f32[512,1024]{1,0:T(8,128)} custom-call(s32[7]{0:T(128)} %stack.68.where_ref, bf16[512,2048]{1,0:T(8,128)(2,1)} %constant_dynamic-update-slice_fusion.refs_0_, bf16[2048,1024]{1,0:T(8,128)(2,1)} %shard_map.77.refs_1_.refs_2_), custom_call_target="tpu_custom_call" | custom-call | tf_op jit(solution)/shard_map/pallas_call | solution.py:146
  70.9 7.1 %shard_map.80 = f32[512,1024]{1,0:T(8,128)} custom-call(s32[7]{0:T(128)} %stack.68.where_ref, bf16[512,2048]{1,0:T(8,128)(2,1)} %constant_dynamic-update-slice_fusion.refs_0_, bf16[2048,1024]{1,0:T(8,128)(2,1)} %shard_map.79.refs_1_), custom_call_target="tpu_custom_call" | custom-call | tf_op jit(solution)/shard_map/pallas_call | solution.py:146
  78.0 2.8 collective-permute-start.11
  80.8 1.7 convert_element_type.100
  82.6 2.4 collective-permute-start.7
  85.0 19.3 %collective-permute-done.7 = bf16[512,1024]{1,0:T(8,128)(2,1)S(1)} collective-permute-done((bf16[512,1024]{1,0:T(8,128)(2,1)S(1)}, bf16[512,1024]{1,0:T(8,128)(2,1)S(1)}, u32[]{:S(2)}, u32[]{:S(2)}) %collective-permute-start.7) | collective-permute-done | bytes 1048608 | tf_op jit(solution)/shard_map/ppermute | solution.py:251
  104.3 1.8 fusion.25
  106.1 3.3 collective-permute-start.10
  109.4 1.9 collective-permute-start.8
  111.3 7.9 %collective-permute-done.10 = bf16[128,1024]{1,0:T(8,128)(2,1)S(1)} collective-permute-done((bf16[128,1024]{1,0:T(8,128)(2,1)S(1)}, bf16[128,1024]{1,0:T(8,128)(2,1)S(1)}, u32[]{:S(2)}, u32[]{:S(2)}) %collective-permute-start.10) | collective-permute-done | bytes 262176 | tf_op jit(solution)/shard_map/ppermute | solution.py:251
  119.2 19.2 %collective-permute-start.9 = (bf16[128,1024]{1,0:T(8,128)(2,1)S(1)}, bf16[128,1024]{1,0:T(8,128)(2,1)S(1)}, u32[]{:S(2)}, u32[]{:S(2)}) collective-permute-start(bf16[128,1024]{1,0:T(8,128)(2,1)S(1)} %get-tuple-element.136), channel_id=1, source_target_pairs={{0,2},{1,3},{2,0},{3,1},{4,6},{5,7},{6,4},{7,5}} | collective-permute-start | bytes 786440 | tf_op jit(solution)/shard_map/ppermute | solution.py:251
  138.4 1.3 copy.18.held_ref
  141.9 4.5 collective-permute-done.9
  146.4 2.0 fusion.22.f_ref
  148.3 12.8 %shard_map.81.held_ref = bf16[128,8192]{1,0:T(8,128)(2,1)} custom-call(s32[1]{0:T(128)} %bitcast.14.active_ref, f32[8,16,256]{2,1,0:T(8,128)} %and_select_fusion.bias_ref, bf16[128,8192]{1,0:T(8,128)(2,1)} %bitcast.50, bf16[128,8192]{1,0:T(8,128)(2,1)} %bitcast.44, bf16[128,16,2048]{2,1,0:T(8,128)(2,1)} %bitcast.39, ...), custom_call_target="tpu_custom_call", output_to_operand_aliasing={{}: (6, {})} | custom-call | tf_op jit(solution)/shard_map/pallas_call | solution.py:211
  161.2 2.6 collective-permute-start.12
  163.8 2.6 collective-permute-start.13
  166.5 2.6 collective-permute-start.14
  169.1 2.6 collective-permute-start.15
  171.8 3.4 collective-permute-start.23
  177.2 114.6 %collective-permute-done.16 = bf16[16,128]{1,0:T(8,128)(2,1)S(1)} collective-permute-done((bf16[16,128]{1,0:T(8,128)(2,1)S(1)}, bf16[16,128]{1,0:T(8,128)(2,1)S(1)}, u32[]{:S(2)}, u32[]{:S(2)}) %collective-permute-start.16) | collective-permute-done | bytes 4128 | tf_op jit(solution)/shard_map/ppermute | solution.py:251
  291.7 2.2 collective-permute-start.17
  293.9 2.6 collective-permute-start.20
  296.6 2.6 collective-permute-start.19
  299.2 2.0 collective-permute-start.18
  301.2 4.7 constant_dynamic-update-slice_fusion.5
  305.9 2.4 constant_dynamic-update-slice_fusion.4.refs_2_
  308.3 1.9 collective-permute-start.24
  310.2 2.7 collective-permute-start.25
  314.9 2.1 fusion.3
  317.0 4.7 fusion.8
  321.8 7.3 %shard_map.82 = (f32[128,1024]{1,0:T(8,128)}, bf16[16384,1024]{1,0:T(8,128)(2,1)}) custom-call(s32[28]{0:T(128)} %stack.81.where_ref, bf16[128,8192]{1,0:T(8,128)(2,1)} %get-tuple-element.141.refs_0_, bf16[128,8192]{1,0:T(8,128)(2,1)} %get-tuple-element.142.refs_1_.refs_0_, bf16[2048,1024]{1,0:T(8,128)(2,1)} %shard_map.77.refs_1_.refs_2_, ...), custom_call_target="tpu_custom_call" | custom-call | tf_op jit(solution)/shard_map/pallas_call | solution.py:146
  329.1 5.4 shard_map.83
  334.4 2.9 shard_map.84.held_ref
  338.2 2.0 collective-permute-start.22
  340.8 94.3 %collective-permute-done.24.refs_3_ = bf16[4096,1024]{1,0:T(8,128)(2,1)} collective-permute-done((bf16[4096,1024]{1,0:T(8,128)(2,1)}, bf16[4096,1024]{1,0:T(8,128)(2,1)}, u32[]{:S(2)}, u32[]{:S(2)}) %collective-permute-start.24) | collective-permute-done | bytes 8388640 | tf_op jit(solution)/shard_map/ppermute | solution.py:251
  435.1 93.7 %collective-permute-done.25.refs_4_ = bf16[4096,1024]{1,0:T(8,128)(2,1)} collective-permute-done((bf16[4096,1024]{1,0:T(8,128)(2,1)}, bf16[4096,1024]{1,0:T(8,128)(2,1)}, u32[]{:S(2)}, u32[]{:S(2)}) %collective-permute-start.25) | collective-permute-done | bytes 8388640 | tf_op jit(solution)/shard_map/ppermute | solution.py:251
  528.8 7.0 %collective-permute-start.28 = (bf16[4096,1024]{1,0:T(8,128)(2,1)}, bf16[4096,1024]{1,0:T(8,128)(2,1)}, u32[]{:S(2)}, u32[]{:S(2)}) collective-permute-start(bf16[4096,1024]{1,0:T(8,128)(2,1)} %constant_dynamic-update-slice_fusion.4.refs_2_), channel_id=1, source_target_pairs={{0,2},{3,1},{24,26},{27,25},{4,6},{7,5},{28,30},{31,29}} | collective-permute-start | bytes 25165832 | tf_op jit(solution)/shard_map/ppermute | solution.py:251
  537.0 2.5 fusion.9
  539.5 4.8 fusion.14
  544.3 7.9 %shard_map.85.f_ref = f32[128,1024]{1,0:T(8,128)} custom-call(s32[34]{0:T(128)} %stack.82.where_ref, bf16[128,8192]{1,0:T(8,128)(2,1)} %get-tuple-element.140.refs_0_, bf16[128,8192]{1,0:T(8,128)(2,1)} %get-tuple-element.139.refs_1_, bf16[2048,1024]{1,0:T(8,128)(2,1)} %shard_map.77.refs_1_.refs_2_, bf16[2048,1024]{1,0:T(8,128)(2,1)} %collective-permute-done.refs_3_, ...), custom_call_target="tpu_custom_call" | custom-call | tf_op jit(solution)/shard_map/pallas_call | solution.py:146
  552.2 2.9 shard_map.86.held_ref
  555.9 2.0 collective-permute-start.27
  561.6 2.1 fusion.18
  563.7 4.7 fusion.20
  568.4 20.7 %shard_map.87 = (f32[128,1024]{1,0:T(8,128)}, bf16[16384,1024]{1,0:T(8,128)(2,1)}) custom-call(s32[19]{0:T(128)} %stack.86.where_ref, bf16[128,8192]{1,0:T(8,128)(2,1)} %get-tuple-element.138.refs_0_, bf16[128,8192]{1,0:T(8,128)(2,1)} %get-tuple-element.137.refs_1_, ...), custom_call_target="tpu_custom_call", output_to_operand_aliasing={{1}: (6, {})} | custom-call | tf_op jit(solution)/shard_map/pallas_call | solution.py:146
  589.1 34.7 %collective-permute-done.28.refs_2_ = bf16[4096,1024]{1,0:T(8,128)(2,1)} collective-permute-done((bf16[4096,1024]{1,0:T(8,128)(2,1)}, bf16[4096,1024]{1,0:T(8,128)(2,1)}, u32[]{:S(2)}, u32[]{:S(2)}) %collective-permute-start.28) | collective-permute-done | bytes 8388640 | tf_op jit(solution)/shard_map/ppermute | solution.py:251
  623.7 7.6 %collective-permute-done.29.refs_3_ = bf16[4096,1024]{1,0:T(8,128)(2,1)} collective-permute-done((bf16[4096,1024]{1,0:T(8,128)(2,1)}, bf16[4096,1024]{1,0:T(8,128)(2,1)}, u32[]{:S(2)}, u32[]{:S(2)}) %collective-permute-start.29) | collective-permute-done | bytes 8388640 | tf_op jit(solution)/shard_map/ppermute | solution.py:251
  631.4 12.0 %shard_map.88 = (f32[128,1024]{1,0:T(8,128)}, bf16[16384,1024]{1,0:T(8,128)(2,1)}) custom-call(s32[14]{0:T(128)} %stack.67.where_ref, bf16[128,8192]{1,0:T(8,128)(2,1)} %get-tuple-element.138.refs_0_, bf16[128,8192]{1,0:T(8,128)(2,1)} %get-tuple-element.137.refs_1_, ...), custom_call_target="tpu_custom_call", output_to_operand_aliasing={{1}: (6, {})} | custom-call | tf_op jit(solution)/shard_map/pallas_call | solution.py:146
  643.4 2.9 shard_map.89
  (69 shorter events, 17.2 us)
Async XLA Ops:
  0.6 5.4 copy-start
  0.7 10.7 %copy-start.5 = (bf16[1,8192]{1,0:T(2,128)(2,1)S(1)}, bf16[1,8192]{1,0:T(2,128)(2,1)}, u32[]{:S(2)}) copy-start(bf16[1,8192]{1,0:T(2,128)(2,1)} %param.7) | copy-start | bytes 49156
  6.5 6.4 collective-permute-start.2
  14.7 22.1 %collective-permute-start.3 = (bf16[128,2048]{1,0:T(8,128)(2,1)}, bf16[128,2048]{1,0:T(8,128)(2,1)S(1)}, u32[]{:S(2)}, u32[]{:S(2)}) collective-permute-start(bf16[128,2048]{1,0:T(8,128)(2,1)} %get-tuple-element.69), channel_id=1, source_target_pairs={{0,1},{1,0},{2,3},{3,2},{4,5},{5,4},{6,7},{7,6}} | collective-permute-start | bytes 1572872 | tf_op jit(solution)/shard_map/ppermute | solution.py:251
  18.7 23.9 %collective-permute-start.4 = (bf16[128,2048]{1,0:T(8,128)(2,1)}, bf16[128,2048]{1,0:T(8,128)(2,1)}, u32[]{:S(2)}, u32[]{:S(2)}) collective-permute-start(bf16[128,2048]{1,0:T(8,128)(2,1)} %get-tuple-element.70), channel_id=1, source_target_pairs={{0,2},{1,3},{2,0},{3,1},{4,6},{5,7},{6,4},{7,5}} | collective-permute-start | bytes 1572872 | tf_op jit(solution)/shard_map/ppermute | solution.py:251
  23.2 33.6 %collective-permute-start.5 = (bf16[128,2048]{1,0:T(8,128)(2,1)}, bf16[128,2048]{1,0:T(8,128)(2,1)}, u32[]{:S(2)}, u32[]{:S(2)}) collective-permute-start(bf16[128,2048]{1,0:T(8,128)(2,1)} %get-tuple-element.71), channel_id=1, source_target_pairs={{0,3},{1,2},{2,1},{3,0},{4,7},{5,6},{6,5},{7,4}} | collective-permute-start | bytes 1572872 | tf_op jit(solution)/shard_map/ppermute | solution.py:251
  25.2 136.0 %collective-permute-start = (bf16[2048,1024]{1,0:T(8,128)(2,1)}, bf16[2048,1024]{1,0:T(8,128)(2,1)}, u32[]{:S(2)}, u32[]{:S(2)}) collective-permute-start(bf16[2048,1024]{1,0:T(8,128)(2,1)} %shard_map.77.refs_1_.refs_2_), channel_id=1, source_target_pairs={{8,9},{9,8},{10,11},{11,10},{16,17},{17,16},{18,19},{19,18},{12,13... | collective-permute-start | bytes 12582920 | tf_op jit(solution)/shard_map/ppermute | solution.py:251
  27.8 133.4 %collective-permute-start.1 = (bf16[2048,1024]{1,0:T(8,128)(2,1)}, bf16[2048,1024]{1,0:T(8,128)(2,1)}, u32[]{:S(2)}, u32[]{:S(2)}) collective-permute-start(bf16[2048,1024]{1,0:T(8,128)(2,1)} %shard_map.77.refs_1_.refs_2_), channel_id=1, source_target_pairs={{8,11},{9,10},{10,9},{11,8},{16,19},{17,18},{18,17},{19,16},{12,15... | collective-permute-start | bytes 12582920 | tf_op jit(solution)/shard_map/ppermute | solution.py:251
  57.6 20.4 %collective-permute-start.6 = (bf16[1,8192]{1,0:T(2,128)(2,1)S(1)}, bf16[1,8192]{1,0:T(2,128)(2,1)S(1)}, u32[]{:S(2)}, u32[]{:S(2)}) collective-permute-start(bf16[1,8192]{1,0:T(2,128)(2,1)S(1)} %copy-done.5), channel_id=1, source_target_pairs={{0,4},{4,0},{8,12},{12,8},{16,20},{20,16},{24,28},{28,24},{1,5},{5... | collective-permute-start | bytes 49160 | tf_op jit(solution)/shard_map/ppermute | solution.py:251
  78.0 26.3 %copy-start.4 = (f32[512,1024]{1,0:T(8,128)S(1)}, f32[512,1024]{1,0:T(8,128)}, u32[]{:S(2)}) copy-start(f32[512,1024]{1,0:T(8,128)} %shard_map.78) | copy-start | bytes 6291460
  78.0 83.2 %collective-permute-start.11 = (bf16[2048,1024]{1,0:T(8,128)(2,1)}, bf16[2048,1024]{1,0:T(8,128)(2,1)}, u32[]{:S(2)}, u32[]{:S(2)}) collective-permute-start(bf16[2048,1024]{1,0:T(8,128)(2,1)} %shard_map.79.refs_1_), channel_id=1, source_target_pairs={{8,12},{12,8},{16,20},{20,16},{9,13},{13,9},{17,21},{21,17},{10,14... | collective-permute-start | bytes 12582920 | tf_op jit(solution)/shard_map/ppermute | solution.py:251
  82.6 21.7 %collective-permute-start.7 = (bf16[512,1024]{1,0:T(8,128)(2,1)S(1)}, bf16[512,1024]{1,0:T(8,128)(2,1)S(1)}, u32[]{:S(2)}, u32[]{:S(2)}) collective-permute-start(bf16[512,1024]{1,0:T(8,128)(2,1)S(1)} %convert_element_type.100), channel_id=1, source_target_pairs={{0,4},{4,0},{1,5},{5,1},{2,6},{6,2},{3,7},{7,3}} | collective-permute-start | bytes 3145736 | tf_op jit(solution)/shard_map/ppermute | solution.py:251
  106.1 34.3 %copy-start.6 = (s32[1,128]{1,0:T(1,128)S(1)}, s32[1,128]{1,0:T(1,128)}, u32[]{:S(2)}) copy-start(s32[1,128]{1,0:T(1,128)} %param.11) | copy-start | bytes 1540
  106.1 13.1 %collective-permute-start.10 = (bf16[128,1024]{1,0:T(8,128)(2,1)S(1)}, bf16[128,1024]{1,0:T(8,128)(2,1)S(1)}, u32[]{:S(2)}, u32[]{:S(2)}) collective-permute-start(bf16[128,1024]{1,0:T(8,128)(2,1)S(1)} %get-tuple-element.135), channel_id=1, source_target_pairs={{0,3},{1,2},{2,1},{3,0},{4,7},{5,6},{6,5},{7,4}} | collective-permute-start | bytes 786440 | tf_op jit(solution)/shard_map/ppermute | solution.py:251
  109.4 32.4 %collective-permute-start.8 = (bf16[128,1024]{1,0:T(8,128)(2,1)S(1)}, bf16[128,1024]{1,0:T(8,128)(2,1)S(1)}, u32[]{:S(2)}, u32[]{:S(2)}) collective-permute-start(bf16[128,1024]{1,0:T(8,128)(2,1)S(1)} %get-tuple-element.134), channel_id=1, source_target_pairs={{0,1},{1,0},{2,3},{3,2},{4,5},{5,4},{6,7},{7,6}} | collective-permute-start | bytes 786440 | tf_op jit(solution)/shard_map/ppermute | solution.py:251
  119.2 27.2 %collective-permute-start.9 = (bf16[128,1024]{1,0:T(8,128)(2,1)S(1)}, bf16[128,1024]{1,0:T(8,128)(2,1)S(1)}, u32[]{:S(2)}, u32[]{:S(2)}) collective-permute-start(bf16[128,1024]{1,0:T(8,128)(2,1)S(1)} %get-tuple-element.136), channel_id=1, source_target_pairs={{0,2},{1,3},{2,0},{3,1},{4,6},{5,7},{6,4},{7,5}} | collective-permute-start | bytes 786440 | tf_op jit(solution)/shard_map/ppermute | solution.py:251
  161.2 14.0 %collective-permute-start.12 = (bf16[2048,1024]{1,0:T(8,128)(2,1)}, bf16[2048,1024]{1,0:T(8,128)(2,1)}, u32[]{:S(2)}, u32[]{:S(2)}) collective-permute-start(bf16[2048,1024]{1,0:T(8,128)(2,1)} %shard_map.77.refs_1_.refs_2_), channel_id=1, source_target_pairs={{8,10},{11,9},{16,18},{19,17},{12,14},{15,13},{20,22},{23,21}} | collective-permute-start | bytes 12582920 | tf_op jit(solution)/shard_map/ppermute | solution.py:251
  163.8 11.3 %collective-permute-start.13 = (bf16[2048,1024]{1,0:T(8,128)(2,1)}, bf16[2048,1024]{1,0:T(8,128)(2,1)}, u32[]{:S(2)}, u32[]{:S(2)}) collective-permute-start(bf16[2048,1024]{1,0:T(8,128)(2,1)} %collective-permute-done.1.refs_4_), channel_id=1, source_target_pairs={{10,11},{9,8},{18,19},{17,16},{14,15},{13,12},{22,23},{21,20}} | collective-permute-start | bytes 12582920 | tf_op jit(solution)/shard_map/ppermute | solution.py:251
  166.5 8.7 %collective-permute-start.14 = (bf16[2048,1024]{1,0:T(8,128)(2,1)}, bf16[2048,1024]{1,0:T(8,128)(2,1)}, u32[]{:S(2)}, u32[]{:S(2)}) collective-permute-start(bf16[2048,1024]{1,0:T(8,128)(2,1)} %collective-permute-done.11.refs_7_), channel_id=1, source_target_pairs={{8,9},{9,8},{10,11},{11,10},{16,17},{17,16},{18,19},{19,18},{12,13... | collective-permute-start | bytes 12582920 | tf_op jit(solution)/shard_map/ppermute | solution.py:251
  169.1 6.1 collective-permute-start.15
  171.8 134.1 %collective-permute-start.23 = (bf16[2048,1024]{1,0:T(8,128)(2,1)}, bf16[2048,1024]{1,0:T(8,128)(2,1)S(1)}, u32[]{:S(2)}, u32[]{:S(2)}) collective-permute-start(bf16[2048,1024]{1,0:T(8,128)(2,1)} %shard_map.79.refs_1_), channel_id=1, source_target_pairs={{0,4},{4,0},{24,28},{28,24},{1,5},{5,1},{25,29},{29,25},{2,6},{6,2... | collective-permute-start | bytes 12582920 | tf_op jit(solution)/shard_map/ppermute | solution.py:251
  175.9 115.9 %collective-permute-start.16 = (bf16[16,128]{1,0:T(8,128)(2,1)S(1)}, bf16[16,128]{1,0:T(8,128)(2,1)S(1)}, u32[]{:S(2)}, u32[]{:S(2)}) collective-permute-start(bf16[16,128]{1,0:T(8,128)(2,1)S(1)} %slice.29), channel_id=1, source_target_pairs={{8,0},{9,1},{10,2},{11,3},{16,24},{17,25},{18,26},{19,27},{12,4},{... | collective-permute-start | bytes 12296 | tf_op jit(solution)/shard_map/ppermute | solution.py:251
  291.7 7.5 %collective-permute-start.17 = (bf16[128,8192]{1,0:T(8,128)(2,1)}, bf16[128,8192]{1,0:T(8,128)(2,1)S(1)}, u32[]{:S(2)}, u32[]{:S(2)}) collective-permute-start(bf16[128,8192]{1,0:T(8,128)(2,1)} %shard_map.81.held_ref), channel_id=1, source_target_pairs={{0,8},{4,12},{1,9},{5,13},{2,10},{6,14},{3,11},{7,15}} | collective-permute-start | bytes 6291464 | tf_op jit(solution)/shard_map/ppermute | solution.py:251
  293.9 35.1 %collective-permute-start.20 = (bf16[2048,1024]{1,0:T(8,128)(2,1)}, bf16[2048,1024]{1,0:T(8,128)(2,1)}, u32[]{:S(2)}, u32[]{:S(2)}) collective-permute-start(bf16[2048,1024]{1,0:T(8,128)(2,1)} %collective-permute-done.15.refs_9_), channel_id=1, source_target_pairs={{10,11},{9,8},{18,19},{17,16},{14,15},{13,12},{22,23},{21,20}} | collective-permute-start | bytes 12582920 | tf_op jit(solution)/shard_map/ppermute | solution.py:251
  296.6 32.4 %collective-permute-start.19 = (bf16[2048,1024]{1,0:T(8,128)(2,1)}, bf16[2048,1024]{1,0:T(8,128)(2,1)}, u32[]{:S(2)}, u32[]{:S(2)}) collective-permute-start(bf16[2048,1024]{1,0:T(8,128)(2,1)} %collective-permute-done.11.refs_7_), channel_id=1, source_target_pairs={{8,10},{11,9},{16,18},{19,17},{12,14},{15,13},{20,22},{23,21}} | collective-permute-start | bytes 12582920 | tf_op jit(solution)/shard_map/ppermute | solution.py:251
  299.2 17.8 %copy-start.2 = (bf16[128,8192]{1,0:T(8,128)(2,1)}, bf16[128,8192]{1,0:T(8,128)(2,1)S(1)}, u32[]{:S(2)}) copy-start(bf16[128,8192]{1,0:T(8,128)(2,1)S(1)} %collective-permute-done.17.x_ref) | copy-start | bytes 6291460
  299.2 15.7 %collective-permute-start.18 = (bf16[128,8192]{1,0:T(8,128)(2,1)S(1)}, bf16[128,8192]{1,0:T(8,128)(2,1)}, u32[]{:S(2)}, u32[]{:S(2)}) collective-permute-start(bf16[128,8192]{1,0:T(8,128)(2,1)S(1)} %collective-permute-done.17.x_ref), channel_id=1, source_target_pairs={{8,12},{12,8},{9,13},{13,9},{10,14},{14,10},{11,15},{15,11}} | collective-permute-start | bytes 6291464 | tf_op jit(solution)/shard_map/ppermute | solution.py:251
  308.3 126.8 %collective-permute-start.24 = (bf16[4096,1024]{1,0:T(8,128)(2,1)}, bf16[4096,1024]{1,0:T(8,128)(2,1)}, u32[]{:S(2)}, u32[]{:S(2)}) collective-permute-start(bf16[4096,1024]{1,0:T(8,128)(2,1)} %constant_dynamic-update-slice_fusion.4.refs_2_), channel_id=1, source_target_pairs={{0,1},{1,0},{2,3},{3,2},{24,25},{25,24},{26,27},{27,26},{4,5},{5,4... | collective-permute-start | bytes 25165832 | tf_op jit(solution)/shard_map/ppermute | solution.py:251
  310.2 218.6 %collective-permute-start.25 = (bf16[4096,1024]{1,0:T(8,128)(2,1)}, bf16[4096,1024]{1,0:T(8,128)(2,1)}, u32[]{:S(2)}, u32[]{:S(2)}) collective-permute-start(bf16[4096,1024]{1,0:T(8,128)(2,1)} %constant_dynamic-update-slice_fusion.4.refs_2_), channel_id=1, source_target_pairs={{0,3},{1,2},{2,1},{3,0},{24,27},{25,26},{26,25},{27,24},{4,7},{5,6... | collective-permute-start | bytes 25165832 | tf_op jit(solution)/shard_map/ppermute | solution.py:251
  337.4 0.8 collective-permute-start.21
  338.2 206.2 %copy-start.1 = (bf16[128,8192]{1,0:T(8,128)(2,1)}, bf16[128,8192]{1,0:T(8,128)(2,1)S(1)}, u32[]{:S(2)}) copy-start(bf16[128,8192]{1,0:T(8,128)(2,1)S(1)} %collective-permute-done.21.x_ref) | copy-start | bytes 6291460
  338.2 2.6 collective-permute-start.22
  528.8 95.0 %collective-permute-start.28 = (bf16[4096,1024]{1,0:T(8,128)(2,1)}, bf16[4096,1024]{1,0:T(8,128)(2,1)}, u32[]{:S(2)}, u32[]{:S(2)}) collective-permute-start(bf16[4096,1024]{1,0:T(8,128)(2,1)} %constant_dynamic-update-slice_fusion.4.refs_2_), channel_id=1, source_target_pairs={{0,2},{3,1},{24,26},{27,25},{4,6},{7,5},{28,30},{31,29}} | collective-permute-start | bytes 25165832 | tf_op jit(solution)/shard_map/ppermute | solution.py:251
  535.7 95.6 %collective-permute-start.29 = (bf16[4096,1024]{1,0:T(8,128)(2,1)}, bf16[4096,1024]{1,0:T(8,128)(2,1)}, u32[]{:S(2)}, u32[]{:S(2)}) collective-permute-start(bf16[4096,1024]{1,0:T(8,128)(2,1)} %collective-permute-done.25.refs_4_), channel_id=1, source_target_pairs={{2,3},{1,0},{26,27},{25,24},{6,7},{5,4},{30,31},{29,28}} | collective-permute-start | bytes 25165832 | tf_op jit(solution)/shard_map/ppermute | solution.py:251
  555.1 0.8 collective-permute-start.26
  555.9 12.4 %copy-start.3 = (bf16[128,8192]{1,0:T(8,128)(2,1)}, bf16[128,8192]{1,0:T(8,128)(2,1)S(1)}, u32[]{:S(2)}) copy-start(bf16[128,8192]{1,0:T(8,128)(2,1)S(1)} %collective-permute-done.26.x_ref) | copy-start | bytes 6291460
  555.9 5.6 collective-permute-start.27
where the time goes:
time: 648 us; the launch traced here: 646 us
  waiting for transfers between devices  399 us (62%)
  Pallas kernels  99.6 us (15%)
  starting transfers between devices  94.7 us (15%)
  other arithmetic  30 us (5%)
  local copies, waits for them, and re-layouts  20.9 us (3%)
    ppermute x30, waiting for transfers between devices, over(): return lax.ppermute(value, ('section', axis), pairs)  399 us
    ppermute x30, starting transfers between devices, over(): return lax.ppermute(value, ('section', axis), pairs)  94.7 us
    pallas_call x7, Pallas kernels, project(): pl.pallas_call(functools.partial(project_kernel, layout, len(lhs), bool(a...  67.5 us
    pallas_call x4, Pallas kernels, attend(): pl.pallas_call(functools.partial(attend_kernel, share), out_shape=jax.Sha...  21.6 us
    convert_element_type x4, other arithmetic, normed_of(): (part.astype(jnp.float32) * inverse[:, None] * gain.astype(jnp.float32))....  14.8 us
  transfers between devices with their start and end apart: 30, of which 12 were waited for; matrix products, arithmetic and copies ran while one was open for 8% of the time, Pallas kernels for 12%

commit v1 on v0

--- a/solution.py
+++ b/solution.py
@@ -342,26 +342,30 @@
     for j in range(1, tensors):
         total = total + over_tensor(partial[j].astype(jnp.bfloat16), (0,), j).astype(jnp.float32)
     total = total.reshape(dps, rows, served)
-    returned = [over_dp(total[b].astype(jnp.bfloat16), (0,), flipped(b)) for b in range(1, dps)]
+    step = 1
+    while step < dps:
+        send = jnp.stack([total[b] for b in range(total.shape[0]) if b & 1]).astype(jnp.bfloat16)
+        keep = jnp.stack([total[b] for b in range(total.shape[0]) if not b & 1])
+        total = keep + over_dp(send, (0,), flipped(step)).astype(jnp.float32)
+        step *= 2
     fresh = total[0]
-    for part in returned:
-        fresh = fresh + part.astype(jnp.float32)
     result = attended(0, hidden, fresh, hidden)
 
     rest[3], rest[1] = over_dp(rest[0], early, flipped(3)), over_dp(rest[0], early, flipped(1))
     own, result, kept = together(own, result, kept)
+    parts = both(result, 0)
     late_rest = others(late, kept)
     kept_back, rest[0] = together(own, rest[0])
     own[RELAYED], own[FAR] = relayed(early, kept_back), far(early, kept_back)
     own, rest = together(own, rest)
     rest[RELAYED], rest[FAR] = relayed(early, rest), far(early, rest)
     token = over("dp", dps, rest[3][:ROW_TILE, :HD], [(a, b, z, z) for a, b in ((1, 0), (2, 3)) for z in range(dps)])
-    token, late_own, result = together(token, kept[0], result)
+    token, late_own, parts = together(token, kept[0], parts)
     whole = jnp.concatenate([late_own, late_rest], axis=0)
     shift = jnp.isnan(token[0, 0]).astype(jnp.int32)
     last = {0: whole, 3: over_dp(whole, late, flipped(3)), 1: over_dp(whole, late, flipped(1))}
 
-    moved = both(hop(result, 1), 1)
+    moved = [hop(part, 1) for part in parts]
     normed = prepared(moved)
     terms = terms_of(0, own, everything) + terms_of(1, rest, (0, 1, 3))
     fresh, rollout = project(turn[1], normed, terms, None, placing(is_early))

time: 648 us -> 644 us (level)
  starting transfers between devices: 94.7 us -> 83.2 us
  waiting for transfers between devices: 399 us -> 407 us
    ppermute x30, starting transfers between devices: 94.7 us -> 83.2 us  [over(): return lax.ppermute(value, ('section', axis), pairs)]
    ppermute x30, waiting for transfers between devices: 399 us -> 407 us  [over(): return lax.ppermute(value, ('section', axis), pairs)]
  transfers between devices with their start and end apart: 30 -> 30, of which waited for: 12 -> 13; matrix products, arithmetic and copies ran while one was open for 8% -> 7% of each run, Pallas kernels for 12% -> 12%
where the time goes in v1:
time: 644 us; the launch traced here: 642 us
  waiting for transfers between devices  407 us (63%)
  Pallas kernels  99.6 us (15%)
  starting transfers between devices  83.2 us (13%)
  other arithmetic  28 us (4%)
  local copies, waits for them, and re-layouts  21.5 us (3%)
    ppermute x30, waiting for transfers between devices, over(): return lax.ppermute(value, ('section', axis), pairs)  407 us
    ppermute x30, starting transfers between devices, over(): return lax.ppermute(value, ('section', axis), pairs)  83.2 us
    pallas_call x7, Pallas kernels, project(): pl.pallas_call(functools.partial(project_kernel, layout, len(lhs), bool(a...  67.5 us
    pallas_call x4, Pallas kernels, attend(): pl.pallas_call(functools.partial(attend_kernel, share), out_shape=jax.Sha...  21.6 us
    convert_element_type x4, other arithmetic, normed_of(): (part.astype(jnp.float32) * inverse[:, None] * gain.astype(jnp.float32))....  15 us
  transfers between devices with their start and end apart: 30, of which 13 were waited for; matrix products, arithmetic and copies ran while one was open for 7% of the time, Pallas kernels for 12%

profile of v1, /device:TPU:0, one launch (start us, length us, event | category | flops | bytes accessed | tf_op | source)
XLA Modules:
  0.0 642.1 jit_solution(5679277879532946019)
XLA Ops:
  0.7 5.3 shard_map.77.refs_1_.refs_2_
  6.5 4.9 collective-permute-start.2
  11.5 1.4 collective-permute-done.2
  14.7 4.0 collective-permute-start.3
  18.7 4.5 collective-permute-start.4
  23.2 1.9 collective-permute-start.5
  25.1 2.6 collective-permute-start
  27.8 2.7 collective-permute-start.1
  31.2 5.2 shard_map.79.refs_1_
  36.8 5.8 collective-permute-done.4
  42.6 14.2 %collective-permute-done.5 = bf16[128,2048]{1,0:T(8,128)(2,1)} collective-permute-done((bf16[128,2048]{1,0:T(8,128)(2,1)}, bf16[128,2048]{1,0:T(8,128)(2,1)}, u32[]{:S(2)}, u32[]{:S(2)}) %collective-permute-start.5) | collective-permute-done | bytes 524320 | tf_op jit(solution)/shard_map/ppermute | solution.py:251
  57.6 1.5 collective-permute-start.6
  60.0 1.9 constant_dynamic-update-slice_fusion.1
  61.8 1.9 constant_dynamic-update-slice_fusion.refs_0_
  63.7 7.2 %shard_map.78 = f32[512,1024]{1,0:T(8,128)} custom-call(s32[7]{0:T(128)} %stack.73.where_ref, bf16[512,2048]{1,0:T(8,128)(2,1)} %constant_dynamic-update-slice_fusion.refs_0_, bf16[2048,1024]{1,0:T(8,128)(2,1)} %shard_map.77.refs_1_.refs_2_), custom_call_target="tpu_custom_call" | custom-call | tf_op jit(solution)/shard_map/pallas_call | solution.py:146
  70.9 7.1 %shard_map.80 = f32[512,1024]{1,0:T(8,128)} custom-call(s32[7]{0:T(128)} %stack.73.where_ref, bf16[512,2048]{1,0:T(8,128)(2,1)} %constant_dynamic-update-slice_fusion.refs_0_, bf16[2048,1024]{1,0:T(8,128)(2,1)} %shard_map.79.refs_1_), custom_call_target="tpu_custom_call" | custom-call | tf_op jit(solution)/shard_map/pallas_call | solution.py:146
  78.0 2.8 collective-permute-start.10
  80.8 1.7 convert_element_type.96
  82.6 2.4 collective-permute-start.7
  85.0 19.4 %collective-permute-done.7 = bf16[512,1024]{1,0:T(8,128)(2,1)S(1)} collective-permute-done((bf16[512,1024]{1,0:T(8,128)(2,1)S(1)}, bf16[512,1024]{1,0:T(8,128)(2,1)S(1)}, u32[]{:S(2)}, u32[]{:S(2)}) %collective-permute-start.7) | collective-permute-done | bytes 1048608 | tf_op jit(solution)/shard_map/ppermute | solution.py:251
  105.0 2.6 collective-permute-start.8
  107.7 14.5 %collective-permute-done.8 = bf16[2,128,1024]{2,1,0:T(8,128)(2,1)S(1)} collective-permute-done((bf16[2,128,1024]{2,1,0:T(8,128)(2,1)S(1)}, bf16[2,128,1024]{2,1,0:T(8,128)(2,1)S(1)}, u32[]{:S(2)}, u32[]{:S(2)}) %collective-permute-start.8) | collective-permute-done | bytes 524320 | tf_op jit(solution)/shard_map/ppermute | solution.py:251
  123.1 2.2 collective-permute-start.9
  125.4 1.3 copy.18.held_ref
  128.6 12.1 %collective-permute-done.9 = bf16[1,128,1024]{2,1,0:T(8,128)(2,1)S(1)} collective-permute-done((bf16[1,128,1024]{2,1,0:T(8,128)(2,1)}, bf16[1,128,1024]{2,1,0:T(8,128)(2,1)S(1)}, u32[]{:S(2)}, u32[]{:S(2)}) %collective-permute-start.9) | collective-permute-done | bytes 262176 | tf_op jit(solution)/shard_map/ppermute | solution.py:251
  141.6 12.8 %shard_map.81.held_ref = bf16[128,8192]{1,0:T(8,128)(2,1)} custom-call(s32[1]{0:T(128)} %bitcast.14.active_ref, f32[8,16,256]{2,1,0:T(8,128)} %and_select_fusion.bias_ref, bf16[128,8192]{1,0:T(8,128)(2,1)} %bitcast.60, bf16[128,8192]{1,0:T(8,128)(2,1)} %bitcast.54, bf16[128,16,2048]{2,1,0:T(8,128)(2,1)} %bitcast.49, ...), custom_call_target="tpu_custom_call", output_to_operand_aliasing={{}: (6, {})} | custom-call | tf_op jit(solution)/shard_map/pallas_call | solution.py:211
  154.5 2.6 collective-permute-start.11
  157.1 2.6 collective-permute-start.12
  159.8 2.6 collective-permute-start.13
  162.4 2.6 collective-permute-start.14
  165.0 3.4 collective-permute-start.23
  168.4 2.4 collective-permute-start.16
  171.6 1.3 collective-permute-start.15
  172.8 65.2 %collective-permute-done.16 = bf16[128,8192]{1,0:T(8,128)(2,1)S(1)} collective-permute-done((bf16[128,8192]{1,0:T(8,128)(2,1)}, bf16[128,8192]{1,0:T(8,128)(2,1)S(1)}, u32[]{:S(2)}, u32[]{:S(2)}) %collective-permute-start.16) | collective-permute-done | bytes 2097184 | tf_op jit(solution)/shard_map/ppermute | solution.py:251
  238.1 48.9 %collective-permute-done.15 = bf16[16,128]{1,0:T(8,128)(2,1)S(1)} collective-permute-done((bf16[16,128]{1,0:T(8,128)(2,1)S(1)}, bf16[16,128]{1,0:T(8,128)(2,1)S(1)}, u32[]{:S(2)}, u32[]{:S(2)}) %collective-permute-start.15) | collective-permute-done | bytes 4128 | tf_op jit(solution)/shard_map/ppermute | solution.py:251
  287.0 3.4 collective-permute-start.18
  290.4 2.6 collective-permute-start.20
  293.0 2.7 collective-permute-start.19
  295.7 3.9 collective-permute-start.17
  299.6 4.7 constant_dynamic-update-slice_fusion.5
  304.3 2.4 constant_dynamic-update-slice_fusion.4.refs_2_
  306.7 1.9 collective-permute-start.24
  308.6 4.6 collective-permute-start.25
  314.7 2.1 fusion.3
  317.3 4.9 fusion.8
  322.2 7.3 %shard_map.82 = (f32[128,1024]{1,0:T(8,128)}, bf16[16384,1024]{1,0:T(8,128)(2,1)}) custom-call(s32[28]{0:T(128)} %stack.88.where_ref, bf16[128,8192]{1,0:T(8,128)(2,1)} %get-tuple-element.144.refs_0_, bf16[128,8192]{1,0:T(8,128)(2,1)} %get-tuple-element.145.refs_1_.refs_0_, bf16[2048,1024]{1,0:T(8,128)(2,1)} %shard_map.77.refs_1_.refs_2_, ...), custom_call_target="tpu_custom_call" | custom-call | tf_op jit(solution)/shard_map/pallas_call | solution.py:146
  329.5 5.3 shard_map.83
  334.9 2.9 shard_map.84.held_ref
  338.6 2.0 collective-permute-start.22
  341.3 89.8 %collective-permute-done.24.refs_3_ = bf16[4096,1024]{1,0:T(8,128)(2,1)} collective-permute-done((bf16[4096,1024]{1,0:T(8,128)(2,1)}, bf16[4096,1024]{1,0:T(8,128)(2,1)}, u32[]{:S(2)}, u32[]{:S(2)}) %collective-permute-start.24) | collective-permute-done | bytes 8388640 | tf_op jit(solution)/shard_map/ppermute | solution.py:251
  431.1 92.9 %collective-permute-done.25.refs_4_ = bf16[4096,1024]{1,0:T(8,128)(2,1)} collective-permute-done((bf16[4096,1024]{1,0:T(8,128)(2,1)}, bf16[4096,1024]{1,0:T(8,128)(2,1)}, u32[]{:S(2)}, u32[]{:S(2)}) %collective-permute-start.25) | collective-permute-done | bytes 8388640 | tf_op jit(solution)/shard_map/ppermute | solution.py:251
  524.0 7.5 %collective-permute-start.28 = (bf16[4096,1024]{1,0:T(8,128)(2,1)}, bf16[4096,1024]{1,0:T(8,128)(2,1)}, u32[]{:S(2)}, u32[]{:S(2)}) collective-permute-start(bf16[4096,1024]{1,0:T(8,128)(2,1)} %constant_dynamic-update-slice_fusion.4.refs_2_), channel_id=1, source_target_pairs={{0,2},{3,1},{24,26},{27,25},{4,6},{7,5},{28,30},{31,29}} | collective-permute-start | bytes 25165832 | tf_op jit(solution)/shard_map/ppermute | solution.py:251
  532.8 2.5 fusion.9
  535.3 4.8 fusion.14
  540.1 7.9 %shard_map.85.f_ref = f32[128,1024]{1,0:T(8,128)} custom-call(s32[34]{0:T(128)} %stack.89.where_ref, bf16[128,8192]{1,0:T(8,128)(2,1)} %get-tuple-element.143.refs_0_, bf16[128,8192]{1,0:T(8,128)(2,1)} %get-tuple-element.142.refs_1_, bf16[2048,1024]{1,0:T(8,128)(2,1)} %shard_map.77.refs_1_.refs_2_, bf16[2048,1024]{1,0:T(8,128)(2,1)} %collective-permute-done.refs_3_, ...), custom_call_target="tpu_custom_call" | custom-call | tf_op jit(solution)/shard_map/pallas_call | solution.py:146
  548.0 2.9 shard_map.86.held_ref
  551.7 2.0 collective-permute-start.27
  557.0 2.1 fusion.18
  559.1 4.7 fusion.20
  563.8 20.7 %shard_map.87 = (f32[128,1024]{1,0:T(8,128)}, bf16[16384,1024]{1,0:T(8,128)(2,1)}) custom-call(s32[19]{0:T(128)} %stack.93.where_ref, bf16[128,8192]{1,0:T(8,128)(2,1)} %get-tuple-element.141.refs_0_, bf16[128,8192]{1,0:T(8,128)(2,1)} %get-tuple-element.140.refs_1_, ...), custom_call_target="tpu_custom_call", output_to_operand_aliasing={{1}: (6, {})} | custom-call | tf_op jit(solution)/shard_map/pallas_call | solution.py:146
  584.5 35.0 %collective-permute-done.28.refs_2_ = bf16[4096,1024]{1,0:T(8,128)(2,1)} collective-permute-done((bf16[4096,1024]{1,0:T(8,128)(2,1)}, bf16[4096,1024]{1,0:T(8,128)(2,1)}, u32[]{:S(2)}, u32[]{:S(2)}) %collective-permute-start.28) | collective-permute-done | bytes 8388640 | tf_op jit(solution)/shard_map/ppermute | solution.py:251
  619.5 7.6 %collective-permute-done.29.refs_3_ = bf16[4096,1024]{1,0:T(8,128)(2,1)} collective-permute-done((bf16[4096,1024]{1,0:T(8,128)(2,1)}, bf16[4096,1024]{1,0:T(8,128)(2,1)}, u32[]{:S(2)}, u32[]{:S(2)}) %collective-permute-start.29) | collective-permute-done | bytes 8388640 | tf_op jit(solution)/shard_map/ppermute | solution.py:251
  627.1 12.0 %shard_map.88 = (f32[128,1024]{1,0:T(8,128)}, bf16[16384,1024]{1,0:T(8,128)(2,1)}) custom-call(s32[14]{0:T(128)} %stack.72.where_ref, bf16[128,8192]{1,0:T(8,128)(2,1)} %get-tuple-element.141.refs_0_, bf16[128,8192]{1,0:T(8,128)(2,1)} %get-tuple-element.140.refs_1_, ...), custom_call_target="tpu_custom_call", output_to_operand_aliasing={{1}: (6, {})} | custom-call | tf_op jit(solution)/shard_map/pallas_call | solution.py:146
  639.1 2.9 shard_map.89
  (73 shorter events, 17.9 us)
Async XLA Ops:
  0.6 5.4 copy-start
  0.7 10.7 %copy-start.5 = (bf16[1,8192]{1,0:T(2,128)(2,1)S(1)}, bf16[1,8192]{1,0:T(2,128)(2,1)}, u32[]{:S(2)}) copy-start(bf16[1,8192]{1,0:T(2,128)(2,1)} %param.7) | copy-start | bytes 49156
  6.5 6.4 collective-permute-start.2
  14.7 22.1 %collective-permute-start.3 = (bf16[128,2048]{1,0:T(8,128)(2,1)}, bf16[128,2048]{1,0:T(8,128)(2,1)S(1)}, u32[]{:S(2)}, u32[]{:S(2)}) collective-permute-start(bf16[128,2048]{1,0:T(8,128)(2,1)} %get-tuple-element.70), channel_id=1, source_target_pairs={{0,1},{1,0},{2,3},{3,2},{4,5},{5,4},{6,7},{7,6}} | collective-permute-start | bytes 1572872 | tf_op jit(solution)/shard_map/ppermute | solution.py:251
  18.7 23.9 %collective-permute-start.4 = (bf16[128,2048]{1,0:T(8,128)(2,1)}, bf16[128,2048]{1,0:T(8,128)(2,1)}, u32[]{:S(2)}, u32[]{:S(2)}) collective-permute-start(bf16[128,2048]{1,0:T(8,128)(2,1)} %get-tuple-element.71), channel_id=1, source_target_pairs={{0,2},{1,3},{2,0},{3,1},{4,6},{5,7},{6,4},{7,5}} | collective-permute-start | bytes 1572872 | tf_op jit(solution)/shard_map/ppermute | solution.py:251
  23.2 33.6 %collective-permute-start.5 = (bf16[128,2048]{1,0:T(8,128)(2,1)}, bf16[128,2048]{1,0:T(8,128)(2,1)}, u32[]{:S(2)}, u32[]{:S(2)}) collective-permute-start(bf16[128,2048]{1,0:T(8,128)(2,1)} %get-tuple-element.72), channel_id=1, source_target_pairs={{0,3},{1,2},{2,1},{3,0},{4,7},{5,6},{6,5},{7,4}} | collective-permute-start | bytes 1572872 | tf_op jit(solution)/shard_map/ppermute | solution.py:251
  25.1 129.3 %collective-permute-start = (bf16[2048,1024]{1,0:T(8,128)(2,1)}, bf16[2048,1024]{1,0:T(8,128)(2,1)}, u32[]{:S(2)}, u32[]{:S(2)}) collective-permute-start(bf16[2048,1024]{1,0:T(8,128)(2,1)} %shard_map.77.refs_1_.refs_2_), channel_id=1, source_target_pairs={{8,9},{9,8},{10,11},{11,10},{16,17},{17,16},{18,19},{19,18},{12,13... | collective-permute-start | bytes 12582920 | tf_op jit(solution)/shard_map/ppermute | solution.py:251
  27.8 126.7 %collective-permute-start.1 = (bf16[2048,1024]{1,0:T(8,128)(2,1)}, bf16[2048,1024]{1,0:T(8,128)(2,1)}, u32[]{:S(2)}, u32[]{:S(2)}) collective-permute-start(bf16[2048,1024]{1,0:T(8,128)(2,1)} %shard_map.77.refs_1_.refs_2_), channel_id=1, source_target_pairs={{8,11},{9,10},{10,9},{11,8},{16,19},{17,18},{18,17},{19,16},{12,15... | collective-permute-start | bytes 12582920 | tf_op jit(solution)/shard_map/ppermute | solution.py:251
  57.6 20.4 %collective-permute-start.6 = (bf16[1,8192]{1,0:T(2,128)(2,1)S(1)}, bf16[1,8192]{1,0:T(2,128)(2,1)S(1)}, u32[]{:S(2)}, u32[]{:S(2)}) collective-permute-start(bf16[1,8192]{1,0:T(2,128)(2,1)S(1)} %copy-done.5), channel_id=1, source_target_pairs={{0,4},{4,0},{8,12},{12,8},{16,20},{20,16},{24,28},{28,24},{1,5},{5... | collective-permute-start | bytes 49160 | tf_op jit(solution)/shard_map/ppermute | solution.py:251
  78.0 26.3 %copy-start.4 = (f32[512,1024]{1,0:T(8,128)S(1)}, f32[512,1024]{1,0:T(8,128)}, u32[]{:S(2)}) copy-start(f32[512,1024]{1,0:T(8,128)} %shard_map.78) | copy-start | bytes 6291460
  78.0 76.4 %collective-permute-start.10 = (bf16[2048,1024]{1,0:T(8,128)(2,1)}, bf16[2048,1024]{1,0:T(8,128)(2,1)}, u32[]{:S(2)}, u32[]{:S(2)}) collective-permute-start(bf16[2048,1024]{1,0:T(8,128)(2,1)} %shard_map.79.refs_1_), channel_id=1, source_target_pairs={{8,12},{12,8},{16,20},{20,16},{9,13},{13,9},{17,21},{21,17},{10,14... | collective-permute-start | bytes 12582920 | tf_op jit(solution)/shard_map/ppermute | solution.py:251
  82.6 21.8 %collective-permute-start.7 = (bf16[512,1024]{1,0:T(8,128)(2,1)S(1)}, bf16[512,1024]{1,0:T(8,128)(2,1)S(1)}, u32[]{:S(2)}, u32[]{:S(2)}) collective-permute-start(bf16[512,1024]{1,0:T(8,128)(2,1)S(1)} %convert_element_type.96), channel_id=1, source_target_pairs={{0,4},{4,0},{1,5},{5,1},{2,6},{6,2},{3,7},{7,3}} | collective-permute-start | bytes 3145736 | tf_op jit(solution)/shard_map/ppermute | solution.py:251
  105.0 17.2 %collective-permute-start.8 = (bf16[2,128,1024]{2,1,0:T(8,128)(2,1)S(1)}, bf16[2,128,1024]{2,1,0:T(8,128)(2,1)S(1)}, u32[]{:S(2)}, u32[]{:S(2)}) collective-permute-start(bf16[2,128,1024]{2,1,0:T(8,128)(2,1)S(1)} %pad_maximum_fusion), channel_id=1, source_target_pairs={{0,1},{1,0},{2,3},{3,2},{4,5},{5,4},{6,7},{7,6}} | collective-permute-start | bytes 1572872 | tf_op jit(solution)/shard_map/ppermute | solution.py:251
  107.7 19.5 %copy-start.6 = (s32[1,128]{1,0:T(1,128)S(1)}, s32[1,128]{1,0:T(1,128)}, u32[]{:S(2)}) copy-start(s32[1,128]{1,0:T(1,128)} %param.11) | copy-start | bytes 1540
  123.1 17.6 %collective-permute-start.9 = (bf16[1,128,1024]{2,1,0:T(8,128)(2,1)}, bf16[1,128,1024]{2,1,0:T(8,128)(2,1)S(1)}, u32[]{:S(2)}, u32[]{:S(2)}) collective-permute-start(bf16[1,128,1024]{2,1,0:T(8,128)(2,1)} %slice.65), channel_id=1, source_target_pairs={{0,2},{1,3},{2,0},{3,1},{4,6},{5,7},{6,4},{7,5}} | collective-permute-start | bytes 786440 | tf_op jit(solution)/shard_map/ppermute | solution.py:251
  154.5 13.9 %collective-permute-start.11 = (bf16[2048,1024]{1,0:T(8,128)(2,1)}, bf16[2048,1024]{1,0:T(8,128)(2,1)}, u32[]{:S(2)}, u32[]{:S(2)}) collective-permute-start(bf16[2048,1024]{1,0:T(8,128)(2,1)} %shard_map.77.refs_1_.refs_2_), channel_id=1, source_target_pairs={{8,10},{11,9},{16,18},{19,17},{12,14},{15,13},{20,22},{23,21}} | collective-permute-start | bytes 12582920 | tf_op jit(solution)/shard_map/ppermute | solution.py:251
  157.1 13.7 %collective-permute-start.12 = (bf16[2048,1024]{1,0:T(8,128)(2,1)}, bf16[2048,1024]{1,0:T(8,128)(2,1)}, u32[]{:S(2)}, u32[]{:S(2)}) collective-permute-start(bf16[2048,1024]{1,0:T(8,128)(2,1)} %collective-permute-done.1.refs_4_), channel_id=1, source_target_pairs={{10,11},{9,8},{18,19},{17,16},{14,15},{13,12},{22,23},{21,20}} | collective-permute-start | bytes 12582920 | tf_op jit(solution)/shard_map/ppermute | solution.py:251
  159.8 11.1 %collective-permute-start.13 = (bf16[2048,1024]{1,0:T(8,128)(2,1)}, bf16[2048,1024]{1,0:T(8,128)(2,1)}, u32[]{:S(2)}, u32[]{:S(2)}) collective-permute-start(bf16[2048,1024]{1,0:T(8,128)(2,1)} %collective-permute-done.10.refs_7_), channel_id=1, source_target_pairs={{8,9},{9,8},{10,11},{11,10},{16,17},{17,16},{18,19},{19,18},{12,13... | collective-permute-start | bytes 12582920 | tf_op jit(solution)/shard_map/ppermute | solution.py:251
  162.4 8.5 %collective-permute-start.14 = (bf16[2048,1024]{1,0:T(8,128)(2,1)}, bf16[2048,1024]{1,0:T(8,128)(2,1)}, u32[]{:S(2)}, u32[]{:S(2)}) collective-permute-start(bf16[2048,1024]{1,0:T(8,128)(2,1)} %collective-permute-done.10.refs_7_), channel_id=1, source_target_pairs={{8,11},{9,10},{10,9},{11,8},{16,19},{17,18},{18,17},{19,16},{12,15... | collective-permute-start | bytes 12582920 | tf_op jit(solution)/shard_map/ppermute | solution.py:251
  165.0 139.3 %collective-permute-start.23 = (bf16[2048,1024]{1,0:T(8,128)(2,1)}, bf16[2048,1024]{1,0:T(8,128)(2,1)S(1)}, u32[]{:S(2)}, u32[]{:S(2)}) collective-permute-start(bf16[2048,1024]{1,0:T(8,128)(2,1)} %shard_map.79.refs_1_), channel_id=1, source_target_pairs={{0,4},{4,0},{24,28},{28,24},{1,5},{5,1},{25,29},{29,25},{2,6},{6,2... | collective-permute-start | bytes 12582920 | tf_op jit(solution)/shard_map/ppermute | solution.py:251
  168.4 69.6 %collective-permute-start.16 = (bf16[128,8192]{1,0:T(8,128)(2,1)}, bf16[128,8192]{1,0:T(8,128)(2,1)S(1)}, u32[]{:S(2)}, u32[]{:S(2)}) collective-permute-start(bf16[128,8192]{1,0:T(8,128)(2,1)} %shard_map.81.held_ref), channel_id=1, source_target_pairs={{0,4},{4,0},{1,5},{5,1},{2,6},{6,2},{3,7},{7,3}} | collective-permute-start | bytes 6291464 | tf_op jit(solution)/shard_map/ppermute | solution.py:251
  171.6 115.4 %collective-permute-start.15 = (bf16[16,128]{1,0:T(8,128)(2,1)S(1)}, bf16[16,128]{1,0:T(8,128)(2,1)S(1)}, u32[]{:S(2)}, u32[]{:S(2)}) collective-permute-start(bf16[16,128]{1,0:T(8,128)(2,1)S(1)} %slice.49), channel_id=1, source_target_pairs={{8,0},{9,1},{10,2},{11,3},{16,24},{17,25},{18,26},{19,27},{12,4},{... | collective-permute-start | bytes 12296 | tf_op jit(solution)/shard_map/ppermute | solution.py:251
  287.0 21.7 %collective-permute-start.18 = (bf16[128,8192]{1,0:T(8,128)(2,1)S(1)}, bf16[128,8192]{1,0:T(8,128)(2,1)}, u32[]{:S(2)}, u32[]{:S(2)}) collective-permute-start(bf16[128,8192]{1,0:T(8,128)(2,1)S(1)} %collective-permute-done.16), channel_id=1, source_target_pairs={{0,8},{4,12},{1,9},{5,13},{2,10},{6,14},{3,11},{7,15}} | collective-permute-start | bytes 6291464 | tf_op jit(solution)/shard_map/ppermute | solution.py:251
  290.4 39.1 %collective-permute-start.20 = (bf16[2048,1024]{1,0:T(8,128)(2,1)}, bf16[2048,1024]{1,0:T(8,128)(2,1)}, u32[]{:S(2)}, u32[]{:S(2)}) collective-permute-start(bf16[2048,1024]{1,0:T(8,128)(2,1)} %collective-permute-done.14.refs_9_), channel_id=1, source_target_pairs={{10,11},{9,8},{18,19},{17,16},{14,15},{13,12},{22,23},{21,20}} | collective-permute-start | bytes 12582920 | tf_op jit(solution)/shard_map/ppermute | solution.py:251
  293.0 36.5 %collective-permute-start.19 = (bf16[2048,1024]{1,0:T(8,128)(2,1)}, bf16[2048,1024]{1,0:T(8,128)(2,1)}, u32[]{:S(2)}, u32[]{:S(2)}) collective-permute-start(bf16[2048,1024]{1,0:T(8,128)(2,1)} %collective-permute-done.10.refs_7_), channel_id=1, source_target_pairs={{8,10},{11,9},{16,18},{19,17},{12,14},{15,13},{20,22},{23,21}} | collective-permute-start | bytes 12582920 | tf_op jit(solution)/shard_map/ppermute | solution.py:251
  295.7 21.1 %collective-permute-start.17 = (bf16[128,8192]{1,0:T(8,128)(2,1)}, bf16[128,8192]{1,0:T(8,128)(2,1)S(1)}, u32[]{:S(2)}, u32[]{:S(2)}) collective-permute-start(bf16[128,8192]{1,0:T(8,128)(2,1)} %shard_map.81.held_ref), channel_id=1, source_target_pairs={{0,8},{4,12},{1,9},{5,13},{2,10},{6,14},{3,11},{7,15}} | collective-permute-start | bytes 6291464 | tf_op jit(solution)/shard_map/ppermute | solution.py:251
  306.7 124.3 %collective-permute-start.24 = (bf16[4096,1024]{1,0:T(8,128)(2,1)}, bf16[4096,1024]{1,0:T(8,128)(2,1)}, u32[]{:S(2)}, u32[]{:S(2)}) collective-permute-start(bf16[4096,1024]{1,0:T(8,128)(2,1)} %constant_dynamic-update-slice_fusion.4.refs_2_), channel_id=1, source_target_pairs={{0,1},{1,0},{2,3},{3,2},{24,25},{25,24},{26,27},{27,26},{4,5},{5,4... | collective-permute-start | bytes 25165832 | tf_op jit(solution)/shard_map/ppermute | solution.py:251
  308.6 215.3 %collective-permute-start.25 = (bf16[4096,1024]{1,0:T(8,128)(2,1)}, bf16[4096,1024]{1,0:T(8,128)(2,1)}, u32[]{:S(2)}, u32[]{:S(2)}) collective-permute-start(bf16[4096,1024]{1,0:T(8,128)(2,1)} %constant_dynamic-update-slice_fusion.4.refs_2_), channel_id=1, source_target_pairs={{0,3},{1,2},{2,1},{3,0},{24,27},{25,26},{26,25},{27,24},{4,7},{5,6... | collective-permute-start | bytes 25165832 | tf_op jit(solution)/shard_map/ppermute | solution.py:251
  316.8 5.4 copy-start.2
  337.8 0.8 collective-permute-start.21
  338.6 201.5 %copy-start.1 = (bf16[128,8192]{1,0:T(8,128)(2,1)}, bf16[128,8192]{1,0:T(8,128)(2,1)S(1)}, u32[]{:S(2)}) copy-start(bf16[128,8192]{1,0:T(8,128)(2,1)S(1)} %collective-permute-done.21.x_ref) | copy-start | bytes 6291460
  338.6 2.7 collective-permute-start.22
  524.0 95.5 %collective-permute-start.28 = (bf16[4096,1024]{1,0:T(8,128)(2,1)}, bf16[4096,1024]{1,0:T(8,128)(2,1)}, u32[]{:S(2)}, u32[]{:S(2)}) collective-permute-start(bf16[4096,1024]{1,0:T(8,128)(2,1)} %constant_dynamic-update-slice_fusion.4.refs_2_), channel_id=1, source_target_pairs={{0,2},{3,1},{24,26},{27,25},{4,6},{7,5},{28,30},{31,29}} | collective-permute-start | bytes 25165832 | tf_op jit(solution)/shard_map/ppermute | solution.py:251
  531.5 95.6 %collective-permute-start.29 = (bf16[4096,1024]{1,0:T(8,128)(2,1)}, bf16[4096,1024]{1,0:T(8,128)(2,1)}, u32[]{:S(2)}, u32[]{:S(2)}) collective-permute-start(bf16[4096,1024]{1,0:T(8,128)(2,1)} %collective-permute-done.25.refs_4_), channel_id=1, source_target_pairs={{2,3},{1,0},{26,27},{25,24},{6,7},{5,4},{30,31},{29,28}} | collective-permute-start | bytes 25165832 | tf_op jit(solution)/shard_map/ppermute | solution.py:251
  550.9 0.8 collective-permute-start.26
  551.7 12.1 %copy-start.3 = (bf16[128,8192]{1,0:T(8,128)(2,1)}, bf16[128,8192]{1,0:T(8,128)(2,1)S(1)}, u32[]{:S(2)}) copy-start(bf16[128,8192]{1,0:T(8,128)(2,1)S(1)} %collective-permute-done.26.x_ref) | copy-start | bytes 6291460
  551.7 5.3 collective-permute-start.27

commit v2 on v1

--- a/solution.py
+++ b/solution.py
@@ -19,7 +19,7 @@
 
 epsilon = 1e-05
 clip_ratio = 2.0
-FAR, RELAYED = 4, 5
+INNER, RELAYED = 4, 5
 FIXED = 4
 VMEM = 60 << 20
 SHORT = pl.CostEstimate(flops=0, bytes_accessed=0, transcendentals=0)
@@ -290,19 +290,16 @@
 
     halves = [[(0, 0)], [(j, (j - 1) * depth) for j in range(1, tensors)], [(j, j * depth) for j in range(tensors)]]
 
-    def far(at, blocks):
-        return over("dp", dps, blocks[0], [(s, s, a, b) for s in at for a, b in ((0, 2), (3, 1))])
+    def across(at, blocks):
+        return over("dp", dps, blocks[0], [(s, s, a, b) for s in at for a, b in ((1, 2), (2, 1))])
 
     def relayed(at, blocks):
-        return over("dp", dps, blocks[3], [(s, s, a, b) for s in at for a, b in ((2, 3), (1, 0))])
-
-    def around(at, blocks):
-        return over_dp(jnp.where(inner == 1, blocks[3], blocks[0]), at, (2, 0, 3, 1))
+        return over("dp", dps, blocks[2], [(s, s, a, b) for s in at for a, b in ((2, 3), (1, 0))])
 
     def terms_of(half, blocks, which, shift=0):
         terms = []
         for name in which:
-            b, has = {FAR: (2, inner), RELAYED: (2, 1 - inner)}.get(name, (name, None))
+            b, has = {INNER: (3, inner), RELAYED: (3, 1 - inner)}.get(name, (name, None))
             source = dp ^ b
             terms.append((blocks[name], has, [
                 (j, source * depth + shift, ((tensor ^ j) * dps + source) * depth, start, depth)
@@ -310,7 +307,7 @@
             ]))
         return terms
 
-    everything = (0, 1, 3, FAR, RELAYED)
+    everything = (0, 1, 2, INNER, RELAYED)
 
     def placing(active):
         return (active, tensor * own_width % served, own_width)
@@ -332,7 +329,7 @@
         received = [over_tensor(kept[j], at, j) for j in range(1, tensors)]
         return received[0] if len(received) == 1 else jnp.concatenate(received, axis=0)
 
-    own = {0: kept[0], 3: over_dp(kept[0], early, flipped(3)), 1: over_dp(kept[0], early, flipped(1))}
+    own = {0: kept[0], 2: over_dp(kept[0], early, flipped(2)), 1: over_dp(kept[0], early, flipped(1))}
 
     lhs = [jnp.concatenate(first, axis=0)]
     partial = [project(turn[0], lhs, [(kept[j], None, [(0, 0, 0, 0, depth)])]) for j in range(tensors)]
@@ -351,37 +348,37 @@
     fresh = total[0]
     result = attended(0, hidden, fresh, hidden)
 
-    rest[3], rest[1] = over_dp(rest[0], early, flipped(3)), over_dp(rest[0], early, flipped(1))
+    rest[2], rest[1] = over_dp(rest[0], early, flipped(2)), over_dp(rest[0], early, flipped(1))
     own, result, kept = together(own, result, kept)
     parts = both(result, 0)
     late_rest = others(late, kept)
     kept_back, rest[0] = together(own, rest[0])
-    own[RELAYED], own[FAR] = relayed(early, kept_back), far(early, kept_back)
+    own[RELAYED], own[INNER] = relayed(early, kept_back), across(early, kept_back)
     own, rest = together(own, rest)
-    rest[RELAYED], rest[FAR] = relayed(early, rest), far(early, rest)
-    token = over("dp", dps, rest[3][:ROW_TILE, :HD], [(a, b, z, z) for a, b in ((1, 0), (2, 3)) for z in range(dps)])
+    rest[RELAYED], rest[INNER] = relayed(early, rest), across(early, rest)
+    token = over("dp", dps, rest[2][:ROW_TILE, :HD], [(a, b, z, z) for a, b in ((1, 0), (2, 3)) for z in range(dps)])
     token, late_own, parts = together(token, kept[0], parts)
     whole = jnp.concatenate([late_own, late_rest], axis=0)
     shift = jnp.isnan(token[0, 0]).astype(jnp.int32)
-    last = {0: whole, 3: over_dp(whole, late, flipped(3)), 1: over_dp(whole, late, flipped(1))}
+    last = {0: whole, 2: over_dp(whole, late, flipped(2)), 1: over_dp(whole, late, flipped(1))}
 
     moved = [hop(part, 1) for part in parts]
     normed = prepared(moved)
-    terms = terms_of(0, own, everything) + terms_of(1, rest, (0, 1, 3))
+    terms = terms_of(0, own, everything) + terms_of(1, rest, (0, 1, 2))
     fresh, rollout = project(turn[1], normed, terms, None, placing(is_early))
     fresh, rollout, rest = together(fresh, rollout, rest)
-    fresh, rollout = project(turn[1], normed, terms_of(1, rest, (FAR, RELAYED)), fresh, placing(is_early), rollout)
+    fresh, rollout = project(turn[1], normed, terms_of(1, rest, (INNER, RELAYED)), fresh, placing(is_early), rollout)
     result = attended(1, moved[0], fresh, result)
 
     terms = terms_of(0, own, everything) + terms_of(1, rest, everything)
     moved, last = together(both(hop(result, 2), 2), last)
-    last[RELAYED], last[FAR] = relayed(late, last), far(late, last)
+    last[RELAYED], last[INNER] = relayed(late, last), across(late, last)
     result = attended(2, moved[0], project(turn[2], prepared(moved), terms), result)
     moved = both(hop(result, 3), 3)
     normed = prepared(moved)
-    fresh, rollout = project(turn[3], normed, terms_of(2, last, (0, 1, 3), shift), None, placing(1 - is_early), rollout)
+    fresh, rollout = project(turn[3], normed, terms_of(2, last, (0, 1, 2), shift), None, placing(1 - is_early), rollout)
     fresh, rollout, last = together(fresh, rollout, last)
-    fresh, rollout = project(turn[3], normed, terms_of(2, last, (FAR, RELAYED)), fresh, placing(1 - is_early), rollout)
+    fresh, rollout = project(turn[3], normed, terms_of(2, last, (INNER, RELAYED)), fresh, placing(1 - is_early), rollout)
     result = attended(3, moved[0], fresh, result)
     return (rollout[None], result[None, None])
 

time: 644 us -> 637 us (0.989)
  transfers between devices with their start and end apart: 30 -> 30, of which waited for: 13 -> 11; matrix products, arithmetic and copies ran while one was open for 7% -> 7% of each run, Pallas kernels for 12% -> 12%
where the time goes in v2:
time: 637 us; the launch traced here: 636 us
  waiting for transfers between devices  406 us (64%)
  Pallas kernels  99.6 us (16%)
  starting transfers between devices  78.4 us (12%)
  other arithmetic  28 us (4%)
  local copies, waits for them, and re-layouts  21.5 us (3%)
    ppermute x30, waiting for transfers between devices, over(): return lax.ppermute(value, ('section', axis), pairs)  406 us
    ppermute x30, starting transfers between devices, over(): return lax.ppermute(value, ('section', axis), pairs)  78.4 us
    pallas_call x7, Pallas kernels, project(): pl.pallas_call(functools.partial(project_kernel, layout, len(lhs), bool(a...  67.5 us
    pallas_call x4, Pallas kernels, attend(): pl.pallas_call(functools.partial(attend_kernel, share), out_shape=jax.Sha...  21.6 us
    convert_element_type x4, other arithmetic, normed_of(): (part.astype(jnp.float32) * inverse[:, None] * gain.astype(jnp.float32))....  15 us
  transfers between devices with their start and end apart: 30, of which 11 were waited for; matrix products, arithmetic and copies ran while one was open for 7% of the time, Pallas kernels for 12%

profile of v2, /device:TPU:0, one launch (start us, length us, event | category | flops | bytes accessed | tf_op | source)
XLA Modules:
  0.0 635.7 jit_solution(10774056267711333864)
XLA Ops:
  0.7 5.3 shard_map.77.refs_1_.refs_2_
  6.5 4.9 collective-permute-start.2
  11.5 1.4 collective-permute-done.2
  14.7 4.0 collective-permute-start.3
  18.7 4.5 collective-permute-start.4
  23.2 1.9 collective-permute-start.5
  25.1 2.6 collective-permute-start
  27.8 2.7 collective-permute-start.1
  31.2 5.2 shard_map.79.refs_1_
  36.3 15.6 %collective-permute-done.3 = bf16[128,2048]{1,0:T(8,128)(2,1)S(1)} collective-permute-done((bf16[128,2048]{1,0:T(8,128)(2,1)}, bf16[128,2048]{1,0:T(8,128)(2,1)S(1)}, u32[]{:S(2)}, u32[]{:S(2)}) %collective-permute-start.3) | collective-permute-done | bytes 524320 | tf_op jit(solution)/shard_map/ppermute | solution.py:251
  52.0 4.8 collective-permute-done.5
  57.6 1.5 collective-permute-start.6
  60.0 1.9 constant_dynamic-update-slice_fusion.1
  61.8 1.9 constant_dynamic-update-slice_fusion.refs_0_
  63.7 7.2 %shard_map.78 = f32[512,1024]{1,0:T(8,128)} custom-call(s32[7]{0:T(128)} %stack.73.where_ref, bf16[512,2048]{1,0:T(8,128)(2,1)} %constant_dynamic-update-slice_fusion.refs_0_, bf16[2048,1024]{1,0:T(8,128)(2,1)} %shard_map.77.refs_1_.refs_2_), custom_call_target="tpu_custom_call" | custom-call | tf_op jit(solution)/shard_map/pallas_call | solution.py:146
  70.9 7.1 %shard_map.80 = f32[512,1024]{1,0:T(8,128)} custom-call(s32[7]{0:T(128)} %stack.73.where_ref, bf16[512,2048]{1,0:T(8,128)(2,1)} %constant_dynamic-update-slice_fusion.refs_0_, bf16[2048,1024]{1,0:T(8,128)(2,1)} %shard_map.79.refs_1_), custom_call_target="tpu_custom_call" | custom-call | tf_op jit(solution)/shard_map/pallas_call | solution.py:146
  78.0 2.8 collective-permute-start.10
  80.8 1.7 convert_element_type.96
  82.6 2.4 collective-permute-start.7
  85.0 19.5 %collective-permute-done.7 = bf16[512,1024]{1,0:T(8,128)(2,1)S(1)} collective-permute-done((bf16[512,1024]{1,0:T(8,128)(2,1)S(1)}, bf16[512,1024]{1,0:T(8,128)(2,1)S(1)}, u32[]{:S(2)}, u32[]{:S(2)}) %collective-permute-start.7) | collective-permute-done | bytes 1048608 | tf_op jit(solution)/shard_map/ppermute | solution.py:251
  105.1 2.4 collective-permute-start.8
  107.6 19.8 %collective-permute-done.8 = bf16[2,128,1024]{2,1,0:T(8,128)(2,1)S(1)} collective-permute-done((bf16[2,128,1024]{2,1,0:T(8,128)(2,1)S(1)}, bf16[2,128,1024]{2,1,0:T(8,128)(2,1)S(1)}, u32[]{:S(2)}, u32[]{:S(2)}) %collective-permute-start.8) | collective-permute-done | bytes 524320 | tf_op jit(solution)/shard_map/ppermute | solution.py:251
  128.3 1.9 collective-permute-start.9
  130.3 1.3 copy.18.held_ref
  133.5 7.3 %collective-permute-done.9 = bf16[1,128,1024]{2,1,0:T(8,128)(2,1)S(1)} collective-permute-done((bf16[1,128,1024]{2,1,0:T(8,128)(2,1)}, bf16[1,128,1024]{2,1,0:T(8,128)(2,1)S(1)}, u32[]{:S(2)}, u32[]{:S(2)}) %collective-permute-start.9) | collective-permute-done | bytes 262176 | tf_op jit(solution)/shard_map/ppermute | solution.py:251
  141.7 12.8 %shard_map.81.held_ref = bf16[128,8192]{1,0:T(8,128)(2,1)} custom-call(s32[1]{0:T(128)} %bitcast.14.active_ref, f32[8,16,256]{2,1,0:T(8,128)} %and_select_fusion.bias_ref, bf16[128,8192]{1,0:T(8,128)(2,1)} %bitcast.60, bf16[128,8192]{1,0:T(8,128)(2,1)} %bitcast.54, bf16[128,16,2048]{2,1,0:T(8,128)(2,1)} %bitcast.49, ...), custom_call_target="tpu_custom_call", output_to_operand_aliasing={{}: (6, {})} | custom-call | tf_op jit(solution)/shard_map/pallas_call | solution.py:211
  154.6 2.6 collective-permute-start.11
  157.2 2.6 collective-permute-start.12
  159.8 2.6 collective-permute-start.13
  162.5 2.6 collective-permute-start.14
  165.1 3.4 collective-permute-start.23
  168.5 2.4 collective-permute-start.16
  171.6 1.3 collective-permute-start.15
  172.9 65.2 %collective-permute-done.16 = bf16[128,8192]{1,0:T(8,128)(2,1)S(1)} collective-permute-done((bf16[128,8192]{1,0:T(8,128)(2,1)}, bf16[128,8192]{1,0:T(8,128)(2,1)S(1)}, u32[]{:S(2)}, u32[]{:S(2)}) %collective-permute-start.16) | collective-permute-done | bytes 2097184 | tf_op jit(solution)/shard_map/ppermute | solution.py:251
  238.1 45.9 %collective-permute-done.15 = bf16[16,128]{1,0:T(8,128)(2,1)S(1)} collective-permute-done((bf16[16,128]{1,0:T(8,128)(2,1)S(1)}, bf16[16,128]{1,0:T(8,128)(2,1)S(1)}, u32[]{:S(2)}, u32[]{:S(2)}) %collective-permute-start.15) | collective-permute-done | bytes 4128 | tf_op jit(solution)/shard_map/ppermute | solution.py:251
  284.0 3.4 collective-permute-start.18
  287.4 2.6 collective-permute-start.20
  290.0 2.7 collective-permute-start.19
  292.7 1.4 collective-permute-start.17
  294.1 4.7 constant_dynamic-update-slice_fusion.5
  298.8 2.4 constant_dynamic-update-slice_fusion.4.refs_2_
  301.2 5.4 collective-permute-start.24
  306.7 2.9 collective-permute-start.25
  311.1 2.1 fusion.3
  313.7 4.9 fusion.8
  318.6 7.3 %shard_map.82 = (f32[128,1024]{1,0:T(8,128)}, bf16[16384,1024]{1,0:T(8,128)(2,1)}) custom-call(s32[28]{0:T(128)} %stack.88.where_ref, bf16[128,8192]{1,0:T(8,128)(2,1)} %get-tuple-element.144.refs_0_, bf16[128,8192]{1,0:T(8,128)(2,1)} %get-tuple-element.145.refs_1_.refs_0_, bf16[2048,1024]{1,0:T(8,128)(2,1)} %shard_map.77.refs_1_.refs_2_, ...), custom_call_target="tpu_custom_call" | custom-call | tf_op jit(solution)/shard_map/pallas_call | solution.py:146
  325.9 5.3 shard_map.83
  331.2 2.9 shard_map.84.held_ref
  335.0 2.0 collective-permute-start.22
  337.6 145.7 %collective-permute-done.24.refs_3_ = bf16[4096,1024]{1,0:T(8,128)(2,1)} collective-permute-done((bf16[4096,1024]{1,0:T(8,128)(2,1)}, bf16[4096,1024]{1,0:T(8,128)(2,1)}, u32[]{:S(2)}, u32[]{:S(2)}) %collective-permute-start.24) | collective-permute-done | bytes 8388640 | tf_op jit(solution)/shard_map/ppermute | solution.py:251
  483.3 37.9 %collective-permute-done.25.refs_4_ = bf16[4096,1024]{1,0:T(8,128)(2,1)} collective-permute-done((bf16[4096,1024]{1,0:T(8,128)(2,1)}, bf16[4096,1024]{1,0:T(8,128)(2,1)}, u32[]{:S(2)}, u32[]{:S(2)}) %collective-permute-start.25) | collective-permute-done | bytes 8388640 | tf_op jit(solution)/shard_map/ppermute | solution.py:251
  521.2 3.9 collective-permute-start.28
  525.1 1.3 collective-permute-start.29
  526.4 2.5 fusion.9
  528.9 4.8 fusion.14
  533.7 7.9 %shard_map.85.f_ref = f32[128,1024]{1,0:T(8,128)} custom-call(s32[34]{0:T(128)} %stack.89.where_ref, bf16[128,8192]{1,0:T(8,128)(2,1)} %get-tuple-element.143.refs_0_, bf16[128,8192]{1,0:T(8,128)(2,1)} %get-tuple-element.142.refs_1_, bf16[2048,1024]{1,0:T(8,128)(2,1)} %shard_map.77.refs_1_.refs_2_, bf16[2048,1024]{1,0:T(8,128)(2,1)} %collective-permute-done.refs_3_, ...), custom_call_target="tpu_custom_call" | custom-call | tf_op jit(solution)/shard_map/pallas_call | solution.py:146
  541.6 2.9 shard_map.86.held_ref
  545.3 2.0 collective-permute-start.27
  550.6 2.1 fusion.18
  552.7 4.7 fusion.20
  557.4 20.7 %shard_map.87 = (f32[128,1024]{1,0:T(8,128)}, bf16[16384,1024]{1,0:T(8,128)(2,1)}) custom-call(s32[19]{0:T(128)} %stack.93.where_ref, bf16[128,8192]{1,0:T(8,128)(2,1)} %get-tuple-element.141.refs_0_, bf16[128,8192]{1,0:T(8,128)(2,1)} %get-tuple-element.140.refs_1_, ...), custom_call_target="tpu_custom_call", output_to_operand_aliasing={{1}: (6, {})} | custom-call | tf_op jit(solution)/shard_map/pallas_call | solution.py:146
  578.1 42.7 %collective-permute-done.29.refs_3_ = bf16[4096,1024]{1,0:T(8,128)(2,1)} collective-permute-done((bf16[4096,1024]{1,0:T(8,128)(2,1)}, bf16[4096,1024]{1,0:T(8,128)(2,1)}, u32[]{:S(2)}, u32[]{:S(2)}) %collective-permute-start.29) | collective-permute-done | bytes 8388640 | tf_op jit(solution)/shard_map/ppermute | solution.py:251
  620.8 12.0 %shard_map.88 = (f32[128,1024]{1,0:T(8,128)}, bf16[16384,1024]{1,0:T(8,128)(2,1)}) custom-call(s32[14]{0:T(128)} %stack.72.where_ref, bf16[128,8192]{1,0:T(8,128)(2,1)} %get-tuple-element.141.refs_0_, bf16[128,8192]{1,0:T(8,128)(2,1)} %get-tuple-element.140.refs_1_, ...), custom_call_target="tpu_custom_call", output_to_operand_aliasing={{1}: (6, {})} | custom-call | tf_op jit(solution)/shard_map/pallas_call | solution.py:146
  632.8 2.9 shard_map.89
  (73 shorter events, 16.2 us)
Async XLA Ops:
  0.6 5.4 copy-start
  0.7 10.7 %copy-start.5 = (bf16[1,8192]{1,0:T(2,128)(2,1)S(1)}, bf16[1,8192]{1,0:T(2,128)(2,1)}, u32[]{:S(2)}) copy-start(bf16[1,8192]{1,0:T(2,128)(2,1)} %param.7) | copy-start | bytes 49156
  6.5 6.4 %collective-permute-start.2 = (f32[128]{0:T(128)S(1)}, f32[128]{0:T(128)S(1)}, u32[]{:S(2)}, u32[]{:S(2)}) collective-permute-start(f32[128]{0:T(128)S(1)} %fusion), channel_id=1, source_target_pairs={{0,4},{4,0},{1,5},{5,1},{2,6},{6,2},{3,7},{7,3}} | collective-permute-start | bytes 1544 | tf_op jit(solution)/shard_map/ppermute | solution.py:251
  14.7 37.2 %collective-permute-start.3 = (bf16[128,2048]{1,0:T(8,128)(2,1)}, bf16[128,2048]{1,0:T(8,128)(2,1)S(1)}, u32[]{:S(2)}, u32[]{:S(2)}) collective-permute-start(bf16[128,2048]{1,0:T(8,128)(2,1)} %get-tuple-element.70), channel_id=1, source_target_pairs={{0,1},{1,0},{2,3},{3,2},{4,5},{5,4},{6,7},{7,6}} | collective-permute-start | bytes 1572872 | tf_op jit(solution)/shard_map/ppermute | solution.py:251
  18.7 33.3 %collective-permute-start.4 = (bf16[128,2048]{1,0:T(8,128)(2,1)}, bf16[128,2048]{1,0:T(8,128)(2,1)}, u32[]{:S(2)}, u32[]{:S(2)}) collective-permute-start(bf16[128,2048]{1,0:T(8,128)(2,1)} %get-tuple-element.71), channel_id=1, source_target_pairs={{0,2},{1,3},{2,0},{3,1},{4,6},{5,7},{6,4},{7,5}} | collective-permute-start | bytes 1572872 | tf_op jit(solution)/shard_map/ppermute | solution.py:251
  23.2 33.6 %collective-permute-start.5 = (bf16[128,2048]{1,0:T(8,128)(2,1)}, bf16[128,2048]{1,0:T(8,128)(2,1)}, u32[]{:S(2)}, u32[]{:S(2)}) collective-permute-start(bf16[128,2048]{1,0:T(8,128)(2,1)} %get-tuple-element.72), channel_id=1, source_target_pairs={{0,3},{1,2},{2,1},{3,0},{4,7},{5,6},{6,5},{7,4}} | collective-permute-start | bytes 1572872 | tf_op jit(solution)/shard_map/ppermute | solution.py:251
  25.1 129.4 %collective-permute-start = (bf16[2048,1024]{1,0:T(8,128)(2,1)}, bf16[2048,1024]{1,0:T(8,128)(2,1)}, u32[]{:S(2)}, u32[]{:S(2)}) collective-permute-start(bf16[2048,1024]{1,0:T(8,128)(2,1)} %shard_map.77.refs_1_.refs_2_), channel_id=1, source_target_pairs={{8,9},{9,8},{10,11},{11,10},{16,17},{17,16},{18,19},{19,18},{12,13... | collective-permute-start | bytes 12582920 | tf_op jit(solution)/shard_map/ppermute | solution.py:251
  27.8 126.8 %collective-permute-start.1 = (bf16[2048,1024]{1,0:T(8,128)(2,1)}, bf16[2048,1024]{1,0:T(8,128)(2,1)}, u32[]{:S(2)}, u32[]{:S(2)}) collective-permute-start(bf16[2048,1024]{1,0:T(8,128)(2,1)} %shard_map.77.refs_1_.refs_2_), channel_id=1, source_target_pairs={{8,10},{9,11},{10,8},{11,9},{16,18},{17,19},{18,16},{19,17},{12,14... | collective-permute-start | bytes 12582920 | tf_op jit(solution)/shard_map/ppermute | solution.py:251
  57.6 20.4 %collective-permute-start.6 = (bf16[1,8192]{1,0:T(2,128)(2,1)S(1)}, bf16[1,8192]{1,0:T(2,128)(2,1)S(1)}, u32[]{:S(2)}, u32[]{:S(2)}) collective-permute-start(bf16[1,8192]{1,0:T(2,128)(2,1)S(1)} %copy-done.5), channel_id=1, source_target_pairs={{0,4},{4,0},{8,12},{12,8},{16,20},{20,16},{24,28},{28,24},{1,5},{5... | collective-permute-start | bytes 49160 | tf_op jit(solution)/shard_map/ppermute | solution.py:251
  78.0 26.4 %copy-start.4 = (f32[512,1024]{1,0:T(8,128)S(1)}, f32[512,1024]{1,0:T(8,128)}, u32[]{:S(2)}) copy-start(f32[512,1024]{1,0:T(8,128)} %shard_map.78) | copy-start | bytes 6291460
  78.0 76.5 %collective-permute-start.10 = (bf16[2048,1024]{1,0:T(8,128)(2,1)}, bf16[2048,1024]{1,0:T(8,128)(2,1)}, u32[]{:S(2)}, u32[]{:S(2)}) collective-permute-start(bf16[2048,1024]{1,0:T(8,128)(2,1)} %shard_map.79.refs_1_), channel_id=1, source_target_pairs={{8,12},{12,8},{16,20},{20,16},{9,13},{13,9},{17,21},{21,17},{10,14... | collective-permute-start | bytes 12582920 | tf_op jit(solution)/shard_map/ppermute | solution.py:251
  82.6 21.9 %collective-permute-start.7 = (bf16[512,1024]{1,0:T(8,128)(2,1)S(1)}, bf16[512,1024]{1,0:T(8,128)(2,1)S(1)}, u32[]{:S(2)}, u32[]{:S(2)}) collective-permute-start(bf16[512,1024]{1,0:T(8,128)(2,1)S(1)} %convert_element_type.96), channel_id=1, source_target_pairs={{0,4},{4,0},{1,5},{5,1},{2,6},{6,2},{3,7},{7,3}} | collective-permute-start | bytes 3145736 | tf_op jit(solution)/shard_map/ppermute | solution.py:251
  105.1 22.3 %collective-permute-start.8 = (bf16[2,128,1024]{2,1,0:T(8,128)(2,1)S(1)}, bf16[2,128,1024]{2,1,0:T(8,128)(2,1)S(1)}, u32[]{:S(2)}, u32[]{:S(2)}) collective-permute-start(bf16[2,128,1024]{2,1,0:T(8,128)(2,1)S(1)} %pad_maximum_fusion), channel_id=1, source_target_pairs={{0,1},{1,0},{2,3},{3,2},{4,5},{5,4},{6,7},{7,6}} | collective-permute-start | bytes 1572872 | tf_op jit(solution)/shard_map/ppermute | solution.py:251
  107.6 24.5 %copy-start.6 = (s32[1,128]{1,0:T(1,128)S(1)}, s32[1,128]{1,0:T(1,128)}, u32[]{:S(2)}) copy-start(s32[1,128]{1,0:T(1,128)} %param.11) | copy-start | bytes 1540
  128.3 12.5 %collective-permute-start.9 = (bf16[1,128,1024]{2,1,0:T(8,128)(2,1)}, bf16[1,128,1024]{2,1,0:T(8,128)(2,1)S(1)}, u32[]{:S(2)}, u32[]{:S(2)}) collective-permute-start(bf16[1,128,1024]{2,1,0:T(8,128)(2,1)} %slice.65), channel_id=1, source_target_pairs={{0,2},{1,3},{2,0},{3,1},{4,6},{5,7},{6,4},{7,5}} | collective-permute-start | bytes 786440 | tf_op jit(solution)/shard_map/ppermute | solution.py:251
  154.6 13.9 %collective-permute-start.11 = (bf16[2048,1024]{1,0:T(8,128)(2,1)}, bf16[2048,1024]{1,0:T(8,128)(2,1)}, u32[]{:S(2)}, u32[]{:S(2)}) collective-permute-start(bf16[2048,1024]{1,0:T(8,128)(2,1)} %shard_map.77.refs_1_.refs_2_), channel_id=1, source_target_pairs={{9,10},{10,9},{17,18},{18,17},{13,14},{14,13},{21,22},{22,21}} | collective-permute-start | bytes 12582920 | tf_op jit(solution)/shard_map/ppermute | solution.py:251
  157.2 13.7 %collective-permute-start.12 = (bf16[2048,1024]{1,0:T(8,128)(2,1)}, bf16[2048,1024]{1,0:T(8,128)(2,1)}, u32[]{:S(2)}, u32[]{:S(2)}) collective-permute-start(bf16[2048,1024]{1,0:T(8,128)(2,1)} %collective-permute-done.1.refs_4_), channel_id=1, source_target_pairs={{10,11},{9,8},{18,19},{17,16},{14,15},{13,12},{22,23},{21,20}} | collective-permute-start | bytes 12582920 | tf_op jit(solution)/shard_map/ppermute | solution.py:251
  159.8 11.1 %collective-permute-start.13 = (bf16[2048,1024]{1,0:T(8,128)(2,1)}, bf16[2048,1024]{1,0:T(8,128)(2,1)}, u32[]{:S(2)}, u32[]{:S(2)}) collective-permute-start(bf16[2048,1024]{1,0:T(8,128)(2,1)} %collective-permute-done.10.refs_7_), channel_id=1, source_target_pairs={{8,9},{9,8},{10,11},{11,10},{16,17},{17,16},{18,19},{19,18},{12,13... | collective-permute-start | bytes 12582920 | tf_op jit(solution)/shard_map/ppermute | solution.py:251
  162.5 8.5 %collective-permute-start.14 = (bf16[2048,1024]{1,0:T(8,128)(2,1)}, bf16[2048,1024]{1,0:T(8,128)(2,1)}, u32[]{:S(2)}, u32[]{:S(2)}) collective-permute-start(bf16[2048,1024]{1,0:T(8,128)(2,1)} %collective-permute-done.10.refs_7_), channel_id=1, source_target_pairs={{8,10},{9,11},{10,8},{11,9},{16,18},{17,19},{18,16},{19,17},{12,14... | collective-permute-start | bytes 12582920 | tf_op jit(solution)/shard_map/ppermute | solution.py:251
  165.1 133.7 %collective-permute-start.23 = (bf16[2048,1024]{1,0:T(8,128)(2,1)}, bf16[2048,1024]{1,0:T(8,128)(2,1)S(1)}, u32[]{:S(2)}, u32[]{:S(2)}) collective-permute-start(bf16[2048,1024]{1,0:T(8,128)(2,1)} %shard_map.79.refs_1_), channel_id=1, source_target_pairs={{0,4},{4,0},{24,28},{28,24},{1,5},{5,1},{25,29},{29,25},{2,6},{6,2... | collective-permute-start | bytes 12582920 | tf_op jit(solution)/shard_map/ppermute | solution.py:251
  168.5 69.6 %collective-permute-start.16 = (bf16[128,8192]{1,0:T(8,128)(2,1)}, bf16[128,8192]{1,0:T(8,128)(2,1)S(1)}, u32[]{:S(2)}, u32[]{:S(2)}) collective-permute-start(bf16[128,8192]{1,0:T(8,128)(2,1)} %shard_map.81.held_ref), channel_id=1, source_target_pairs={{0,4},{4,0},{1,5},{5,1},{2,6},{6,2},{3,7},{7,3}} | collective-permute-start | bytes 6291464 | tf_op jit(solution)/shard_map/ppermute | solution.py:251
  171.6 112.3 %collective-permute-start.15 = (bf16[16,128]{1,0:T(8,128)(2,1)S(1)}, bf16[16,128]{1,0:T(8,128)(2,1)S(1)}, u32[]{:S(2)}, u32[]{:S(2)}) collective-permute-start(bf16[16,128]{1,0:T(8,128)(2,1)S(1)} %slice.49), channel_id=1, source_target_pairs={{8,0},{9,1},{10,2},{11,3},{16,24},{17,25},{18,26},{19,27},{12,4},{... | collective-permute-start | bytes 12296 | tf_op jit(solution)/shard_map/ppermute | solution.py:251
  284.0 22.7 %collective-permute-start.18 = (bf16[128,8192]{1,0:T(8,128)(2,1)S(1)}, bf16[128,8192]{1,0:T(8,128)(2,1)}, u32[]{:S(2)}, u32[]{:S(2)}) collective-permute-start(bf16[128,8192]{1,0:T(8,128)(2,1)S(1)} %collective-permute-done.16), channel_id=1, source_target_pairs={{0,8},{4,12},{1,9},{5,13},{2,10},{6,14},{3,11},{7,15}} | collective-permute-start | bytes 6291464 | tf_op jit(solution)/shard_map/ppermute | solution.py:251
  287.4 38.5 %collective-permute-start.20 = (bf16[2048,1024]{1,0:T(8,128)(2,1)}, bf16[2048,1024]{1,0:T(8,128)(2,1)}, u32[]{:S(2)}, u32[]{:S(2)}) collective-permute-start(bf16[2048,1024]{1,0:T(8,128)(2,1)} %collective-permute-done.14.refs_9_), channel_id=1, source_target_pairs={{10,11},{9,8},{18,19},{17,16},{14,15},{13,12},{22,23},{21,20}} | collective-permute-start | bytes 12582920 | tf_op jit(solution)/shard_map/ppermute | solution.py:251
  290.0 35.8 %collective-permute-start.19 = (bf16[2048,1024]{1,0:T(8,128)(2,1)}, bf16[2048,1024]{1,0:T(8,128)(2,1)}, u32[]{:S(2)}, u32[]{:S(2)}) collective-permute-start(bf16[2048,1024]{1,0:T(8,128)(2,1)} %collective-permute-done.10.refs_7_), channel_id=1, source_target_pairs={{9,10},{10,9},{17,18},{18,17},{13,14},{14,13},{21,22},{22,21}} | collective-permute-start | bytes 12582920 | tf_op jit(solution)/shard_map/ppermute | solution.py:251
  292.7 20.5 %collective-permute-start.17 = (bf16[128,8192]{1,0:T(8,128)(2,1)}, bf16[128,8192]{1,0:T(8,128)(2,1)S(1)}, u32[]{:S(2)}, u32[]{:S(2)}) collective-permute-start(bf16[128,8192]{1,0:T(8,128)(2,1)} %shard_map.81.held_ref), channel_id=1, source_target_pairs={{0,8},{4,12},{1,9},{5,13},{2,10},{6,14},{3,11},{7,15}} | collective-permute-start | bytes 6291464 | tf_op jit(solution)/shard_map/ppermute | solution.py:251
  301.2 182.1 %collective-permute-start.24 = (bf16[4096,1024]{1,0:T(8,128)(2,1)}, bf16[4096,1024]{1,0:T(8,128)(2,1)}, u32[]{:S(2)}, u32[]{:S(2)}) collective-permute-start(bf16[4096,1024]{1,0:T(8,128)(2,1)} %constant_dynamic-update-slice_fusion.4.refs_2_), channel_id=1, source_target_pairs={{0,1},{1,0},{2,3},{3,2},{24,25},{25,24},{26,27},{27,26},{4,5},{5,4... | collective-permute-start | bytes 25165832 | tf_op jit(solution)/shard_map/ppermute | solution.py:251
  306.7 214.5 %collective-permute-start.25 = (bf16[4096,1024]{1,0:T(8,128)(2,1)}, bf16[4096,1024]{1,0:T(8,128)(2,1)}, u32[]{:S(2)}, u32[]{:S(2)}) collective-permute-start(bf16[4096,1024]{1,0:T(8,128)(2,1)} %constant_dynamic-update-slice_fusion.4.refs_2_), channel_id=1, source_target_pairs={{0,2},{1,3},{2,0},{3,1},{24,26},{25,27},{26,24},{27,25},{4,6},{5,7... | collective-permute-start | bytes 25165832 | tf_op jit(solution)/shard_map/ppermute | solution.py:251
  313.2 5.4 copy-start.2
  334.2 0.8 collective-permute-start.21
  335.0 198.8 %copy-start.1 = (bf16[128,8192]{1,0:T(8,128)(2,1)}, bf16[128,8192]{1,0:T(8,128)(2,1)S(1)}, u32[]{:S(2)}) copy-start(bf16[128,8192]{1,0:T(8,128)(2,1)S(1)} %collective-permute-done.21.x_ref) | copy-start | bytes 6291460
  335.0 2.7 collective-permute-start.22
  521.2 56.9 %collective-permute-start.28 = (bf16[4096,1024]{1,0:T(8,128)(2,1)}, bf16[4096,1024]{1,0:T(8,128)(2,1)}, u32[]{:S(2)}, u32[]{:S(2)}) collective-permute-start(bf16[4096,1024]{1,0:T(8,128)(2,1)} %constant_dynamic-update-slice_fusion.4.refs_2_), channel_id=1, source_target_pairs={{1,2},{2,1},{25,26},{26,25},{5,6},{6,5},{29,30},{30,29}} | collective-permute-start | bytes 25165832 | tf_op jit(solution)/shard_map/ppermute | solution.py:251
  525.1 95.6 %collective-permute-start.29 = (bf16[4096,1024]{1,0:T(8,128)(2,1)}, bf16[4096,1024]{1,0:T(8,128)(2,1)}, u32[]{:S(2)}, u32[]{:S(2)}) collective-permute-start(bf16[4096,1024]{1,0:T(8,128)(2,1)} %collective-permute-done.25.refs_4_), channel_id=1, source_target_pairs={{2,3},{1,0},{26,27},{25,24},{6,7},{5,4},{30,31},{29,28}} | collective-permute-start | bytes 25165832 | tf_op jit(solution)/shard_map/ppermute | solution.py:251
  544.5 0.8 collective-permute-start.26
  545.3 12.1 %copy-start.3 = (bf16[128,8192]{1,0:T(8,128)(2,1)}, bf16[128,8192]{1,0:T(8,128)(2,1)S(1)}, u32[]{:S(2)}) copy-start(bf16[128,8192]{1,0:T(8,128)(2,1)S(1)} %collective-permute-done.26.x_ref) | copy-start | bytes 6291460
  545.3 5.3 collective-permute-start.27

commit v3 on v2

--- a/solution.py
+++ b/solution.py
@@ -353,8 +353,10 @@
     parts = both(result, 0)
     late_rest = others(late, kept)
     kept_back, rest[0] = together(own, rest[0])
-    own[RELAYED], own[INNER] = relayed(early, kept_back), across(early, kept_back)
+    own[INNER], own[RELAYED] = across(early, kept_back), relayed(early, kept_back)
+    swapped = own.pop(INNER)
     own, rest = together(own, rest)
+    own[INNER], rest = together(swapped, rest)
     rest[RELAYED], rest[INNER] = relayed(early, rest), across(early, rest)
     token = over("dp", dps, rest[2][:ROW_TILE, :HD], [(a, b, z, z) for a, b in ((1, 0), (2, 3)) for z in range(dps)])
     token, late_own, parts = together(token, kept[0], parts)
@@ -366,18 +368,23 @@
     normed = prepared(moved)
     terms = terms_of(0, own, everything) + terms_of(1, rest, (0, 1, 2))
     fresh, rollout = project(turn[1], normed, terms, None, placing(is_early))
+    swapped = rest.pop(INNER)
     fresh, rollout, rest = together(fresh, rollout, rest)
+    fresh, rest[INNER] = together(fresh, swapped)
     fresh, rollout = project(turn[1], normed, terms_of(1, rest, (INNER, RELAYED)), fresh, placing(is_early), rollout)
     result = attended(1, moved[0], fresh, result)
 
     terms = terms_of(0, own, everything) + terms_of(1, rest, everything)
-    moved, last = together(both(hop(result, 2), 2), last)
-    last[RELAYED], last[INNER] = relayed(late, last), across(late, last)
+    moved = both(hop(result, 2), 2)
     result = attended(2, moved[0], project(turn[2], prepared(moved), terms), result)
+    result, last = together(result, last)
+    last[INNER], last[RELAYED] = across(late, last), relayed(late, last)
     moved = both(hop(result, 3), 3)
     normed = prepared(moved)
     fresh, rollout = project(turn[3], normed, terms_of(2, last, (0, 1, 2), shift), None, placing(1 - is_early), rollout)
+    swapped = last.pop(INNER)
     fresh, rollout, last = together(fresh, rollout, last)
+    fresh, last[INNER] = together(fresh, swapped)
     fresh, rollout = project(turn[3], normed, terms_of(2, last, (INNER, RELAYED)), fresh, placing(1 - is_early), rollout)
     result = attended(3, moved[0], fresh, result)
     return (rollout[None], result[None, None])

time: 637 us -> 643 us (level)
  waiting for transfers between devices: 406 us -> 398 us
  starting transfers between devices: 78.4 us -> 85.2 us
    ppermute x30, waiting for transfers between devices: 406 us -> 398 us  [over(): return lax.ppermute(value, ('section', axis), pairs)]
    ppermute x30, starting transfers between devices: 78.4 us -> 85.2 us  [over(): return lax.ppermute(value, ('section', axis), pairs)]
  transfers between devices with their start and end apart: 30 -> 30, of which waited for: 11 -> 11; matrix products, arithmetic and copies ran while one was open for 7% -> 8% of each run, Pallas kernels for 12% -> 12%
where the time goes in v3:
time: 643 us; the launch traced here: 637 us
  waiting for transfers between devices  398 us (62%)
  Pallas kernels  99.7 us (16%)
  starting transfers between devices  85.2 us (13%)
  other arithmetic  28.1 us (4%)
  local copies, waits for them, and re-layouts  23.6 us (4%)
    ppermute x30, waiting for transfers between devices, over(): return lax.ppermute(value, ('section', axis), pairs)  398 us
    ppermute x30, starting transfers between devices, over(): return lax.ppermute(value, ('section', axis), pairs)  85.2 us
    pallas_call x7, Pallas kernels, project(): pl.pallas_call(functools.partial(project_kernel, layout, len(lhs), bool(a...  67.6 us
    pallas_call x4, Pallas kernels, attend(): pl.pallas_call(functools.partial(attend_kernel, share), out_shape=jax.Sha...  21.6 us
    convert_element_type x4, other arithmetic, normed_of(): (part.astype(jnp.float32) * inverse[:, None] * gain.astype(jnp.float32))....  15 us
  transfers between devices with their start and end apart: 30, of which 11 were waited for; matrix products, arithmetic and copies ran while one was open for 8% of the time, Pallas kernels for 12%

profile of v3, /device:TPU:0, one launch (start us, length us, event | category | flops | bytes accessed | tf_op | source)
XLA Modules:
  0.0 637.1 jit_solution(4001691046904885836)
XLA Ops:
  0.7 5.3 shard_map.77.refs_1_.refs_2_
  6.5 4.9 collective-permute-start.2
  11.5 1.4 collective-permute-done.2
  14.8 4.0 collective-permute-start.3
  18.7 4.5 collective-permute-start.4
  23.2 1.9 collective-permute-start.5
  25.2 2.7 collective-permute-start
  27.8 2.6 collective-permute-start.1
  31.1 5.2 shard_map.79.refs_1_
  36.3 15.8 %collective-permute-done.3 = bf16[128,2048]{1,0:T(8,128)(2,1)S(1)} collective-permute-done((bf16[128,2048]{1,0:T(8,128)(2,1)}, bf16[128,2048]{1,0:T(8,128)(2,1)S(1)}, u32[]{:S(2)}, u32[]{:S(2)}) %collective-permute-start.3) | collective-permute-done | bytes 524320 | tf_op jit(solution)/shard_map/ppermute | solution.py:251
  52.0 4.8 collective-permute-done.5
  57.6 1.5 collective-permute-start.6
  60.0 1.9 constant_dynamic-update-slice_fusion.1
  61.9 1.9 constant_dynamic-update-slice_fusion.refs_0_
  63.7 7.1 %shard_map.78 = f32[512,1024]{1,0:T(8,128)} custom-call(s32[7]{0:T(128)} %stack.73.where_ref, bf16[512,2048]{1,0:T(8,128)(2,1)} %constant_dynamic-update-slice_fusion.refs_0_, bf16[2048,1024]{1,0:T(8,128)(2,1)} %shard_map.77.refs_1_.refs_2_), custom_call_target="tpu_custom_call" | custom-call | tf_op jit(solution)/shard_map/pallas_call | solution.py:146
  70.9 7.1 %shard_map.80 = f32[512,1024]{1,0:T(8,128)} custom-call(s32[7]{0:T(128)} %stack.73.where_ref, bf16[512,2048]{1,0:T(8,128)(2,1)} %constant_dynamic-update-slice_fusion.refs_0_, bf16[2048,1024]{1,0:T(8,128)(2,1)} %shard_map.79.refs_1_), custom_call_target="tpu_custom_call" | custom-call | tf_op jit(solution)/shard_map/pallas_call | solution.py:146
  78.0 2.7 collective-permute-start.10
  80.8 1.7 convert_element_type.96
  82.5 2.4 collective-permute-start.7
  84.9 19.5 %collective-permute-done.7 = bf16[512,1024]{1,0:T(8,128)(2,1)S(1)} collective-permute-done((bf16[512,1024]{1,0:T(8,128)(2,1)S(1)}, bf16[512,1024]{1,0:T(8,128)(2,1)S(1)}, u32[]{:S(2)}, u32[]{:S(2)}) %collective-permute-start.7) | collective-permute-done | bytes 1048608 | tf_op jit(solution)/shard_map/ppermute | solution.py:251
  105.1 2.4 collective-permute-start.8
  107.6 19.8 %collective-permute-done.8 = bf16[2,128,1024]{2,1,0:T(8,128)(2,1)S(1)} collective-permute-done((bf16[2,128,1024]{2,1,0:T(8,128)(2,1)S(1)}, bf16[2,128,1024]{2,1,0:T(8,128)(2,1)S(1)}, u32[]{:S(2)}, u32[]{:S(2)}) %collective-permute-start.8) | collective-permute-done | bytes 524320 | tf_op jit(solution)/shard_map/ppermute | solution.py:251
  128.3 1.9 collective-permute-start.9
  130.2 1.3 copy.18.held_ref
  133.6 7.3 %collective-permute-done.9 = bf16[1,128,1024]{2,1,0:T(8,128)(2,1)S(1)} collective-permute-done((bf16[1,128,1024]{2,1,0:T(8,128)(2,1)}, bf16[1,128,1024]{2,1,0:T(8,128)(2,1)S(1)}, u32[]{:S(2)}, u32[]{:S(2)}) %collective-permute-start.9) | collective-permute-done | bytes 262176 | tf_op jit(solution)/shard_map/ppermute | solution.py:251
  141.7 12.8 %shard_map.81.held_ref = bf16[128,8192]{1,0:T(8,128)(2,1)} custom-call(s32[1]{0:T(128)} %bitcast.14.active_ref, f32[8,16,256]{2,1,0:T(8,128)} %and_select_fusion.bias_ref, bf16[128,8192]{1,0:T(8,128)(2,1)} %bitcast.60, bf16[128,8192]{1,0:T(8,128)(2,1)} %bitcast.54, bf16[128,16,2048]{2,1,0:T(8,128)(2,1)} %bitcast.49, ...), custom_call_target="tpu_custom_call", output_to_operand_aliasing={{}: (6, {})} | custom-call | tf_op jit(solution)/shard_map/pallas_call | solution.py:211
  154.6 2.7 collective-permute-start.12
  157.3 2.7 collective-permute-start.13
  160.0 2.6 collective-permute-start.14
  162.6 2.6 collective-permute-start.11
  165.2 3.4 collective-permute-start.23
  168.6 2.4 collective-permute-start.16
  171.8 1.3 collective-permute-start.15
  173.0 65.3 %collective-permute-done.16 = bf16[128,8192]{1,0:T(8,128)(2,1)} collective-permute-done((bf16[128,8192]{1,0:T(8,128)(2,1)}, bf16[128,8192]{1,0:T(8,128)(2,1)}, u32[]{:S(2)}, u32[]{:S(2)}) %collective-permute-start.16) | collective-permute-done | bytes 2097184 | tf_op jit(solution)/shard_map/ppermute | solution.py:251
  238.4 43.1 %collective-permute-done.15 = bf16[16,128]{1,0:T(8,128)(2,1)S(1)} collective-permute-done((bf16[16,128]{1,0:T(8,128)(2,1)S(1)}, bf16[16,128]{1,0:T(8,128)(2,1)S(1)}, u32[]{:S(2)}, u32[]{:S(2)}) %collective-permute-start.15) | collective-permute-done | bytes 4128 | tf_op jit(solution)/shard_map/ppermute | solution.py:251
  281.4 3.4 collective-permute-start.18
  284.9 1.4 collective-permute-start.17
  286.3 2.6 collective-permute-start.19
  288.9 2.6 collective-permute-start.20
  292.8 4.7 constant_dynamic-update-slice_fusion.5
  297.5 4.6 constant_dynamic-update-slice_fusion.4.refs_2_
  302.1 11.5 %collective-permute-start.24 = (bf16[4096,1024]{1,0:T(8,128)(2,1)}, bf16[4096,1024]{1,0:T(8,128)(2,1)}, u32[]{:S(2)}, u32[]{:S(2)}) collective-permute-start(bf16[4096,1024]{1,0:T(8,128)(2,1)} %constant_dynamic-update-slice_fusion.4.refs_2_), channel_id=1, source_target_pairs={{0,1},{1,0},{2,3},{3,2},{24,25},{25,24},{26,27},{27,26},{4,5},{5,4... | collective-permute-start | bytes 25165832 | tf_op jit(solution)/shard_map/ppermute | solution.py:251
  313.6 3.7 collective-permute-start.25
  317.4 2.1 fusion.3
  320.0 4.9 fusion.8
  324.9 7.3 %shard_map.82 = (f32[128,1024]{1,0:T(8,128)}, bf16[16384,1024]{1,0:T(8,128)(2,1)}) custom-call(s32[28]{0:T(128)} %stack.88.where_ref, bf16[128,8192]{1,0:T(8,128)(2,1)} %get-tuple-element.152.refs_0_, bf16[128,8192]{1,0:T(8,128)(2,1)} %get-tuple-element.153.refs_1_.refs_0_, bf16[2048,1024]{1,0:T(8,128)(2,1)} %shard_map.77.refs_1_.refs_2_, ...), custom_call_target="tpu_custom_call" | custom-call | tf_op jit(solution)/shard_map/pallas_call | solution.py:146
  332.2 5.4 shard_map.83
  337.6 2.9 shard_map.84.held_ref
  341.4 2.0 collective-permute-start.22
  344.5 2.1 fusion.12
  346.6 4.8 fusion.14
  351.4 7.9 %shard_map.85.f_ref = f32[128,1024]{1,0:T(8,128)} custom-call(s32[34]{0:T(128)} %stack.89.where_ref, bf16[128,8192]{1,0:T(8,128)(2,1)} %get-tuple-element.151.refs_0_, bf16[128,8192]{1,0:T(8,128)(2,1)} %get-tuple-element.150.refs_1_, bf16[2048,1024]{1,0:T(8,128)(2,1)} %shard_map.77.refs_1_.refs_2_, bf16[2048,1024]{1,0:T(8,128)(2,1)} %collective-permute-done.refs_3_, ...), custom_call_target="tpu_custom_call" | custom-call | tf_op jit(solution)/shard_map/pallas_call | solution.py:146
  359.3 2.9 shard_map.86.held_ref
  362.2 130.6 %collective-permute-done.24.refs_3_ = bf16[4096,1024]{1,0:T(8,128)(2,1)} collective-permute-done((bf16[4096,1024]{1,0:T(8,128)(2,1)}, bf16[4096,1024]{1,0:T(8,128)(2,1)}, u32[]{:S(2)}, u32[]{:S(2)}) %collective-permute-start.24) | collective-permute-done | bytes 8388640 | tf_op jit(solution)/shard_map/ppermute | solution.py:251
  492.9 33.6 %collective-permute-done.25.refs_4_ = bf16[4096,1024]{1,0:T(8,128)(2,1)} collective-permute-done((bf16[4096,1024]{1,0:T(8,128)(2,1)}, bf16[4096,1024]{1,0:T(8,128)(2,1)}, u32[]{:S(2)}, u32[]{:S(2)}) %collective-permute-start.25) | collective-permute-done | bytes 8388640 | tf_op jit(solution)/shard_map/ppermute | solution.py:251
  526.5 1.3 collective-permute-start.28
  527.8 3.9 collective-permute-start.29
  532.5 2.0 collective-permute-start.27
  537.8 2.1 fusion.18
  539.9 4.7 fusion.20
  544.5 20.7 %shard_map.87 = (f32[128,1024]{1,0:T(8,128)}, bf16[16384,1024]{1,0:T(8,128)(2,1)}) custom-call(s32[19]{0:T(128)} %stack.93.where_ref, bf16[128,8192]{1,0:T(8,128)(2,1)} %get-tuple-element.149.refs_0_, bf16[128,8192]{1,0:T(8,128)(2,1)} %get-tuple-element.148.refs_1_, ...), custom_call_target="tpu_custom_call", output_to_operand_aliasing={{1}: (6, {})} | custom-call | tf_op jit(solution)/shard_map/pallas_call | solution.py:146
  565.3 56.9 %collective-permute-done.28.refs_3_ = bf16[4096,1024]{1,0:T(8,128)(2,1)} collective-permute-done((bf16[4096,1024]{1,0:T(8,128)(2,1)}, bf16[4096,1024]{1,0:T(8,128)(2,1)}, u32[]{:S(2)}, u32[]{:S(2)}) %collective-permute-start.28) | collective-permute-done | bytes 8388640 | tf_op jit(solution)/shard_map/ppermute | solution.py:251
  622.1 12.0 %shard_map.88 = (f32[128,1024]{1,0:T(8,128)}, bf16[16384,1024]{1,0:T(8,128)(2,1)}) custom-call(s32[14]{0:T(128)} %stack.72.where_ref, bf16[128,8192]{1,0:T(8,128)(2,1)} %get-tuple-element.149.refs_0_, bf16[128,8192]{1,0:T(8,128)(2,1)} %get-tuple-element.148.refs_1_, ...), custom_call_target="tpu_custom_call", output_to_operand_aliasing={{1}: (6, {})} | custom-call | tf_op jit(solution)/shard_map/pallas_call | solution.py:146
  634.1 2.9 shard_map.89
  (74 shorter events, 16.6 us)
Async XLA Ops:
  0.6 5.4 copy-start
  0.7 10.7 %copy-start.5 = (bf16[1,8192]{1,0:T(2,128)(2,1)S(1)}, bf16[1,8192]{1,0:T(2,128)(2,1)}, u32[]{:S(2)}) copy-start(bf16[1,8192]{1,0:T(2,128)(2,1)} %param.7) | copy-start | bytes 49156
  6.5 6.4 %collective-permute-start.2 = (f32[128]{0:T(128)S(1)}, f32[128]{0:T(128)S(1)}, u32[]{:S(2)}, u32[]{:S(2)}) collective-permute-start(f32[128]{0:T(128)S(1)} %fusion), channel_id=1, source_target_pairs={{0,4},{4,0},{1,5},{5,1},{2,6},{6,2},{3,7},{7,3}} | collective-permute-start | bytes 1544 | tf_op jit(solution)/shard_map/ppermute | solution.py:251
  14.8 37.3 %collective-permute-start.3 = (bf16[128,2048]{1,0:T(8,128)(2,1)}, bf16[128,2048]{1,0:T(8,128)(2,1)S(1)}, u32[]{:S(2)}, u32[]{:S(2)}) collective-permute-start(bf16[128,2048]{1,0:T(8,128)(2,1)} %get-tuple-element.74), channel_id=1, source_target_pairs={{0,1},{1,0},{2,3},{3,2},{4,5},{5,4},{6,7},{7,6}} | collective-permute-start | bytes 1572872 | tf_op jit(solution)/shard_map/ppermute | solution.py:251
  18.7 33.3 %collective-permute-start.4 = (bf16[128,2048]{1,0:T(8,128)(2,1)}, bf16[128,2048]{1,0:T(8,128)(2,1)}, u32[]{:S(2)}, u32[]{:S(2)}) collective-permute-start(bf16[128,2048]{1,0:T(8,128)(2,1)} %get-tuple-element.75), channel_id=1, source_target_pairs={{0,2},{1,3},{2,0},{3,1},{4,6},{5,7},{6,4},{7,5}} | collective-permute-start | bytes 1572872 | tf_op jit(solution)/shard_map/ppermute | solution.py:251
  23.2 33.6 %collective-permute-start.5 = (bf16[128,2048]{1,0:T(8,128)(2,1)}, bf16[128,2048]{1,0:T(8,128)(2,1)}, u32[]{:S(2)}, u32[]{:S(2)}) collective-permute-start(bf16[128,2048]{1,0:T(8,128)(2,1)} %get-tuple-element.76), channel_id=1, source_target_pairs={{0,3},{1,2},{2,1},{3,0},{4,7},{5,6},{6,5},{7,4}} | collective-permute-start | bytes 1572872 | tf_op jit(solution)/shard_map/ppermute | solution.py:251
  25.2 129.4 %collective-permute-start = (bf16[2048,1024]{1,0:T(8,128)(2,1)}, bf16[2048,1024]{1,0:T(8,128)(2,1)}, u32[]{:S(2)}, u32[]{:S(2)}) collective-permute-start(bf16[2048,1024]{1,0:T(8,128)(2,1)} %shard_map.77.refs_1_.refs_2_), channel_id=1, source_target_pairs={{8,9},{9,8},{10,11},{11,10},{16,17},{17,16},{18,19},{19,18},{12,13... | collective-permute-start | bytes 12582920 | tf_op jit(solution)/shard_map/ppermute | solution.py:251
  27.8 126.7 %collective-permute-start.1 = (bf16[2048,1024]{1,0:T(8,128)(2,1)}, bf16[2048,1024]{1,0:T(8,128)(2,1)}, u32[]{:S(2)}, u32[]{:S(2)}) collective-permute-start(bf16[2048,1024]{1,0:T(8,128)(2,1)} %shard_map.77.refs_1_.refs_2_), channel_id=1, source_target_pairs={{8,10},{9,11},{10,8},{11,9},{16,18},{17,19},{18,16},{19,17},{12,14... | collective-permute-start | bytes 12582920 | tf_op jit(solution)/shard_map/ppermute | solution.py:251
  57.6 20.4 %collective-permute-start.6 = (bf16[1,8192]{1,0:T(2,128)(2,1)S(1)}, bf16[1,8192]{1,0:T(2,128)(2,1)S(1)}, u32[]{:S(2)}, u32[]{:S(2)}) collective-permute-start(bf16[1,8192]{1,0:T(2,128)(2,1)S(1)} %copy-done.5), channel_id=1, source_target_pairs={{0,4},{4,0},{8,12},{12,8},{16,20},{20,16},{24,28},{28,24},{1,5},{5... | collective-permute-start | bytes 49160 | tf_op jit(solution)/shard_map/ppermute | solution.py:251
  78.0 26.4 %copy-start.4 = (f32[512,1024]{1,0:T(8,128)S(1)}, f32[512,1024]{1,0:T(8,128)}, u32[]{:S(2)}) copy-start(f32[512,1024]{1,0:T(8,128)} %shard_map.78) | copy-start | bytes 6291460
  78.0 76.5 %collective-permute-start.10 = (bf16[2048,1024]{1,0:T(8,128)(2,1)}, bf16[2048,1024]{1,0:T(8,128)(2,1)}, u32[]{:S(2)}, u32[]{:S(2)}) collective-permute-start(bf16[2048,1024]{1,0:T(8,128)(2,1)} %shard_map.79.refs_1_), channel_id=1, source_target_pairs={{8,12},{12,8},{16,20},{20,16},{9,13},{13,9},{17,21},{21,17},{10,14... | collective-permute-start | bytes 12582920 | tf_op jit(solution)/shard_map/ppermute | solution.py:251
  82.5 21.9 %collective-permute-start.7 = (bf16[512,1024]{1,0:T(8,128)(2,1)S(1)}, bf16[512,1024]{1,0:T(8,128)(2,1)S(1)}, u32[]{:S(2)}, u32[]{:S(2)}) collective-permute-start(bf16[512,1024]{1,0:T(8,128)(2,1)S(1)} %convert_element_type.96), channel_id=1, source_target_pairs={{0,4},{4,0},{1,5},{5,1},{2,6},{6,2},{3,7},{7,3}} | collective-permute-start | bytes 3145736 | tf_op jit(solution)/shard_map/ppermute | solution.py:251
  105.1 22.3 %collective-permute-start.8 = (bf16[2,128,1024]{2,1,0:T(8,128)(2,1)S(1)}, bf16[2,128,1024]{2,1,0:T(8,128)(2,1)S(1)}, u32[]{:S(2)}, u32[]{:S(2)}) collective-permute-start(bf16[2,128,1024]{2,1,0:T(8,128)(2,1)S(1)} %pad_maximum_fusion), channel_id=1, source_target_pairs={{0,1},{1,0},{2,3},{3,2},{4,5},{5,4},{6,7},{7,6}} | collective-permute-start | bytes 1572872 | tf_op jit(solution)/shard_map/ppermute | solution.py:251
  107.5 24.6 %copy-start.6 = (s32[1,128]{1,0:T(1,128)S(1)}, s32[1,128]{1,0:T(1,128)}, u32[]{:S(2)}) copy-start(s32[1,128]{1,0:T(1,128)} %param.11) | copy-start | bytes 1540
  128.3 12.5 %collective-permute-start.9 = (bf16[1,128,1024]{2,1,0:T(8,128)(2,1)}, bf16[1,128,1024]{2,1,0:T(8,128)(2,1)S(1)}, u32[]{:S(2)}, u32[]{:S(2)}) collective-permute-start(bf16[1,128,1024]{2,1,0:T(8,128)(2,1)} %slice.65), channel_id=1, source_target_pairs={{0,2},{1,3},{2,0},{3,1},{4,6},{5,7},{6,4},{7,5}} | collective-permute-start | bytes 786440 | tf_op jit(solution)/shard_map/ppermute | solution.py:251
  154.6 14.0 %collective-permute-start.12 = (bf16[2048,1024]{1,0:T(8,128)(2,1)}, bf16[2048,1024]{1,0:T(8,128)(2,1)}, u32[]{:S(2)}, u32[]{:S(2)}) collective-permute-start(bf16[2048,1024]{1,0:T(8,128)(2,1)} %collective-permute-done.1.refs_4_), channel_id=1, source_target_pairs={{10,11},{9,8},{18,19},{17,16},{14,15},{13,12},{22,23},{21,20}} | collective-permute-start | bytes 12582920 | tf_op jit(solution)/shard_map/ppermute | solution.py:251
  157.3 13.7 %collective-permute-start.13 = (bf16[2048,1024]{1,0:T(8,128)(2,1)}, bf16[2048,1024]{1,0:T(8,128)(2,1)}, u32[]{:S(2)}, u32[]{:S(2)}) collective-permute-start(bf16[2048,1024]{1,0:T(8,128)(2,1)} %collective-permute-done.10.refs_7_), channel_id=1, source_target_pairs={{8,9},{9,8},{10,11},{11,10},{16,17},{17,16},{18,19},{19,18},{12,13... | collective-permute-start | bytes 12582920 | tf_op jit(solution)/shard_map/ppermute | solution.py:251
  160.0 11.1 %collective-permute-start.14 = (bf16[2048,1024]{1,0:T(8,128)(2,1)}, bf16[2048,1024]{1,0:T(8,128)(2,1)}, u32[]{:S(2)}, u32[]{:S(2)}) collective-permute-start(bf16[2048,1024]{1,0:T(8,128)(2,1)} %collective-permute-done.10.refs_7_), channel_id=1, source_target_pairs={{8,10},{9,11},{10,8},{11,9},{16,18},{17,19},{18,16},{19,17},{12,14... | collective-permute-start | bytes 12582920 | tf_op jit(solution)/shard_map/ppermute | solution.py:251
  162.6 8.5 %collective-permute-start.11 = (bf16[2048,1024]{1,0:T(8,128)(2,1)}, bf16[2048,1024]{1,0:T(8,128)(2,1)}, u32[]{:S(2)}, u32[]{:S(2)}) collective-permute-start(bf16[2048,1024]{1,0:T(8,128)(2,1)} %shard_map.77.refs_1_.refs_2_), channel_id=1, source_target_pairs={{9,10},{10,9},{17,18},{18,17},{13,14},{14,13},{21,22},{22,21}} | collective-permute-start | bytes 12582920 | tf_op jit(solution)/shard_map/ppermute | solution.py:251
  165.2 132.3 %collective-permute-start.23 = (bf16[2048,1024]{1,0:T(8,128)(2,1)}, bf16[2048,1024]{1,0:T(8,128)(2,1)}, u32[]{:S(2)}, u32[]{:S(2)}) collective-permute-start(bf16[2048,1024]{1,0:T(8,128)(2,1)} %shard_map.79.refs_1_), channel_id=1, source_target_pairs={{0,4},{4,0},{24,28},{28,24},{1,5},{5,1},{25,29},{29,25},{2,6},{6,2... | collective-permute-start | bytes 12582920 | tf_op jit(solution)/shard_map/ppermute | solution.py:251
  168.6 69.7 %collective-permute-start.16 = (bf16[128,8192]{1,0:T(8,128)(2,1)}, bf16[128,8192]{1,0:T(8,128)(2,1)}, u32[]{:S(2)}, u32[]{:S(2)}) collective-permute-start(bf16[128,8192]{1,0:T(8,128)(2,1)} %shard_map.81.held_ref), channel_id=1, source_target_pairs={{0,4},{4,0},{1,5},{5,1},{2,6},{6,2},{3,7},{7,3}} | collective-permute-start | bytes 6291464 | tf_op jit(solution)/shard_map/ppermute | solution.py:251
  171.8 109.7 %collective-permute-start.15 = (bf16[16,128]{1,0:T(8,128)(2,1)S(1)}, bf16[16,128]{1,0:T(8,128)(2,1)S(1)}, u32[]{:S(2)}, u32[]{:S(2)}) collective-permute-start(bf16[16,128]{1,0:T(8,128)(2,1)S(1)} %slice.49), channel_id=1, source_target_pairs={{8,0},{9,1},{10,2},{11,3},{16,24},{17,25},{18,26},{19,27},{12,4},{... | collective-permute-start | bytes 12296 | tf_op jit(solution)/shard_map/ppermute | solution.py:251
  281.4 32.2 %collective-permute-start.18 = (bf16[128,8192]{1,0:T(8,128)(2,1)}, bf16[128,8192]{1,0:T(8,128)(2,1)}, u32[]{:S(2)}, u32[]{:S(2)}) collective-permute-start(bf16[128,8192]{1,0:T(8,128)(2,1)} %collective-permute-done.16), channel_id=1, source_target_pairs={{0,8},{4,12},{1,9},{5,13},{2,10},{6,14},{3,11},{7,15}} | collective-permute-start | bytes 6291464 | tf_op jit(solution)/shard_map/ppermute | solution.py:251
  284.9 34.6 %collective-permute-start.17 = (bf16[128,8192]{1,0:T(8,128)(2,1)}, bf16[128,8192]{1,0:T(8,128)(2,1)S(1)}, u32[]{:S(2)}, u32[]{:S(2)}) collective-permute-start(bf16[128,8192]{1,0:T(8,128)(2,1)} %shard_map.81.held_ref), channel_id=1, source_target_pairs={{0,8},{4,12},{1,9},{5,13},{2,10},{6,14},{3,11},{7,15}} | collective-permute-start | bytes 6291464 | tf_op jit(solution)/shard_map/ppermute | solution.py:251
  286.3 45.9 %collective-permute-start.19 = (bf16[2048,1024]{1,0:T(8,128)(2,1)}, bf16[2048,1024]{1,0:T(8,128)(2,1)}, u32[]{:S(2)}, u32[]{:S(2)}) collective-permute-start(bf16[2048,1024]{1,0:T(8,128)(2,1)} %collective-permute-done.14.refs_9_), channel_id=1, source_target_pairs={{10,11},{9,8},{18,19},{17,16},{14,15},{13,12},{22,23},{21,20}} | collective-permute-start | bytes 12582920 | tf_op jit(solution)/shard_map/ppermute | solution.py:251
  288.9 43.3 %collective-permute-start.20 = (bf16[2048,1024]{1,0:T(8,128)(2,1)}, bf16[2048,1024]{1,0:T(8,128)(2,1)}, u32[]{:S(2)}, u32[]{:S(2)}) collective-permute-start(bf16[2048,1024]{1,0:T(8,128)(2,1)} %collective-permute-done.10.refs_7_), channel_id=1, source_target_pairs={{9,10},{10,9},{17,18},{18,17},{13,14},{14,13},{21,22},{22,21}} | collective-permute-start | bytes 12582920 | tf_op jit(solution)/shard_map/ppermute | solution.py:251
  302.1 190.7 %collective-permute-start.24 = (bf16[4096,1024]{1,0:T(8,128)(2,1)}, bf16[4096,1024]{1,0:T(8,128)(2,1)}, u32[]{:S(2)}, u32[]{:S(2)}) collective-permute-start(bf16[4096,1024]{1,0:T(8,128)(2,1)} %constant_dynamic-update-slice_fusion.4.refs_2_), channel_id=1, source_target_pairs={{0,1},{1,0},{2,3},{3,2},{24,25},{25,24},{26,27},{27,26},{4,5},{5,4... | collective-permute-start | bytes 25165832 | tf_op jit(solution)/shard_map/ppermute | solution.py:251
  313.6 212.8 %collective-permute-start.25 = (bf16[4096,1024]{1,0:T(8,128)(2,1)}, bf16[4096,1024]{1,0:T(8,128)(2,1)}, u32[]{:S(2)}, u32[]{:S(2)}) collective-permute-start(bf16[4096,1024]{1,0:T(8,128)(2,1)} %constant_dynamic-update-slice_fusion.4.refs_2_), channel_id=1, source_target_pairs={{0,2},{1,3},{2,0},{3,1},{24,26},{25,27},{26,24},{27,25},{4,6},{5,7... | collective-permute-start | bytes 25165832 | tf_op jit(solution)/shard_map/ppermute | solution.py:251
  319.5 5.5 copy-start.1
  340.6 0.8 collective-permute-start.21
  341.4 10.0 %copy-start.3 = (bf16[128,8192]{1,0:T(8,128)(2,1)}, bf16[128,8192]{1,0:T(8,128)(2,1)S(1)}, u32[]{:S(2)}) copy-start(bf16[128,8192]{1,0:T(8,128)(2,1)S(1)} %collective-permute-done.21.x_ref) | copy-start | bytes 6291460
  341.4 3.2 collective-permute-start.22
  526.5 95.6 %collective-permute-start.28 = (bf16[4096,1024]{1,0:T(8,128)(2,1)}, bf16[4096,1024]{1,0:T(8,128)(2,1)}, u32[]{:S(2)}, u32[]{:S(2)}) collective-permute-start(bf16[4096,1024]{1,0:T(8,128)(2,1)} %collective-permute-done.25.refs_4_), channel_id=1, source_target_pairs={{2,3},{1,0},{26,27},{25,24},{6,7},{5,4},{30,31},{29,28}} | collective-permute-start | bytes 25165832 | tf_op jit(solution)/shard_map/ppermute | solution.py:251
  527.8 94.4 %collective-permute-start.29 = (bf16[4096,1024]{1,0:T(8,128)(2,1)}, bf16[4096,1024]{1,0:T(8,128)(2,1)}, u32[]{:S(2)}, u32[]{:S(2)}) collective-permute-start(bf16[4096,1024]{1,0:T(8,128)(2,1)} %constant_dynamic-update-slice_fusion.4.refs_2_), channel_id=1, source_target_pairs={{1,2},{2,1},{25,26},{26,25},{5,6},{6,5},{29,30},{30,29}} | collective-permute-start | bytes 25165832 | tf_op jit(solution)/shard_map/ppermute | solution.py:251
  531.7 0.8 collective-permute-start.26
  532.5 12.0 %copy-start.2 = (bf16[128,8192]{1,0:T(8,128)(2,1)}, bf16[128,8192]{1,0:T(8,128)(2,1)S(1)}, u32[]{:S(2)}) copy-start(bf16[128,8192]{1,0:T(8,128)(2,1)S(1)} %collective-permute-done.26.x_ref) | copy-start | bytes 6291460
  532.5 5.3 collective-permute-start.27

commit v4 on v2

--- a/solution.py
+++ b/solution.py
@@ -19,7 +19,6 @@
 
 epsilon = 1e-05
 clip_ratio = 2.0
-INNER, RELAYED = 4, 5
 FIXED = 4
 VMEM = 60 << 20
 SHORT = pl.CostEstimate(flops=0, bytes_accessed=0, transcendentals=0)
@@ -62,95 +61,76 @@
     if has_held:
         rest.pop(0)
     o_ref = rest.pop(0)
-    segments = [(n, *segment) for n, (_, of_block) in enumerate(layout) for segment in of_block]
-
-    def copy(i):
-        n, _, start, depth = segments[i]
+    segments = [(block, *segment) for block, of_block in zip(blocks, layout) for segment in of_block]
+
+    def copies():
         out, sems = rest
         width = min(out.shape[1], o_ref.shape[1])
-        rows = pl.ds(pl.multiple_of(where_ref[FIXED + len(layout) + 2 * i + 1], GROUP), depth)
-        columns = pl.ds(pl.multiple_of(pl.program_id(0) * width, HD), width)
-        source = blocks[n].at[pl.ds(start, depth)]
-        if width < blocks[n].shape[1]:
-            source = blocks[n].at[pl.ds(start, depth), pl.ds(pl.multiple_of(where_ref[2], HD), width)]
-        return pltpu.make_async_copy(source, out.at[rows, columns], sems.at[i])
-
-    def add(which):
-        total = o_ref[...]
-        for i in which:
-            n, j, start, depth = segments[i]
-            columns = pl.ds(pl.multiple_of(where_ref[FIXED + len(layout) + 2 * i], GROUP), depth)
-            rows = blocks[n][start : start + depth, :]
-            total += jnp.dot(lhs[j][:, columns], rows, preferred_element_type=jnp.float32)
+        for i, (block, _, start, depth) in enumerate(segments):
+            rows = pl.ds(pl.multiple_of(where_ref[FIXED + 2 * i + 1], GROUP), depth)
+            columns = pl.ds(pl.multiple_of(pl.program_id(0) * width, HD), width)
+            source = block.at[pl.ds(start, depth)]
+            if width < block.shape[1]:
+                source = block.at[pl.ds(start, depth), pl.ds(pl.multiple_of(where_ref[2], HD), width)]
+            yield pltpu.make_async_copy(source, out.at[rows, columns], sems.at[i])
+
+    if placed:
+
+        @pl.when(where_ref[1] == 1)
+        def _():
+            for copy in copies():
+                copy.start()
+
+    @pl.when(where_ref[0] == 1)
+    def _():
+        total = total_ref[...] if has_total else None
+        for i, (block, j, start, depth) in enumerate(segments):
+            columns = pl.ds(pl.multiple_of(where_ref[FIXED + 2 * i], GROUP), depth)
+            term = jnp.dot(
+                lhs[j][:, columns], block[start : start + depth, :], preferred_element_type=jnp.float32
+            )
+            total = term if total is None else total + term
         o_ref[...] = total
 
-    def start(which):
-        for i in which:
-            copy(i).start()
-
-    def wait(which):
-        for i in which:
-            copy(i).wait()
-
-    groups = [(None, [i for i, segment in enumerate(segments) if not layout[segment[0]][0]])]
-    for n, (gated, _) in enumerate(layout):
-        if gated:
-            groups.append((n, [i for i, segment in enumerate(segments) if segment[0] == n]))
-
-    for n, which in groups:
-        has = 1 if n is None else where_ref[FIXED + n]
-
-        if placed and which:
-            pl.when(where_ref[1] * has == 1)(functools.partial(start, which))
-
-    o_ref[...] = total_ref[...] if has_total else jnp.zeros(o_ref.shape, jnp.float32)
-    for n, which in groups:
-        if which:
-            has = 1 if n is None else where_ref[FIXED + n]
-            pl.when(where_ref[0] * has == 1)(functools.partial(add, which))
-
-    for n, which in groups:
-        has = 1 if n is None else where_ref[FIXED + n]
-
-        if placed and which:
-            pl.when(where_ref[1] * has == 1)(functools.partial(wait, which))
+    @pl.when(where_ref[0] == 0)
+    def _():
+        o_ref[...] = jnp.zeros(o_ref.shape, jnp.float32)
+
+    if placed:
+
+        @pl.when(where_ref[1] == 1)
+        def _():
+            for copy in copies():
+                copy.wait()
 
 
 def project(active, lhs, terms, total=None, placing=None, rollout=None):
-    used = sorted({segment[0] for _, _, segments in terms for segment in segments})
+    used = sorted({segment[0] for _, segments in terms for segment in segments})
     lhs = [lhs[j] for j in used]
     rows = lhs[0].shape[0]
     served = terms[0][0].shape[1]
     tile = min(served, 256)
     places, first_column, width = placing or (0, 0, 0)
     where = [active, places, first_column, active | places]
-    where += [1 if has is None else has for _, has, _ in terms]
-    for _, _, segments in terms:
+    for _, segments in terms:
         for _, offset, row, _, _ in segments:
             where += [offset, row]
-    layout = [
-        (has is not None, [(used.index(j), start, depth) for j, _, _, start, depth in segments])
-        for _, has, segments in terms
-    ]
-    count = sum(len(segments) for _, segments in layout)
+    layout = [[(used.index(j), start, depth) for j, _, _, start, depth in segments] for _, segments in terms]
+    count = sum(len(segments) for segments in layout)
     added = () if total is None else (total,)
     held = () if rollout is None else (rollout,)
     column = lambda i, where: (0, i)
-
-    def read(n):
-        return lambda i, where: (0, i * where[3] * where[FIXED + n])
-
+    read = lambda i, where: (0, i * where[3])
     anywhere = pl.BlockSpec(memory_space=pl.ANY)
     fresh_shape, fresh_spec = jax.ShapeDtypeStruct((rows, served), jnp.float32), pl.BlockSpec((rows, tile), column)
-    placed = int(placing is not None)
     return pl.pallas_call(
-        functools.partial(project_kernel, layout, len(lhs), bool(added), bool(held), placed),
+        functools.partial(project_kernel, layout, len(lhs), bool(added), bool(held), placing is not None),
         out_shape=[fresh_shape, jax.ShapeDtypeStruct((D, width), jnp.bfloat16)] if placing else fresh_shape,
         grid_spec=pltpu.PrefetchScalarGridSpec(
             num_scalar_prefetch=1,
             grid=(served // tile,),
             in_specs=[pl.BlockSpec(part.shape, lambda i, where: (0, 0)) for part in lhs]
-            + [pl.BlockSpec((term[0].shape[0], tile), read(n)) for n, term in enumerate(terms)]
+            + [pl.BlockSpec((block.shape[0], tile), read) for block, _ in terms]
             + [fresh_spec for _ in added]
             + [anywhere for _ in held],
             out_specs=[fresh_spec, anywhere] if placing else fresh_spec,
@@ -159,7 +139,7 @@
         input_output_aliases={1 + len(lhs) + len(terms) + len(added): 1} if held else {},
         compiler_params=pltpu.CompilerParams(vmem_limit_bytes=VMEM),
         cost_estimate=SHORT,
-    )(jnp.stack([jnp.asarray(v, jnp.int32) for v in where]), *lhs, *[term[0] for term in terms], *added, *held)
+    )(jnp.stack([jnp.asarray(v, jnp.int32) for v in where]), *lhs, *[block for block, _ in terms], *added, *held)
 
 
 def attend_kernel(share, active_ref, bias_ref, x_ref, q_ref, c_ref, f_ref, held_ref, o_ref):
@@ -244,7 +224,6 @@
     early, late = (1, 2), (0, 3)
     everyone = tuple(range(sections))
     is_early = ((section == 1) | (section == 2)).astype(jnp.int32)
-    inner = ((dp == 1) | (dp == 2)).astype(jnp.int32)
 
     def over(axis, count, value, routes):
         pairs = [(a * count + i, b * count + j) for a, b, i, j in routes]
@@ -290,24 +269,21 @@
 
     halves = [[(0, 0)], [(j, (j - 1) * depth) for j in range(1, tensors)], [(j, j * depth) for j in range(tensors)]]
 
-    def across(at, blocks):
-        return over("dp", dps, blocks[0], [(s, s, a, b) for s in at for a, b in ((1, 2), (2, 1))])
-
-    def relayed(at, blocks):
-        return over("dp", dps, blocks[2], [(s, s, a, b) for s in at for a, b in ((2, 3), (1, 0))])
+    def straight(at, block):
+        return {0: block, 2: over_dp(block, at, flipped(2)), 1: over_dp(block, at, flipped(1))}
+
+    def handed_on(at, blocks):
+        return over_dp(blocks[2], at, flipped(1))
 
     def terms_of(half, blocks, which, shift=0):
         terms = []
-        for name in which:
-            b, has = {INNER: (3, inner), RELAYED: (3, 1 - inner)}.get(name, (name, None))
+        for b in which:
             source = dp ^ b
-            terms.append((blocks[name], has, [
+            terms.append((blocks[b], [
                 (j, source * depth + shift, ((tensor ^ j) * dps + source) * depth, start, depth)
                 for j, start in halves[half]
             ]))
         return terms
-
-    everything = (0, 1, 2, INNER, RELAYED)
 
     def placing(active):
         return (active, tensor * own_width % served, own_width)
@@ -329,12 +305,12 @@
         received = [over_tensor(kept[j], at, j) for j in range(1, tensors)]
         return received[0] if len(received) == 1 else jnp.concatenate(received, axis=0)
 
-    own = {0: kept[0], 2: over_dp(kept[0], early, flipped(2)), 1: over_dp(kept[0], early, flipped(1))}
+    own = straight(early, kept[0])
 
     lhs = [jnp.concatenate(first, axis=0)]
-    partial = [project(turn[0], lhs, [(kept[j], None, [(0, 0, 0, 0, depth)])]) for j in range(tensors)]
+    partial = [project(turn[0], lhs, [(kept[j], [(0, 0, 0, 0, depth)])]) for j in range(tensors)]
     partial, kept, gains = together(partial, kept, gains)
-    rest = {0: others(early, kept)}
+    rest = others(early, kept)
     total = partial[0]
     for j in range(1, tensors):
         total = total + over_tensor(partial[j].astype(jnp.bfloat16), (0,), j).astype(jnp.float32)
@@ -348,37 +324,37 @@
     fresh = total[0]
     result = attended(0, hidden, fresh, hidden)
 
-    rest[2], rest[1] = over_dp(rest[0], early, flipped(2)), over_dp(rest[0], early, flipped(1))
+    rest = straight(early, rest)
     own, result, kept = together(own, result, kept)
     parts = both(result, 0)
     late_rest = others(late, kept)
-    kept_back, rest[0] = together(own, rest[0])
-    own[RELAYED], own[INNER] = relayed(early, kept_back), across(early, kept_back)
+    own[3] = handed_on(early, own)
     own, rest = together(own, rest)
-    rest[RELAYED], rest[INNER] = relayed(early, rest), across(early, rest)
+    rest[3] = handed_on(early, rest)
     token = over("dp", dps, rest[2][:ROW_TILE, :HD], [(a, b, z, z) for a, b in ((1, 0), (2, 3)) for z in range(dps)])
     token, late_own, parts = together(token, kept[0], parts)
     whole = jnp.concatenate([late_own, late_rest], axis=0)
     shift = jnp.isnan(token[0, 0]).astype(jnp.int32)
-    last = {0: whole, 2: over_dp(whole, late, flipped(2)), 1: over_dp(whole, late, flipped(1))}
+    last = straight(late, whole)
 
     moved = [hop(part, 1) for part in parts]
     normed = prepared(moved)
-    terms = terms_of(0, own, everything) + terms_of(1, rest, (0, 1, 2))
+    terms = terms_of(0, own, range(dps)) + terms_of(1, rest, (0, 1, 2))
     fresh, rollout = project(turn[1], normed, terms, None, placing(is_early))
     fresh, rollout, rest = together(fresh, rollout, rest)
-    fresh, rollout = project(turn[1], normed, terms_of(1, rest, (INNER, RELAYED)), fresh, placing(is_early), rollout)
+    fresh, rollout = project(turn[1], normed, terms_of(1, rest, (3,)), fresh, placing(is_early), rollout)
     result = attended(1, moved[0], fresh, result)
 
-    terms = terms_of(0, own, everything) + terms_of(1, rest, everything)
-    moved, last = together(both(hop(result, 2), 2), last)
-    last[RELAYED], last[INNER] = relayed(late, last), across(late, last)
+    terms = terms_of(0, own, range(dps)) + terms_of(1, rest, range(dps))
+    moved = both(hop(result, 2), 2)
     result = attended(2, moved[0], project(turn[2], prepared(moved), terms), result)
+    result, last = together(result, last)
+    last[3] = handed_on(late, last)
     moved = both(hop(result, 3), 3)
     normed = prepared(moved)
     fresh, rollout = project(turn[3], normed, terms_of(2, last, (0, 1, 2), shift), None, placing(1 - is_early), rollout)
     fresh, rollout, last = together(fresh, rollout, last)
-    fresh, rollout = project(turn[3], normed, terms_of(2, last, (INNER, RELAYED)), fresh, placing(1 - is_early), rollout)
+    fresh, rollout = project(turn[3], normed, terms_of(2, last, (3,)), fresh, placing(1 - is_early), rollout)
     result = attended(3, moved[0], fresh, result)
     return (rollout[None], result[None, None])
 

time: 637 us -> 652 us (1.024)
  the two profiles are of different devices: /device:TPU:0 before, /device:TPU:7 now
where the time goes in v4:
time: 652 us; the launch traced here: 650 us
  waiting for transfers between devices  454 us (70%)
  Pallas kernels  91.7 us (14%)
  starting transfers between devices  49.8 us (8%)
  other arithmetic  28.8 us (4%)
  local copies, waits for them, and re-layouts  23.1 us (4%)
    ppermute x27, waiting for transfers between devices, over(): return lax.ppermute(value, ('section', axis), pairs)  454 us
    pallas_call x7, Pallas kernels, project(): pl.pallas_call(functools.partial(project_kernel, layout, len(lhs), bool(a...  59.6 us
    ppermute x27, starting transfers between devices, over(): return lax.ppermute(value, ('section', axis), pairs)  49.8 us
    pallas_call x4, Pallas kernels, attend(): pl.pallas_call(functools.partial(attend_kernel, share), out_shape=jax.Sha...  21.6 us
    convert_element_type x4, other arithmetic, normed_of(): (part.astype(jnp.float32) * inverse[:, None] * gain.astype(jnp.float32))....  15 us
  transfers between devices with their start and end apart: 27, of which 4 were waited for; matrix products, arithmetic and copies ran while one was open for 8% of the time, Pallas kernels for 10%

profile of v4, /device:TPU:7, one launch (start us, length us, event | category | flops | bytes accessed | tf_op | source)
XLA Modules:
  0.0 650.1 jit_solution(9989140991053784696)
XLA Ops:
  0.7 5.3 shard_map.77.refs_1_.refs_2_
  6.5 0.7 collective-permute-start.2
  7.9 1.2 constant_dynamic-slice_fusion
  9.1 0.7 collective-permute-start.3
  9.8 1.5 collective-permute-start.4
  11.2 1.5 collective-permute-start.5
  12.7 2.7 collective-permute-start
  15.4 2.7 collective-permute-start.1
  18.7 5.2 shard_map.79.refs_1_
  23.9 0.8 constant_dynamic-update-slice_fusion.3
  24.9 0.8 constant_dynamic-update-slice_fusion.2
  25.7 1.9 constant_dynamic-update-slice_fusion.1
  27.6 1.9 constant_dynamic-update-slice_fusion.refs_0_
  29.5 4.6 shard_map.78
  34.1 4.6 shard_map.80
  38.7 2.8 collective-permute-start.11
  41.5 1.7 convert_element_type.92
  43.2 0.7 collective-permute-start.7
  44.7 0.7 collective-permute-start.8
  45.7 0.7 slice.65
  46.4 0.7 collective-permute-start.9
  47.1 1.3 copy.18.held_ref
  49.0 0.7 reduce.3
  49.7 0.7 and_select_fusion.bias_ref
  50.4 0.9 fusion.21.f_ref
  51.3 2.9 shard_map.81.held_ref
  54.2 2.6 collective-permute-start.10
  56.8 2.7 collective-permute-start.12
  59.6 2.6 collective-permute-start.13
  62.1 3.1 collective-permute-start.21
  65.3 2.0 collective-permute-start.15
  67.3 0.7 slice.49
  68.0 1.3 collective-permute-start.14
  69.3 187.4 %collective-permute-done.14 = bf16[16,128]{1,0:T(8,128)(2,1)S(1)} collective-permute-done((bf16[16,128]{1,0:T(8,128)(2,1)S(1)}, bf16[16,128]{1,0:T(8,128)(2,1)S(1)}, u32[]{:S(2)}, u32[]{:S(2)}) %collective-permute-start.14) | collective-permute-done | bytes 4128 | tf_op jit(solution)/shard_map/ppermute | solution.py:230
  256.7 2.0 collective-permute-start.17
  258.7 0.8 collective-permute-start.16
  259.5 2.7 collective-permute-start.18
  263.4 4.6 constant_dynamic-update-slice_fusion.5
  268.0 4.6 constant_dynamic-update-slice_fusion.4.refs_2_
  272.6 2.6 collective-permute-start.22
  275.2 3.8 collective-permute-start.23
  279.1 2.1 fusion.3
  281.7 4.9 fusion.8
  286.6 6.8 %shard_map.82 = (f32[128,1024]{1,0:T(8,128)}, bf16[16384,1024]{1,0:T(8,128)(2,1)}) custom-call(s32[18]{0:T(128)} %stack.161.where_ref, bf16[128,8192]{1,0:T(8,128)(2,1)} %get-tuple-element.130.refs_0_, bf16[128,8192]{1,0:T(8,128)(2,1)} %get-tuple-element.131.refs_1_.refs_0_, bf16[2048,1024]{1,0:T(8,128)(2,1)} %shard_map.77.refs_1_.refs_2_, ...), custom_call_target="tpu_custom_call" | custom-call | tf_op jit(solution)/shard_map/pallas_call | solution.py:126
  293.5 5.0 shard_map.83
  298.4 2.9 shard_map.84.held_ref
  301.4 0.8 collective-permute-start.19
  302.2 2.0 collective-permute-start.20
  305.3 2.1 fusion.12
  307.4 4.8 fusion.14
  312.2 7.1 %shard_map.85.f_ref = f32[128,1024]{1,0:T(8,128)} custom-call(s32[20]{0:T(128)} %stack.162.where_ref, bf16[128,8192]{1,0:T(8,128)(2,1)} %get-tuple-element.129.refs_0_, bf16[128,8192]{1,0:T(8,128)(2,1)} %get-tuple-element.128.refs_1_, bf16[2048,1024]{1,0:T(8,128)(2,1)} %shard_map.77.refs_1_.refs_2_, bf16[2048,1024]{1,0:T(8,128)(2,1)} %collective-permute-done.refs_3_, ...), custom_call_target="tpu_custom_call" | custom-call | tf_op jit(solution)/shard_map/pallas_call | solution.py:126
  319.4 2.9 shard_map.86.held_ref
  322.3 167.3 %collective-permute-done.22.refs_3_ = bf16[4096,1024]{1,0:T(8,128)(2,1)} collective-permute-done((bf16[4096,1024]{1,0:T(8,128)(2,1)}, bf16[4096,1024]{1,0:T(8,128)(2,1)}, u32[]{:S(2)}, u32[]{:S(2)}) %collective-permute-start.22) | collective-permute-done | bytes 8388640 | tf_op jit(solution)/shard_map/ppermute | solution.py:230
  489.6 2.5 collective-permute-start.26
  492.1 1.3 collective-permute-start.24
  493.4 78.7 %collective-permute-done.24.x_ref = bf16[128,8192]{1,0:T(8,128)(2,1)S(1)} collective-permute-done((bf16[128,8192]{1,0:T(8,128)(2,1)}, bf16[128,8192]{1,0:T(8,128)(2,1)S(1)}, u32[]{:S(2)}, u32[]{:S(2)}) %collective-permute-start.24) | collective-permute-done | bytes 2097184 | tf_op jit(solution)/shard_map/ppermute | solution.py:230
  572.1 2.3 collective-permute-start.25
  577.0 0.7 stack.166.where_ref
  578.2 20.8 %collective-permute-done.25 = bf16[128,8192]{1,0:T(8,128)(2,1)} collective-permute-done((bf16[128,8192]{1,0:T(8,128)(2,1)S(1)}, bf16[128,8192]{1,0:T(8,128)(2,1)}, u32[]{:S(2)}, u32[]{:S(2)}) %collective-permute-start.25) | collective-permute-done | bytes 2097184 | tf_op jit(solution)/shard_map/ppermute | solution.py:230
  599.0 2.1 fusion.18
  601.0 4.7 fusion.20
  605.7 20.7 %shard_map.87 = (f32[128,1024]{1,0:T(8,128)}, bf16[16384,1024]{1,0:T(8,128)(2,1)}) custom-call(s32[16]{0:T(128)} %stack.166.where_ref, bf16[128,8192]{1,0:T(8,128)(2,1)} %get-tuple-element.127.refs_0_, bf16[128,8192]{1,0:T(8,128)(2,1)} %get-tuple-element.126.refs_1_, ...), custom_call_target="tpu_custom_call", output_to_operand_aliasing={{1}: (6, {})} | custom-call | tf_op jit(solution)/shard_map/pallas_call | solution.py:126
  626.5 10.7 %shard_map.88 = (f32[128,1024]{1,0:T(8,128)}, bf16[16384,1024]{1,0:T(8,128)(2,1)}) custom-call(s32[8]{0:T(128)} %stack.66.where_ref, bf16[128,8192]{1,0:T(8,128)(2,1)} %get-tuple-element.127.refs_0_, bf16[128,8192]{1,0:T(8,128)(2,1)} %get-tuple-element.126.refs_1_, ...), custom_call_target="tpu_custom_call", output_to_operand_aliasing={{1}: (5, {})} | custom-call | tf_op jit(solution)/shard_map/pallas_call | solution.py:126
  637.2 12.9 %shard_map.89 = bf16[128,8192]{1,0:T(8,128)(2,1)} custom-call(s32[1]{0:T(128)} %bitcast.active_ref, f32[8,16,256]{2,1,0:T(8,128)} %and_select_fusion.bias_ref, bf16[128,8192]{1,0:T(8,128)(2,1)} %copy-done.2, bf16[128,8192]{1,0:T(8,128)(2,1)} %bitcast.55, bf16[128,16,2048]{2,1,0:T(8,128)(2,1)} %bitcast.50, ...), custom_call_target="tpu_custom_call", output_to_operand_aliasing={{}: (6, {})} | custom-call | tf_op jit(solution)/shard_map/pallas_call | solution.py:191
  (67 shorter events, 8.2 us)
Async XLA Ops:
  0.6 5.4 copy-start
  0.7 6.5 %copy-start.5 = (bf16[1,8192]{1,0:T(2,128)(2,1)S(1)}, bf16[1,8192]{1,0:T(2,128)(2,1)}, u32[]{:S(2)}) copy-start(bf16[1,8192]{1,0:T(2,128)(2,1)} %param.7) | copy-start | bytes 49156
  6.5 0.8 collective-permute-start.2
  9.1 14.8 %collective-permute-start.3 = (bf16[128,2048]{1,0:T(8,128)(2,1)}, bf16[128,2048]{1,0:T(8,128)(2,1)S(1)}, u32[]{:S(2)}, u32[]{:S(2)}) collective-permute-start(bf16[128,2048]{1,0:T(8,128)(2,1)} %get-tuple-element.63), channel_id=1, source_target_pairs={{0,1},{1,0},{2,3},{3,2},{4,5},{5,4},{6,7},{7,6}} | collective-permute-start | bytes 1572872 | tf_op jit(solution)/shard_map/ppermute | solution.py:230
  9.8 14.1 %collective-permute-start.4 = (bf16[128,2048]{1,0:T(8,128)(2,1)}, bf16[128,2048]{1,0:T(8,128)(2,1)}, u32[]{:S(2)}, u32[]{:S(2)}) collective-permute-start(bf16[128,2048]{1,0:T(8,128)(2,1)} %get-tuple-element.64), channel_id=1, source_target_pairs={{0,2},{1,3},{2,0},{3,1},{4,6},{5,7},{6,4},{7,5}} | collective-permute-start | bytes 1572872 | tf_op jit(solution)/shard_map/ppermute | solution.py:230
  11.2 12.6 %collective-permute-start.5 = (bf16[128,2048]{1,0:T(8,128)(2,1)}, bf16[128,2048]{1,0:T(8,128)(2,1)}, u32[]{:S(2)}, u32[]{:S(2)}) collective-permute-start(bf16[128,2048]{1,0:T(8,128)(2,1)} %get-tuple-element.65), channel_id=1, source_target_pairs={{0,3},{1,2},{2,1},{3,0},{4,7},{5,6},{6,5},{7,4}} | collective-permute-start | bytes 1572872 | tf_op jit(solution)/shard_map/ppermute | solution.py:230
  12.7 41.5 %collective-permute-start = (bf16[2048,1024]{1,0:T(8,128)(2,1)}, bf16[2048,1024]{1,0:T(8,128)(2,1)}, u32[]{:S(2)}, u32[]{:S(2)}) collective-permute-start(bf16[2048,1024]{1,0:T(8,128)(2,1)} %shard_map.77.refs_1_.refs_2_), channel_id=1, source_target_pairs={{8,9},{9,8},{10,11},{11,10},{16,17},{17,16},{18,19},{19,18},{12,13... | collective-permute-start | bytes 12582920 | tf_op jit(solution)/shard_map/ppermute | solution.py:230
  15.4 38.9 %collective-permute-start.1 = (bf16[2048,1024]{1,0:T(8,128)(2,1)}, bf16[2048,1024]{1,0:T(8,128)(2,1)}, u32[]{:S(2)}, u32[]{:S(2)}) collective-permute-start(bf16[2048,1024]{1,0:T(8,128)(2,1)} %shard_map.77.refs_1_.refs_2_), channel_id=1, source_target_pairs={{8,10},{9,11},{10,8},{11,9},{16,18},{17,19},{18,16},{19,17},{12,14... | collective-permute-start | bytes 12582920 | tf_op jit(solution)/shard_map/ppermute | solution.py:230
  24.7 14.0 %collective-permute-start.6 = (bf16[1,8192]{1,0:T(2,128)(2,1)S(1)}, bf16[1,8192]{1,0:T(2,128)(2,1)S(1)}, u32[]{:S(2)}, u32[]{:S(2)}) collective-permute-start(bf16[1,8192]{1,0:T(2,128)(2,1)S(1)} %copy-done.5), channel_id=1, source_target_pairs={{0,4},{4,0},{8,12},{12,8},{16,20},{20,16},{24,28},{28,24},{1,5},{5... | collective-permute-start | bytes 49160 | tf_op jit(solution)/shard_map/ppermute | solution.py:230
  38.7 5.3 copy-start.4
  38.7 18.1 %collective-permute-start.11 = (bf16[2048,1024]{1,0:T(8,128)(2,1)}, bf16[2048,1024]{1,0:T(8,128)(2,1)}, u32[]{:S(2)}, u32[]{:S(2)}) collective-permute-start(bf16[2048,1024]{1,0:T(8,128)(2,1)} %shard_map.79.refs_1_), channel_id=1, source_target_pairs={{8,12},{12,8},{16,20},{20,16},{9,13},{13,9},{17,21},{21,17},{10,14... | collective-permute-start | bytes 12582920 | tf_op jit(solution)/shard_map/ppermute | solution.py:230
  43.2 0.7 collective-permute-start.7
  44.7 0.8 collective-permute-start.8
  45.5 3.5 copy-start.6
  46.4 4.0 collective-permute-start.9
  54.2 13.0 %collective-permute-start.10 = (bf16[2048,1024]{1,0:T(8,128)(2,1)}, bf16[2048,1024]{1,0:T(8,128)(2,1)}, u32[]{:S(2)}, u32[]{:S(2)}) collective-permute-start(bf16[2048,1024]{1,0:T(8,128)(2,1)} %collective-permute-done.1.refs_4_), channel_id=1, source_target_pairs={{8,9},{9,8},{10,11},{11,10},{16,17},{17,16},{18,19},{19,18},{12,13... | collective-permute-start | bytes 12582920 | tf_op jit(solution)/shard_map/ppermute | solution.py:230
  56.8 10.4 %collective-permute-start.12 = (bf16[2048,1024]{1,0:T(8,128)(2,1)}, bf16[2048,1024]{1,0:T(8,128)(2,1)}, u32[]{:S(2)}, u32[]{:S(2)}) collective-permute-start(bf16[2048,1024]{1,0:T(8,128)(2,1)} %collective-permute-done.11.refs_6_), channel_id=1, source_target_pairs={{8,9},{9,8},{10,11},{11,10},{16,17},{17,16},{18,19},{19,18},{12,13... | collective-permute-start | bytes 12582920 | tf_op jit(solution)/shard_map/ppermute | solution.py:230
  59.6 7.7 %collective-permute-start.13 = (bf16[2048,1024]{1,0:T(8,128)(2,1)}, bf16[2048,1024]{1,0:T(8,128)(2,1)}, u32[]{:S(2)}, u32[]{:S(2)}) collective-permute-start(bf16[2048,1024]{1,0:T(8,128)(2,1)} %collective-permute-done.11.refs_6_), channel_id=1, source_target_pairs={{8,10},{9,11},{10,8},{11,9},{16,18},{17,19},{18,16},{19,17},{12,14... | collective-permute-start | bytes 12582920 | tf_op jit(solution)/shard_map/ppermute | solution.py:230
  62.1 205.9 %collective-permute-start.21 = (bf16[2048,1024]{1,0:T(8,128)(2,1)}, bf16[2048,1024]{1,0:T(8,128)(2,1)}, u32[]{:S(2)}, u32[]{:S(2)}) collective-permute-start(bf16[2048,1024]{1,0:T(8,128)(2,1)} %shard_map.79.refs_1_), channel_id=1, source_target_pairs={{0,4},{4,0},{24,28},{28,24},{1,5},{5,1},{25,29},{29,25},{2,6},{6,2... | collective-permute-start | bytes 12582920 | tf_op jit(solution)/shard_map/ppermute | solution.py:230
  65.3 4.0 collective-permute-start.15
  68.0 188.7 %collective-permute-start.14 = (bf16[16,128]{1,0:T(8,128)(2,1)S(1)}, bf16[16,128]{1,0:T(8,128)(2,1)S(1)}, u32[]{:S(2)}, u32[]{:S(2)}) collective-permute-start(bf16[16,128]{1,0:T(8,128)(2,1)S(1)} %slice.49), channel_id=1, source_target_pairs={{8,0},{9,1},{10,2},{11,3},{16,24},{17,25},{18,26},{19,27},{12,4},{... | collective-permute-start | bytes 12296 | tf_op jit(solution)/shard_map/ppermute | solution.py:230
  256.7 22.4 %collective-permute-start.17 = (bf16[128,8192]{1,0:T(8,128)(2,1)}, bf16[128,8192]{1,0:T(8,128)(2,1)}, u32[]{:S(2)}, u32[]{:S(2)}) collective-permute-start(bf16[128,8192]{1,0:T(8,128)(2,1)} %collective-permute-done.15), channel_id=1, source_target_pairs={{0,8},{4,12},{1,9},{5,13},{2,10},{6,14},{3,11},{7,15}} | collective-permute-start | bytes 6291464 | tf_op jit(solution)/shard_map/ppermute | solution.py:230
  258.7 22.5 %collective-permute-start.16 = (bf16[128,8192]{1,0:T(8,128)(2,1)}, bf16[128,8192]{1,0:T(8,128)(2,1)S(1)}, u32[]{:S(2)}, u32[]{:S(2)}) collective-permute-start(bf16[128,8192]{1,0:T(8,128)(2,1)} %shard_map.81.held_ref), channel_id=1, source_target_pairs={{0,8},{4,12},{1,9},{5,13},{2,10},{6,14},{3,11},{7,15}} | collective-permute-start | bytes 6291464 | tf_op jit(solution)/shard_map/ppermute | solution.py:230
  259.5 34.0 %collective-permute-start.18 = (bf16[2048,1024]{1,0:T(8,128)(2,1)}, bf16[2048,1024]{1,0:T(8,128)(2,1)}, u32[]{:S(2)}, u32[]{:S(2)}) collective-permute-start(bf16[2048,1024]{1,0:T(8,128)(2,1)} %collective-permute-done.13.refs_8_), channel_id=1, source_target_pairs={{8,9},{9,8},{10,11},{11,10},{16,17},{17,16},{18,19},{19,18},{12,13... | collective-permute-start | bytes 12582920 | tf_op jit(solution)/shard_map/ppermute | solution.py:230
  272.6 217.0 %collective-permute-start.22 = (bf16[4096,1024]{1,0:T(8,128)(2,1)}, bf16[4096,1024]{1,0:T(8,128)(2,1)}, u32[]{:S(2)}, u32[]{:S(2)}) collective-permute-start(bf16[4096,1024]{1,0:T(8,128)(2,1)} %constant_dynamic-update-slice_fusion.4.refs_2_), channel_id=1, source_target_pairs={{0,1},{1,0},{2,3},{3,2},{24,25},{25,24},{26,27},{27,26},{4,5},{5,4... | collective-permute-start | bytes 25165832 | tf_op jit(solution)/shard_map/ppermute | solution.py:230
  275.2 214.4 %collective-permute-start.23 = (bf16[4096,1024]{1,0:T(8,128)(2,1)}, bf16[4096,1024]{1,0:T(8,128)(2,1)}, u32[]{:S(2)}, u32[]{:S(2)}) collective-permute-start(bf16[4096,1024]{1,0:T(8,128)(2,1)} %constant_dynamic-update-slice_fusion.4.refs_2_), channel_id=1, source_target_pairs={{0,2},{1,3},{2,0},{3,1},{24,26},{25,27},{26,24},{27,25},{4,6},{5,7... | collective-permute-start | bytes 25165832 | tf_op jit(solution)/shard_map/ppermute | solution.py:230
  281.2 5.4 copy-start.1
  301.4 0.8 collective-permute-start.19
  302.2 10.1 %copy-start.3 = (bf16[128,8192]{1,0:T(8,128)(2,1)}, bf16[128,8192]{1,0:T(8,128)(2,1)S(1)}, u32[]{:S(2)}) copy-start(bf16[128,8192]{1,0:T(8,128)(2,1)S(1)} %collective-permute-done.19.x_ref) | copy-start | bytes 6291460
  302.2 3.2 collective-permute-start.20
  489.6 136.8 %collective-permute-start.26 = (bf16[4096,1024]{1,0:T(8,128)(2,1)}, bf16[4096,1024]{1,0:T(8,128)(2,1)}, u32[]{:S(2)}, u32[]{:S(2)}) collective-permute-start(bf16[4096,1024]{1,0:T(8,128)(2,1)} %collective-permute-done.23.refs_4_), channel_id=1, source_target_pairs={{0,1},{1,0},{2,3},{3,2},{24,25},{25,24},{26,27},{27,26},{4,5},{5,4... | collective-permute-start | bytes 25165832 | tf_op jit(solution)/shard_map/ppermute | solution.py:230
  492.1 80.0 %collective-permute-start.24 = (bf16[128,8192]{1,0:T(8,128)(2,1)}, bf16[128,8192]{1,0:T(8,128)(2,1)S(1)}, u32[]{:S(2)}, u32[]{:S(2)}) collective-permute-start(bf16[128,8192]{1,0:T(8,128)(2,1)} %shard_map.86.held_ref), channel_id=1, source_target_pairs={{16,24},{20,28},{17,25},{21,29},{18,26},{22,30},{19,27},{23,31}} | collective-permute-start | bytes 6291464 | tf_op jit(solution)/shard_map/ppermute | solution.py:230
  572.1 33.7 %copy-start.2 = (bf16[128,8192]{1,0:T(8,128)(2,1)}, bf16[128,8192]{1,0:T(8,128)(2,1)S(1)}, u32[]{:S(2)}) copy-start(bf16[128,8192]{1,0:T(8,128)(2,1)S(1)} %collective-permute-done.24.x_ref) | copy-start | bytes 6291460
  572.1 26.9 %collective-permute-start.25 = (bf16[128,8192]{1,0:T(8,128)(2,1)S(1)}, bf16[128,8192]{1,0:T(8,128)(2,1)}, u32[]{:S(2)}, u32[]{:S(2)}) collective-permute-start(bf16[128,8192]{1,0:T(8,128)(2,1)S(1)} %collective-permute-done.24.x_ref), channel_id=1, source_target_pairs={{24,28},{28,24},{25,29},{29,25},{26,30},{30,26},{27,31},{31,27}} | collective-permute-start | bytes 6291464 | tf_op jit(solution)/shard_map/ppermute | solution.py:230

commit v5 on v4

--- a/solution.py
+++ b/solution.py
@@ -331,16 +331,18 @@
     own[3] = handed_on(early, own)
     own, rest = together(own, rest)
     rest[3] = handed_on(early, rest)
-    token = over("dp", dps, rest[2][:ROW_TILE, :HD], [(a, b, z, z) for a, b in ((1, 0), (2, 3)) for z in range(dps)])
-    token, late_own, parts = together(token, kept[0], parts)
-    whole = jnp.concatenate([late_own, late_rest], axis=0)
-    shift = jnp.isnan(token[0, 0]).astype(jnp.int32)
-    last = straight(late, whole)
-
     moved = [hop(part, 1) for part in parts]
     normed = prepared(moved)
     terms = terms_of(0, own, range(dps)) + terms_of(1, rest, (0, 1, 2))
     fresh, rollout = project(turn[1], normed, terms, None, placing(is_early))
+
+    token, fresh = together(rest[2][:ROW_TILE, :HD], fresh)
+    token = over("dp", dps, token, [(a, b, z, z) for a, b in ((1, 0), (2, 3)) for z in range(dps)])
+    token, late_own, fresh = together(token, kept[0], fresh)
+    whole = jnp.concatenate([late_own, late_rest], axis=0)
+    shift = jnp.isnan(token[0, 0]).astype(jnp.int32)
+    last = straight(late, whole)
+
     fresh, rollout, rest = together(fresh, rollout, rest)
     fresh, rollout = project(turn[1], normed, terms_of(1, rest, (3,)), fresh, placing(is_early), rollout)
     result = attended(1, moved[0], fresh, result)

time: 652 us -> 640 us (0.982)
  the two profiles are of different devices: /device:TPU:7 before, /device:TPU:0 now
where the time goes in v5:
time: 640 us; the launch traced here: 638 us
  waiting for transfers between devices  408 us (64%)
  Pallas kernels  96.8 us (15%)
  starting transfers between devices  79.1 us (12%)
  other arithmetic  28.4 us (4%)
  local copies, waits for them, and re-layouts  23.1 us (4%)
    ppermute x27, waiting for transfers between devices, over(): return lax.ppermute(value, ('section', axis), pairs)  408 us
    ppermute x27, starting transfers between devices, over(): return lax.ppermute(value, ('section', axis), pairs)  79.1 us
    pallas_call x7, Pallas kernels, project(): pl.pallas_call(functools.partial(project_kernel, layout, len(lhs), bool(a...  64.7 us
    pallas_call x4, Pallas kernels, attend(): pl.pallas_call(functools.partial(attend_kernel, share), out_shape=jax.Sha...  21.6 us
    convert_element_type x4, other arithmetic, normed_of(): (part.astype(jnp.float32) * inverse[:, None] * gain.astype(jnp.float32))....  14.8 us
  transfers between devices with their start and end apart: 27, of which 11 were waited for; matrix products, arithmetic and copies ran while one was open for 8% of the time, Pallas kernels for 12%

profile of v5, /device:TPU:0, one launch (start us, length us, event | category | flops | bytes accessed | tf_op | source)
XLA Modules:
  0.0 638.3 jit_solution(13441208436571177064)
XLA Ops:
  0.7 5.3 shard_map.77.refs_1_.refs_2_
  6.5 4.9 collective-permute-start.2
  11.5 1.4 collective-permute-done.2
  13.5 1.2 constant_dynamic-slice_fusion
  14.7 4.0 collective-permute-start.3
  18.7 4.5 collective-permute-start.4
  23.2 1.9 collective-permute-start.5
  25.1 2.7 collective-permute-start.1
  27.9 2.7 collective-permute-start
  31.2 5.2 shard_map.79.refs_1_
  36.4 53.0 %collective-permute-done.4 = bf16[128,2048]{1,0:T(8,128)(2,1)} collective-permute-done((bf16[128,2048]{1,0:T(8,128)(2,1)}, bf16[128,2048]{1,0:T(8,128)(2,1)}, u32[]{:S(2)}, u32[]{:S(2)}) %collective-permute-start.4) | collective-permute-done | bytes 524320 | tf_op jit(solution)/shard_map/ppermute | solution.py:230
  89.4 1.6 collective-permute-start.6
  91.0 0.8 constant_dynamic-update-slice_fusion.3
  92.7 1.9 constant_dynamic-update-slice_fusion.1
  94.6 1.9 constant_dynamic-update-slice_fusion.refs_0_
  96.4 7.1 %shard_map.78 = f32[512,1024]{1,0:T(8,128)} custom-call(s32[6]{0:T(128)} %pad_add_fusion.where_ref, bf16[512,2048]{1,0:T(8,128)(2,1)} %constant_dynamic-update-slice_fusion.refs_0_, bf16[2048,1024]{1,0:T(8,128)(2,1)} %shard_map.77.refs_1_.refs_2_), custom_call_target="tpu_custom_call" | custom-call | tf_op jit(solution)/shard_map/pallas_call | solution.py:126
  103.6 7.2 %shard_map.80 = f32[512,1024]{1,0:T(8,128)} custom-call(s32[6]{0:T(128)} %pad_add_fusion.where_ref, bf16[512,2048]{1,0:T(8,128)(2,1)} %constant_dynamic-update-slice_fusion.refs_0_, bf16[2048,1024]{1,0:T(8,128)(2,1)} %shard_map.79.refs_1_), custom_call_target="tpu_custom_call" | custom-call | tf_op jit(solution)/shard_map/pallas_call | solution.py:126
  110.7 2.8 collective-permute-start.14
  113.5 1.7 convert_element_type.92
  115.2 2.3 collective-permute-start.7
  117.6 14.4 %collective-permute-done.7 = bf16[512,1024]{1,0:T(8,128)(2,1)S(1)} collective-permute-done((bf16[512,1024]{1,0:T(8,128)(2,1)S(1)}, bf16[512,1024]{1,0:T(8,128)(2,1)S(1)}, u32[]{:S(2)}, u32[]{:S(2)}) %collective-permute-start.7) | collective-permute-done | bytes 1048608 | tf_op jit(solution)/shard_map/ppermute | solution.py:230
  132.6 13.6 %collective-permute-start.8 = (bf16[2,128,1024]{2,1,0:T(8,128)(2,1)S(1)}, bf16[2,128,1024]{2,1,0:T(8,128)(2,1)S(1)}, u32[]{:S(2)}, u32[]{:S(2)}) collective-permute-start(bf16[2,128,1024]{2,1,0:T(8,128)(2,1)S(1)} %pad_maximum_fusion), channel_id=1, source_target_pairs={{0,1},{1,0},{2,3},{3,2},{4,5},{5,4},{6,7},{7,6}} | collective-permute-start | bytes 1572872 | tf_op jit(solution)/shard_map/ppermute | solution.py:230
  146.4 52.5 %collective-permute-done.8 = bf16[2,128,1024]{2,1,0:T(8,128)(2,1)S(1)} collective-permute-done((bf16[2,128,1024]{2,1,0:T(8,128)(2,1)S(1)}, bf16[2,128,1024]{2,1,0:T(8,128)(2,1)S(1)}, u32[]{:S(2)}, u32[]{:S(2)}) %collective-permute-start.8) | collective-permute-done | bytes 524320 | tf_op jit(solution)/shard_map/ppermute | solution.py:230
  199.8 2.3 collective-permute-start.9
  202.2 1.3 copy.18.held_ref
  205.4 36.2 %collective-permute-done.9 = bf16[1,128,1024]{2,1,0:T(8,128)(2,1)S(1)} collective-permute-done((bf16[1,128,1024]{2,1,0:T(8,128)(2,1)}, bf16[1,128,1024]{2,1,0:T(8,128)(2,1)S(1)}, u32[]{:S(2)}, u32[]{:S(2)}) %collective-permute-start.9) | collective-permute-done | bytes 262176 | tf_op jit(solution)/shard_map/ppermute | solution.py:230
  241.6 0.9 fusion.21.f_ref
  242.4 12.8 %shard_map.81.held_ref = bf16[128,8192]{1,0:T(8,128)(2,1)} custom-call(s32[1]{0:T(128)} %bitcast.12.active_ref, f32[8,16,256]{2,1,0:T(8,128)} %and_select_fusion.bias_ref, bf16[128,8192]{1,0:T(8,128)(2,1)} %bitcast.58, bf16[128,8192]{1,0:T(8,128)(2,1)} %bitcast.52, bf16[128,16,2048]{2,1,0:T(8,128)(2,1)} %bitcast.47, ...), custom_call_target="tpu_custom_call", output_to_operand_aliasing={{}: (6, {})} | custom-call | tf_op jit(solution)/shard_map/pallas_call | solution.py:191
  255.3 3.4 collective-permute-start.11
  258.7 2.6 collective-permute-start.13
  261.3 2.6 collective-permute-start.16
  263.9 2.7 collective-permute-start.15
  266.6 1.4 collective-permute-start.10
  268.0 15.5 %collective-permute-done.11 = bf16[128,8192]{1,0:T(8,128)(2,1)} collective-permute-done((bf16[128,8192]{1,0:T(8,128)(2,1)}, bf16[128,8192]{1,0:T(8,128)(2,1)}, u32[]{:S(2)}, u32[]{:S(2)}) %collective-permute-start.11) | collective-permute-done | bytes 2097184 | tf_op jit(solution)/shard_map/ppermute | solution.py:230
  283.5 2.7 collective-permute-start.12
  286.2 3.4 collective-permute-start.21
  290.9 2.1 fusion.3
  293.0 2.7 collective-permute-start.18
  295.7 4.7 fusion.8
  301.0 6.9 %shard_map.82 = (f32[128,1024]{1,0:T(8,128)}, bf16[16384,1024]{1,0:T(8,128)(2,1)}) custom-call(s32[18]{0:T(128)} %stack.161.where_ref, bf16[128,8192]{1,0:T(8,128)(2,1)} %get-tuple-element.132.refs_0_, bf16[128,8192]{1,0:T(8,128)(2,1)} %get-tuple-element.133.refs_1_.refs_0_, bf16[2048,1024]{1,0:T(8,128)(2,1)} %shard_map.77.refs_1_.refs_2_, ...), custom_call_target="tpu_custom_call" | custom-call | tf_op jit(solution)/shard_map/pallas_call | solution.py:126
  307.9 1.3 collective-permute-start.17
  309.2 15.1 %collective-permute-done.17 = bf16[16,128]{1,0:T(8,128)(2,1)S(1)} collective-permute-done((bf16[16,128]{1,0:T(8,128)(2,1)S(1)}, bf16[16,128]{1,0:T(8,128)(2,1)S(1)}, u32[]{:S(2)}, u32[]{:S(2)}) %collective-permute-start.17) | collective-permute-done | bytes 4128 | tf_op jit(solution)/shard_map/ppermute | solution.py:230
  324.2 4.6 constant_dynamic-update-slice_fusion.5
  328.8 8.1 %collective-permute-done.21 = bf16[2048,1024]{1,0:T(8,128)(2,1)} collective-permute-done((bf16[2048,1024]{1,0:T(8,128)(2,1)}, bf16[2048,1024]{1,0:T(8,128)(2,1)}, u32[]{:S(2)}, u32[]{:S(2)}) %collective-permute-start.21) | collective-permute-done | bytes 4194336 | tf_op jit(solution)/shard_map/ppermute | solution.py:230
  336.9 4.6 constant_dynamic-update-slice_fusion.4.refs_2_
  341.5 2.1 collective-permute-start.23
  343.6 3.3 collective-permute-start.22
  347.5 5.0 shard_map.83
  352.5 2.9 shard_map.84.held_ref
  356.2 2.0 collective-permute-start.20
  359.4 2.1 fusion.12
  361.5 4.8 fusion.14
  366.3 7.1 %shard_map.85.f_ref = f32[128,1024]{1,0:T(8,128)} custom-call(s32[20]{0:T(128)} %stack.162.where_ref, bf16[128,8192]{1,0:T(8,128)(2,1)} %get-tuple-element.131.refs_0_, bf16[128,8192]{1,0:T(8,128)(2,1)} %get-tuple-element.130.refs_1_, bf16[2048,1024]{1,0:T(8,128)(2,1)} %shard_map.77.refs_1_.refs_2_, bf16[2048,1024]{1,0:T(8,128)(2,1)} %collective-permute-done.refs_3_, ...), custom_call_target="tpu_custom_call" | custom-call | tf_op jit(solution)/shard_map/pallas_call | solution.py:126
  373.4 2.9 shard_map.86.held_ref
  376.4 149.9 %collective-permute-done.23.refs_4_ = bf16[4096,1024]{1,0:T(8,128)(2,1)} collective-permute-done((bf16[4096,1024]{1,0:T(8,128)(2,1)}, bf16[4096,1024]{1,0:T(8,128)(2,1)}, u32[]{:S(2)}, u32[]{:S(2)}) %collective-permute-start.23) | collective-permute-done | bytes 8388640 | tf_op jit(solution)/shard_map/ppermute | solution.py:230
  526.3 2.7 collective-permute-done.22.refs_3_
  529.0 1.9 collective-permute-start.26
  531.7 2.1 collective-permute-start.25
  537.6 2.1 fusion.18
  539.7 4.7 fusion.20
  544.4 20.7 %shard_map.87 = (f32[128,1024]{1,0:T(8,128)}, bf16[16384,1024]{1,0:T(8,128)(2,1)}) custom-call(s32[16]{0:T(128)} %stack.166.where_ref, bf16[128,8192]{1,0:T(8,128)(2,1)} %get-tuple-element.129.refs_0_, bf16[128,8192]{1,0:T(8,128)(2,1)} %get-tuple-element.128.refs_1_, ...), custom_call_target="tpu_custom_call", output_to_operand_aliasing={{1}: (6, {})} | custom-call | tf_op jit(solution)/shard_map/pallas_call | solution.py:126
  565.1 59.5 %collective-permute-done.26.refs_2_ = bf16[4096,1024]{1,0:T(8,128)(2,1)} collective-permute-done((bf16[4096,1024]{1,0:T(8,128)(2,1)}, bf16[4096,1024]{1,0:T(8,128)(2,1)}, u32[]{:S(2)}, u32[]{:S(2)}) %collective-permute-start.26) | collective-permute-done | bytes 8388640 | tf_op jit(solution)/shard_map/ppermute | solution.py:230
  624.7 10.7 %shard_map.88 = (f32[128,1024]{1,0:T(8,128)}, bf16[16384,1024]{1,0:T(8,128)(2,1)}) custom-call(s32[8]{0:T(128)} %stack.66.where_ref, bf16[128,8192]{1,0:T(8,128)(2,1)} %get-tuple-element.129.refs_0_, bf16[128,8192]{1,0:T(8,128)(2,1)} %get-tuple-element.128.refs_1_, ...), custom_call_target="tpu_custom_call", output_to_operand_aliasing={{1}: (5, {})} | custom-call | tf_op jit(solution)/shard_map/pallas_call | solution.py:126
  635.4 2.9 shard_map.89
  (67 shorter events, 13.8 us)
Async XLA Ops:
  0.6 5.4 copy-start
  0.7 10.8 %copy-start.5 = (bf16[1,8192]{1,0:T(2,128)(2,1)S(1)}, bf16[1,8192]{1,0:T(2,128)(2,1)}, u32[]{:S(2)}) copy-start(bf16[1,8192]{1,0:T(2,128)(2,1)} %param.7) | copy-start | bytes 49156
  6.5 6.4 %collective-permute-start.2 = (f32[128]{0:T(128)S(1)}, f32[128]{0:T(128)S(1)}, u32[]{:S(2)}, u32[]{:S(2)}) collective-permute-start(f32[128]{0:T(128)S(1)} %fusion), channel_id=1, source_target_pairs={{0,4},{4,0},{1,5},{5,1},{2,6},{6,2},{3,7},{7,3}} | collective-permute-start | bytes 1544 | tf_op jit(solution)/shard_map/ppermute | solution.py:230
  14.7 21.6 %collective-permute-start.3 = (bf16[128,2048]{1,0:T(8,128)(2,1)}, bf16[128,2048]{1,0:T(8,128)(2,1)S(1)}, u32[]{:S(2)}, u32[]{:S(2)}) collective-permute-start(bf16[128,2048]{1,0:T(8,128)(2,1)} %get-tuple-element.64), channel_id=1, source_target_pairs={{0,1},{1,0},{2,3},{3,2},{4,5},{5,4},{6,7},{7,6}} | collective-permute-start | bytes 1572872 | tf_op jit(solution)/shard_map/ppermute | solution.py:230
  18.7 70.7 %collective-permute-start.4 = (bf16[128,2048]{1,0:T(8,128)(2,1)}, bf16[128,2048]{1,0:T(8,128)(2,1)}, u32[]{:S(2)}, u32[]{:S(2)}) collective-permute-start(bf16[128,2048]{1,0:T(8,128)(2,1)} %get-tuple-element.65), channel_id=1, source_target_pairs={{0,2},{1,3},{2,0},{3,1},{4,6},{5,7},{6,4},{7,5}} | collective-permute-start | bytes 1572872 | tf_op jit(solution)/shard_map/ppermute | solution.py:230
  23.2 66.2 %collective-permute-start.5 = (bf16[128,2048]{1,0:T(8,128)(2,1)}, bf16[128,2048]{1,0:T(8,128)(2,1)}, u32[]{:S(2)}, u32[]{:S(2)}) collective-permute-start(bf16[128,2048]{1,0:T(8,128)(2,1)} %get-tuple-element.66), channel_id=1, source_target_pairs={{0,3},{1,2},{2,1},{3,0},{4,7},{5,6},{6,5},{7,4}} | collective-permute-start | bytes 1572872 | tf_op jit(solution)/shard_map/ppermute | solution.py:230
  25.1 230.1 %collective-permute-start.1 = (bf16[2048,1024]{1,0:T(8,128)(2,1)}, bf16[2048,1024]{1,0:T(8,128)(2,1)}, u32[]{:S(2)}, u32[]{:S(2)}) collective-permute-start(bf16[2048,1024]{1,0:T(8,128)(2,1)} %shard_map.77.refs_1_.refs_2_), channel_id=1, source_target_pairs={{8,10},{9,11},{10,8},{11,9},{16,18},{17,19},{18,16},{19,17},{12,14... | collective-permute-start | bytes 12582920 | tf_op jit(solution)/shard_map/ppermute | solution.py:230
  27.9 227.4 %collective-permute-start = (bf16[2048,1024]{1,0:T(8,128)(2,1)}, bf16[2048,1024]{1,0:T(8,128)(2,1)}, u32[]{:S(2)}, u32[]{:S(2)}) collective-permute-start(bf16[2048,1024]{1,0:T(8,128)(2,1)} %shard_map.77.refs_1_.refs_2_), channel_id=1, source_target_pairs={{8,9},{9,8},{10,11},{11,10},{16,17},{17,16},{18,19},{19,18},{12,13... | collective-permute-start | bytes 12582920 | tf_op jit(solution)/shard_map/ppermute | solution.py:230
  89.4 21.3 %collective-permute-start.6 = (bf16[1,8192]{1,0:T(2,128)(2,1)S(1)}, bf16[1,8192]{1,0:T(2,128)(2,1)S(1)}, u32[]{:S(2)}, u32[]{:S(2)}) collective-permute-start(bf16[1,8192]{1,0:T(2,128)(2,1)S(1)} %copy-done.5), channel_id=1, source_target_pairs={{0,4},{4,0},{8,12},{12,8},{16,20},{20,16},{24,28},{28,24},{1,5},{5... | collective-permute-start | bytes 49160 | tf_op jit(solution)/shard_map/ppermute | solution.py:230
  110.7 21.2 %copy-start.4 = (f32[512,1024]{1,0:T(8,128)S(1)}, f32[512,1024]{1,0:T(8,128)}, u32[]{:S(2)}) copy-start(f32[512,1024]{1,0:T(8,128)} %shard_map.78) | copy-start | bytes 6291460
  110.7 150.6 %collective-permute-start.14 = (bf16[2048,1024]{1,0:T(8,128)(2,1)}, bf16[2048,1024]{1,0:T(8,128)(2,1)}, u32[]{:S(2)}, u32[]{:S(2)}) collective-permute-start(bf16[2048,1024]{1,0:T(8,128)(2,1)} %shard_map.79.refs_1_), channel_id=1, source_target_pairs={{8,12},{12,8},{16,20},{20,16},{9,13},{13,9},{17,21},{21,17},{10,14... | collective-permute-start | bytes 12582920 | tf_op jit(solution)/shard_map/ppermute | solution.py:230
  115.2 16.7 %collective-permute-start.7 = (bf16[512,1024]{1,0:T(8,128)(2,1)S(1)}, bf16[512,1024]{1,0:T(8,128)(2,1)S(1)}, u32[]{:S(2)}, u32[]{:S(2)}) collective-permute-start(bf16[512,1024]{1,0:T(8,128)(2,1)S(1)} %convert_element_type.92), channel_id=1, source_target_pairs={{0,4},{4,0},{1,5},{5,1},{2,6},{6,2},{3,7},{7,3}} | collective-permute-start | bytes 3145736 | tf_op jit(solution)/shard_map/ppermute | solution.py:230
  132.6 66.3 %collective-permute-start.8 = (bf16[2,128,1024]{2,1,0:T(8,128)(2,1)S(1)}, bf16[2,128,1024]{2,1,0:T(8,128)(2,1)S(1)}, u32[]{:S(2)}, u32[]{:S(2)}) collective-permute-start(bf16[2,128,1024]{2,1,0:T(8,128)(2,1)S(1)} %pad_maximum_fusion), channel_id=1, source_target_pairs={{0,1},{1,0},{2,3},{3,2},{4,5},{5,4},{6,7},{7,6}} | collective-permute-start | bytes 1572872 | tf_op jit(solution)/shard_map/ppermute | solution.py:230
  146.3 57.6 %copy-start.6 = (s32[1,128]{1,0:T(1,128)S(1)}, s32[1,128]{1,0:T(1,128)}, u32[]{:S(2)}) copy-start(s32[1,128]{1,0:T(1,128)} %param.11) | copy-start | bytes 1540
  199.8 41.7 %collective-permute-start.9 = (bf16[1,128,1024]{2,1,0:T(8,128)(2,1)}, bf16[1,128,1024]{2,1,0:T(8,128)(2,1)S(1)}, u32[]{:S(2)}, u32[]{:S(2)}) collective-permute-start(bf16[1,128,1024]{2,1,0:T(8,128)(2,1)} %slice.65), channel_id=1, source_target_pairs={{0,2},{1,3},{2,0},{3,1},{4,6},{5,7},{6,4},{7,5}} | collective-permute-start | bytes 786440 | tf_op jit(solution)/shard_map/ppermute | solution.py:230
  255.3 28.2 %collective-permute-start.11 = (bf16[128,8192]{1,0:T(8,128)(2,1)}, bf16[128,8192]{1,0:T(8,128)(2,1)}, u32[]{:S(2)}, u32[]{:S(2)}) collective-permute-start(bf16[128,8192]{1,0:T(8,128)(2,1)} %shard_map.81.held_ref), channel_id=1, source_target_pairs={{0,4},{4,0},{1,5},{5,1},{2,6},{6,2},{3,7},{7,3}} | collective-permute-start | bytes 6291464 | tf_op jit(solution)/shard_map/ppermute | solution.py:230
  258.7 34.3 %collective-permute-start.13 = (bf16[2048,1024]{1,0:T(8,128)(2,1)}, bf16[2048,1024]{1,0:T(8,128)(2,1)}, u32[]{:S(2)}, u32[]{:S(2)}) collective-permute-start(bf16[2048,1024]{1,0:T(8,128)(2,1)} %collective-permute-done.1.refs_4_), channel_id=1, source_target_pairs={{8,9},{9,8},{10,11},{11,10},{16,17},{17,16},{18,19},{19,18},{12,13... | collective-permute-start | bytes 12582920 | tf_op jit(solution)/shard_map/ppermute | solution.py:230
  261.3 31.7 %collective-permute-start.16 = (bf16[2048,1024]{1,0:T(8,128)(2,1)}, bf16[2048,1024]{1,0:T(8,128)(2,1)}, u32[]{:S(2)}, u32[]{:S(2)}) collective-permute-start(bf16[2048,1024]{1,0:T(8,128)(2,1)} %collective-permute-done.14.refs_6_), channel_id=1, source_target_pairs={{8,10},{9,11},{10,8},{11,9},{16,18},{17,19},{18,16},{19,17},{12,14... | collective-permute-start | bytes 12582920 | tf_op jit(solution)/shard_map/ppermute | solution.py:230
  263.9 29.1 %collective-permute-start.15 = (bf16[2048,1024]{1,0:T(8,128)(2,1)}, bf16[2048,1024]{1,0:T(8,128)(2,1)}, u32[]{:S(2)}, u32[]{:S(2)}) collective-permute-start(bf16[2048,1024]{1,0:T(8,128)(2,1)} %collective-permute-done.14.refs_6_), channel_id=1, source_target_pairs={{8,9},{9,8},{10,11},{11,10},{16,17},{17,16},{18,19},{19,18},{12,13... | collective-permute-start | bytes 12582920 | tf_op jit(solution)/shard_map/ppermute | solution.py:230
  266.6 19.6 %collective-permute-start.10 = (bf16[128,8192]{1,0:T(8,128)(2,1)}, bf16[128,8192]{1,0:T(8,128)(2,1)S(1)}, u32[]{:S(2)}, u32[]{:S(2)}) collective-permute-start(bf16[128,8192]{1,0:T(8,128)(2,1)} %shard_map.81.held_ref), channel_id=1, source_target_pairs={{0,8},{4,12},{1,9},{5,13},{2,10},{6,14},{3,11},{7,15}} | collective-permute-start | bytes 6291464 | tf_op jit(solution)/shard_map/ppermute | solution.py:230
  283.5 7.4 %collective-permute-start.12 = (bf16[128,8192]{1,0:T(8,128)(2,1)}, bf16[128,8192]{1,0:T(8,128)(2,1)}, u32[]{:S(2)}, u32[]{:S(2)}) collective-permute-start(bf16[128,8192]{1,0:T(8,128)(2,1)} %collective-permute-done.11), channel_id=1, source_target_pairs={{0,8},{4,12},{1,9},{5,13},{2,10},{6,14},{3,11},{7,15}} | collective-permute-start | bytes 6291464 | tf_op jit(solution)/shard_map/ppermute | solution.py:230
  286.2 14.1 %copy-start.1 = (bf16[128,8192]{1,0:T(8,128)(2,1)}, bf16[128,8192]{1,0:T(8,128)(2,1)S(1)}, u32[]{:S(2)}) copy-start(bf16[128,8192]{1,0:T(8,128)(2,1)S(1)} %collective-permute-done.10.x_ref) | copy-start | bytes 6291460
  286.2 50.7 %collective-permute-start.21 = (bf16[2048,1024]{1,0:T(8,128)(2,1)}, bf16[2048,1024]{1,0:T(8,128)(2,1)}, u32[]{:S(2)}, u32[]{:S(2)}) collective-permute-start(bf16[2048,1024]{1,0:T(8,128)(2,1)} %shard_map.79.refs_1_), channel_id=1, source_target_pairs={{0,4},{4,0},{24,28},{28,24},{1,5},{5,1},{25,29},{29,25},{2,6},{6,2... | collective-permute-start | bytes 12582920 | tf_op jit(solution)/shard_map/ppermute | solution.py:230
  293.0 54.5 %collective-permute-start.18 = (bf16[2048,1024]{1,0:T(8,128)(2,1)}, bf16[2048,1024]{1,0:T(8,128)(2,1)}, u32[]{:S(2)}, u32[]{:S(2)}) collective-permute-start(bf16[2048,1024]{1,0:T(8,128)(2,1)} %collective-permute-done.16.refs_8_), channel_id=1, source_target_pairs={{8,9},{9,8},{10,11},{11,10},{16,17},{17,16},{18,19},{19,18},{12,13... | collective-permute-start | bytes 12582920 | tf_op jit(solution)/shard_map/ppermute | solution.py:230
  307.9 16.4 %collective-permute-start.17 = (bf16[16,128]{1,0:T(8,128)(2,1)S(1)}, bf16[16,128]{1,0:T(8,128)(2,1)S(1)}, u32[]{:S(2)}, u32[]{:S(2)}) collective-permute-start(bf16[16,128]{1,0:T(8,128)(2,1)S(1)} %slice.49), channel_id=1, source_target_pairs={{8,0},{9,1},{10,2},{11,3},{16,24},{17,25},{18,26},{19,27},{12,4},{... | collective-permute-start | bytes 12296 | tf_op jit(solution)/shard_map/ppermute | solution.py:230
  341.5 184.8 %collective-permute-start.23 = (bf16[4096,1024]{1,0:T(8,128)(2,1)}, bf16[4096,1024]{1,0:T(8,128)(2,1)}, u32[]{:S(2)}, u32[]{:S(2)}) collective-permute-start(bf16[4096,1024]{1,0:T(8,128)(2,1)} %constant_dynamic-update-slice_fusion.4.refs_2_), channel_id=1, source_target_pairs={{0,2},{1,3},{2,0},{3,1},{24,26},{25,27},{26,24},{27,25},{4,6},{5,7... | collective-permute-start | bytes 25165832 | tf_op jit(solution)/shard_map/ppermute | solution.py:230
  343.6 185.4 %collective-permute-start.22 = (bf16[4096,1024]{1,0:T(8,128)(2,1)}, bf16[4096,1024]{1,0:T(8,128)(2,1)}, u32[]{:S(2)}, u32[]{:S(2)}) collective-permute-start(bf16[4096,1024]{1,0:T(8,128)(2,1)} %constant_dynamic-update-slice_fusion.4.refs_2_), channel_id=1, source_target_pairs={{0,1},{1,0},{2,3},{3,2},{24,25},{25,24},{26,27},{27,26},{4,5},{5,4... | collective-permute-start | bytes 25165832 | tf_op jit(solution)/shard_map/ppermute | solution.py:230
  355.4 0.8 collective-permute-start.19
  356.2 10.1 %copy-start.3 = (bf16[128,8192]{1,0:T(8,128)(2,1)}, bf16[128,8192]{1,0:T(8,128)(2,1)S(1)}, u32[]{:S(2)}) copy-start(bf16[128,8192]{1,0:T(8,128)(2,1)S(1)} %collective-permute-done.19.x_ref) | copy-start | bytes 6291460
  356.2 3.2 collective-permute-start.20
  529.0 95.6 %collective-permute-start.26 = (bf16[4096,1024]{1,0:T(8,128)(2,1)}, bf16[4096,1024]{1,0:T(8,128)(2,1)}, u32[]{:S(2)}, u32[]{:S(2)}) collective-permute-start(bf16[4096,1024]{1,0:T(8,128)(2,1)} %collective-permute-done.23.refs_4_), channel_id=1, source_target_pairs={{0,1},{1,0},{2,3},{3,2},{24,25},{25,24},{26,27},{27,26},{4,5},{5,4... | collective-permute-start | bytes 25165832 | tf_op jit(solution)/shard_map/ppermute | solution.py:230
  530.9 0.8 collective-permute-start.24
  531.7 12.7 %copy-start.2 = (bf16[128,8192]{1,0:T(8,128)(2,1)}, bf16[128,8192]{1,0:T(8,128)(2,1)S(1)}, u32[]{:S(2)}) copy-start(bf16[128,8192]{1,0:T(8,128)(2,1)S(1)} %collective-permute-done.24.x_ref) | copy-start | bytes 6291460
  531.7 5.9 collective-permute-start.25

commit v6 on v5

--- a/solution.py
+++ b/solution.py
@@ -305,7 +305,9 @@
         received = [over_tensor(kept[j], at, j) for j in range(1, tensors)]
         return received[0] if len(received) == 1 else jnp.concatenate(received, axis=0)
 
-    own = straight(early, kept[0])
+    own = {0: kept[0], 1: over_dp(kept[0], early, flipped(1))}
+    later, kept[1:] = together(kept[0], kept[1:])
+    own[2] = over_dp(later, early, flipped(2))
 
     lhs = [jnp.concatenate(first, axis=0)]
     partial = [project(turn[0], lhs, [(kept[j], [(0, 0, 0, 0, depth)])]) for j in range(tensors)]
@@ -325,6 +327,7 @@
     result = attended(0, hidden, fresh, hidden)
 
     rest = straight(early, rest)
+    own[1], result = together(own[1], result)
     own, result, kept = together(own, result, kept)
     parts = both(result, 0)
     late_rest = others(late, kept)
@@ -338,8 +341,7 @@
 
     token, fresh = together(rest[2][:ROW_TILE, :HD], fresh)
     token = over("dp", dps, token, [(a, b, z, z) for a, b in ((1, 0), (2, 3)) for z in range(dps)])
-    token, late_own, fresh = together(token, kept[0], fresh)
-    whole = jnp.concatenate([late_own, late_rest], axis=0)
+    token, whole, fresh = together(token, jnp.concatenate([kept[0], late_rest], axis=0), fresh)
     shift = jnp.isnan(token[0, 0]).astype(jnp.int32)
     last = straight(late, whole)
 

time: 640 us -> 626 us (0.978)
  starting transfers between devices: 79.1 us -> 69.4 us
  local copies, waits for them, and re-layouts: 23.1 us -> 14 us
  other arithmetic: 28.4 us -> 36.2 us
    ppermute x27, starting transfers between devices: 79.1 us -> 69.4 us  [over(): return lax.ppermute(value, ('section', axis), pairs)]
    concatenate x0 -> x1, other arithmetic: none -> 7.67 us  [body(): jnp.concatenate([kept[0], late_rest], axis=0)]
  transfers between devices with their start and end apart: 27 -> 27, of which waited for: 11 -> 13; matrix products, arithmetic and copies ran while one was open for 8% -> 8% of each run, Pallas kernels for 12% -> 12%
where the time goes in v6:
time: 626 us; the launch traced here: 625 us
  waiting for transfers between devices  406 us (65%)
  Pallas kernels  96.8 us (15%)
  starting transfers between devices  69.4 us (11%)
  other arithmetic  36.2 us (6%)
  local copies, waits for them, and re-layouts  14 us (2%)
    ppermute x27, waiting for transfers between devices, over(): return lax.ppermute(value, ('section', axis), pairs)  406 us
    ppermute x27, starting transfers between devices, over(): return lax.ppermute(value, ('section', axis), pairs)  69.4 us
    pallas_call x7, Pallas kernels, project(): pl.pallas_call(functools.partial(project_kernel, layout, len(lhs), bool(a...  64.6 us
    pallas_call x4, Pallas kernels, attend(): pl.pallas_call(functools.partial(attend_kernel, share), out_shape=jax.Sha...  21.6 us
    convert_element_type x4, other arithmetic, normed_of(): (part.astype(jnp.float32) * inverse[:, None] * gain.astype(jnp.float32))....  14.8 us
  transfers between devices with their start and end apart: 27, of which 13 were waited for; matrix products, arithmetic and copies ran while one was open for 8% of the time, Pallas kernels for 12%

profile of v6, /device:TPU:0, one launch (start us, length us, event | category | flops | bytes accessed | tf_op | source)
XLA Modules:
  0.0 624.7 jit_solution(13497203953428254463)
XLA Ops:
  0.7 5.4 shard_map.77.refs_1_.refs_2_
  6.5 4.9 collective-permute-start.1
  11.5 1.4 collective-permute-done.1
  13.5 1.2 constant_dynamic-slice_fusion
  14.7 4.0 collective-permute-start.2
  18.7 4.5 collective-permute-start.3
  23.2 1.9 collective-permute-start.4
  25.1 2.6 collective-permute-start
  28.4 5.2 shard_map.79.refs_1_
  33.6 2.7 collective-permute-start.9
  36.3 5.7 collective-permute-done.2
  42.6 14.2 %collective-permute-done.4 = bf16[128,2048]{1,0:T(8,128)(2,1)} collective-permute-done((bf16[128,2048]{1,0:T(8,128)(2,1)}, bf16[128,2048]{1,0:T(8,128)(2,1)}, u32[]{:S(2)}, u32[]{:S(2)}) %collective-permute-start.4) | collective-permute-done | bytes 524320 | tf_op jit(solution)/shard_map/ppermute | solution.py:230
  56.8 1.5 collective-permute-start.5
  58.3 0.8 constant_dynamic-update-slice_fusion.3
  60.0 1.9 constant_dynamic-update-slice_fusion.1
  61.9 1.9 constant_dynamic-update-slice_fusion.refs_0_
  63.8 7.1 %shard_map.78 = f32[512,1024]{1,0:T(8,128)} custom-call(s32[6]{0:T(128)} %pad_add_fusion.where_ref, bf16[512,2048]{1,0:T(8,128)(2,1)} %constant_dynamic-update-slice_fusion.refs_0_, bf16[2048,1024]{1,0:T(8,128)(2,1)} %shard_map.77.refs_1_.refs_2_), custom_call_target="tpu_custom_call" | custom-call | tf_op jit(solution)/shard_map/pallas_call | solution.py:126
  70.9 7.2 %shard_map.80 = f32[512,1024]{1,0:T(8,128)} custom-call(s32[6]{0:T(128)} %pad_add_fusion.where_ref, bf16[512,2048]{1,0:T(8,128)(2,1)} %constant_dynamic-update-slice_fusion.refs_0_, bf16[2048,1024]{1,0:T(8,128)(2,1)} %shard_map.79.refs_1_), custom_call_target="tpu_custom_call" | custom-call | tf_op jit(solution)/shard_map/pallas_call | solution.py:126
  78.0 2.8 collective-permute-start.14
  80.8 1.7 convert_element_type.92
  82.5 2.4 collective-permute-start.6
  85.0 19.4 %collective-permute-done.6 = bf16[512,1024]{1,0:T(8,128)(2,1)S(1)} collective-permute-done((bf16[512,1024]{1,0:T(8,128)(2,1)S(1)}, bf16[512,1024]{1,0:T(8,128)(2,1)S(1)}, u32[]{:S(2)}, u32[]{:S(2)}) %collective-permute-start.6) | collective-permute-done | bytes 1048608 | tf_op jit(solution)/shard_map/ppermute | solution.py:230
  105.1 2.4 collective-permute-start.7
  107.5 18.8 %collective-permute-done.7 = bf16[2,128,1024]{2,1,0:T(8,128)(2,1)S(1)} collective-permute-done((bf16[2,128,1024]{2,1,0:T(8,128)(2,1)S(1)}, bf16[2,128,1024]{2,1,0:T(8,128)(2,1)S(1)}, u32[]{:S(2)}, u32[]{:S(2)}) %collective-permute-start.7) | collective-permute-done | bytes 524320 | tf_op jit(solution)/shard_map/ppermute | solution.py:230
  127.3 1.9 collective-permute-start.8
  129.2 1.3 copy.18.held_ref
  132.6 9.0 %collective-permute-done.8 = bf16[1,128,1024]{2,1,0:T(8,128)(2,1)S(1)} collective-permute-done((bf16[1,128,1024]{2,1,0:T(8,128)(2,1)}, bf16[1,128,1024]{2,1,0:T(8,128)(2,1)S(1)}, u32[]{:S(2)}, u32[]{:S(2)}) %collective-permute-start.8) | collective-permute-done | bytes 262176 | tf_op jit(solution)/shard_map/ppermute | solution.py:230
  141.6 0.9 fusion.21.f_ref
  142.4 12.8 %shard_map.81.held_ref = bf16[128,8192]{1,0:T(8,128)(2,1)} custom-call(s32[1]{0:T(128)} %bitcast.12.active_ref, f32[8,16,256]{2,1,0:T(8,128)} %and_select_fusion.bias_ref, bf16[128,8192]{1,0:T(8,128)(2,1)} %bitcast.58, bf16[128,8192]{1,0:T(8,128)(2,1)} %bitcast.52, bf16[128,16,2048]{2,1,0:T(8,128)(2,1)} %bitcast.47, ...), custom_call_target="tpu_custom_call", output_to_operand_aliasing={{}: (6, {})} | custom-call | tf_op jit(solution)/shard_map/pallas_call | solution.py:191
  155.3 3.4 collective-permute-start.11
  158.7 1.4 collective-permute-start.10
  160.2 2.6 collective-permute-start.13
  162.8 2.6 collective-permute-start.16
  165.4 2.7 collective-permute-start.15
  168.1 15.5 %collective-permute-done.11 = bf16[128,8192]{1,0:T(8,128)(2,1)} collective-permute-done((bf16[128,8192]{1,0:T(8,128)(2,1)}, bf16[128,8192]{1,0:T(8,128)(2,1)}, u32[]{:S(2)}, u32[]{:S(2)}) %collective-permute-start.11) | collective-permute-done | bytes 2097184 | tf_op jit(solution)/shard_map/ppermute | solution.py:230
  183.5 2.7 collective-permute-start.12
  186.2 3.4 collective-permute-start.18
  190.9 2.1 fusion.3
  193.0 2.7 collective-permute-start.19
  195.7 4.7 fusion.8
  201.0 6.9 %shard_map.82 = (f32[128,1024]{1,0:T(8,128)}, bf16[16384,1024]{1,0:T(8,128)(2,1)}) custom-call(s32[18]{0:T(128)} %stack.161.where_ref, bf16[128,8192]{1,0:T(8,128)(2,1)} %get-tuple-element.140.refs_0_, bf16[128,8192]{1,0:T(8,128)(2,1)} %get-tuple-element.141.refs_1_.refs_0_, bf16[2048,1024]{1,0:T(8,128)(2,1)} %shard_map.77.refs_1_.refs_2_, ...), custom_call_target="tpu_custom_call" | custom-call | tf_op jit(solution)/shard_map/pallas_call | solution.py:126
  207.9 1.5 collective-permute-start.17
  209.4 27.5 %collective-permute-done.18 = bf16[2048,1024]{1,0:T(8,128)(2,1)} collective-permute-done((bf16[2048,1024]{1,0:T(8,128)(2,1)}, bf16[2048,1024]{1,0:T(8,128)(2,1)}, u32[]{:S(2)}, u32[]{:S(2)}) %collective-permute-start.18) | collective-permute-done | bytes 4194336 | tf_op jit(solution)/shard_map/ppermute | solution.py:230
  236.9 7.7 %pad_maximum_fusion.refs_2_ = bf16[4096,1024]{1,0:T(8,128)(2,1)} fusion(bf16[2048,1024]{1,0:T(8,128)(2,1)} %collective-permute-done.18, bf16[2048,1024]{1,0:T(8,128)(2,1)} %shard_map.77.refs_1_.refs_2_), kind=kLoop, calls=%fused_computation | loop fusion | flops 16777216 | bytes 16777216 | tf_op jit(solution)/shard_map/concatenate | solution.py:344
  244.6 74.2 %collective-permute-done.17 = bf16[16,128]{1,0:T(8,128)(2,1)S(1)} collective-permute-done((bf16[16,128]{1,0:T(8,128)(2,1)S(1)}, bf16[16,128]{1,0:T(8,128)(2,1)S(1)}, u32[]{:S(2)}, u32[]{:S(2)}) %collective-permute-start.17) | collective-permute-done | bytes 4128 | tf_op jit(solution)/shard_map/ppermute | solution.py:230
  318.8 4.6 collective-permute-start.23
  323.4 2.2 collective-permute-start.22
  326.3 5.0 shard_map.83
  331.3 2.9 shard_map.84.held_ref
  335.0 2.0 collective-permute-start.21
  338.2 2.1 fusion.12
  340.3 4.8 fusion.14
  345.1 7.1 %shard_map.85.f_ref = f32[128,1024]{1,0:T(8,128)} custom-call(s32[20]{0:T(128)} %stack.162.where_ref, bf16[128,8192]{1,0:T(8,128)(2,1)} %get-tuple-element.139.refs_0_, bf16[128,8192]{1,0:T(8,128)(2,1)} %get-tuple-element.138.refs_1_, bf16[2048,1024]{1,0:T(8,128)(2,1)} %shard_map.77.refs_1_.refs_2_, bf16[2048,1024]{1,0:T(8,128)(2,1)} %collective-permute-done.refs_3_, ...), custom_call_target="tpu_custom_call" | custom-call | tf_op jit(solution)/shard_map/pallas_call | solution.py:126
  352.1 2.9 shard_map.86.held_ref
  355.1 150.3 %collective-permute-done.23.refs_4_ = bf16[4096,1024]{1,0:T(8,128)(2,1)} collective-permute-done((bf16[4096,1024]{1,0:T(8,128)(2,1)}, bf16[4096,1024]{1,0:T(8,128)(2,1)}, u32[]{:S(2)}, u32[]{:S(2)}) %collective-permute-start.23) | collective-permute-done | bytes 8388640 | tf_op jit(solution)/shard_map/ppermute | solution.py:230
  505.3 10.0 %collective-permute-done.22.refs_3_ = bf16[4096,1024]{1,0:T(8,128)(2,1)} collective-permute-done((bf16[4096,1024]{1,0:T(8,128)(2,1)}, bf16[4096,1024]{1,0:T(8,128)(2,1)}, u32[]{:S(2)}, u32[]{:S(2)}) %collective-permute-start.22) | collective-permute-done | bytes 8388640 | tf_op jit(solution)/shard_map/ppermute | solution.py:230
  515.4 2.3 collective-permute-start.26
  518.5 2.1 collective-permute-start.25
  524.4 2.1 fusion.18
  526.5 4.7 fusion.20
  531.2 20.7 %shard_map.87 = (f32[128,1024]{1,0:T(8,128)}, bf16[16384,1024]{1,0:T(8,128)(2,1)}) custom-call(s32[16]{0:T(128)} %stack.166.where_ref, bf16[128,8192]{1,0:T(8,128)(2,1)} %get-tuple-element.137.refs_0_, bf16[128,8192]{1,0:T(8,128)(2,1)} %get-tuple-element.136.refs_1_, bf16[4096,1024]{1,0:T(8,128)(2,1)} %pad_maximum_fusion.refs_2_, ...), custom_call_target="tpu_custom_call", output_to_operand_aliasing={{1}: (6, {})} | custom-call | tf_op jit(solution)/shard_map/pallas_call | solution.py:126
  551.9 59.1 %collective-permute-done.26.refs_2_ = bf16[4096,1024]{1,0:T(8,128)(2,1)} collective-permute-done((bf16[4096,1024]{1,0:T(8,128)(2,1)}, bf16[4096,1024]{1,0:T(8,128)(2,1)}, u32[]{:S(2)}, u32[]{:S(2)}) %collective-permute-start.26) | collective-permute-done | bytes 8388640 | tf_op jit(solution)/shard_map/ppermute | solution.py:230
  611.0 10.7 %shard_map.88 = (f32[128,1024]{1,0:T(8,128)}, bf16[16384,1024]{1,0:T(8,128)(2,1)}) custom-call(s32[8]{0:T(128)} %stack.66.where_ref, bf16[128,8192]{1,0:T(8,128)(2,1)} %get-tuple-element.137.refs_0_, bf16[128,8192]{1,0:T(8,128)(2,1)} %get-tuple-element.136.refs_1_, ...), custom_call_target="tpu_custom_call", output_to_operand_aliasing={{1}: (5, {})} | custom-call | tf_op jit(solution)/shard_map/pallas_call | solution.py:126
  621.8 2.9 shard_map.89
  (66 shorter events, 14.6 us)
Async XLA Ops:
  0.6 5.4 copy-start
  0.7 10.8 %copy-start.5 = (bf16[1,8192]{1,0:T(2,128)(2,1)S(1)}, bf16[1,8192]{1,0:T(2,128)(2,1)}, u32[]{:S(2)}) copy-start(bf16[1,8192]{1,0:T(2,128)(2,1)} %param.7) | copy-start | bytes 49156
  6.5 6.4 %collective-permute-start.1 = (f32[128]{0:T(128)S(1)}, f32[128]{0:T(128)S(1)}, u32[]{:S(2)}, u32[]{:S(2)}) collective-permute-start(f32[128]{0:T(128)S(1)} %fusion), channel_id=1, source_target_pairs={{0,4},{4,0},{1,5},{5,1},{2,6},{6,2},{3,7},{7,3}} | collective-permute-start | bytes 1544 | tf_op jit(solution)/shard_map/ppermute | solution.py:230
  14.7 27.3 %collective-permute-start.2 = (bf16[128,2048]{1,0:T(8,128)(2,1)}, bf16[128,2048]{1,0:T(8,128)(2,1)S(1)}, u32[]{:S(2)}, u32[]{:S(2)}) collective-permute-start(bf16[128,2048]{1,0:T(8,128)(2,1)} %get-tuple-element.68), channel_id=1, source_target_pairs={{0,1},{1,0},{2,3},{3,2},{4,5},{5,4},{6,7},{7,6}} | collective-permute-start | bytes 1572872 | tf_op jit(solution)/shard_map/ppermute | solution.py:230
  18.7 23.9 %collective-permute-start.3 = (bf16[128,2048]{1,0:T(8,128)(2,1)}, bf16[128,2048]{1,0:T(8,128)(2,1)}, u32[]{:S(2)}, u32[]{:S(2)}) collective-permute-start(bf16[128,2048]{1,0:T(8,128)(2,1)} %get-tuple-element.69), channel_id=1, source_target_pairs={{0,2},{1,3},{2,0},{3,1},{4,6},{5,7},{6,4},{7,5}} | collective-permute-start | bytes 1572872 | tf_op jit(solution)/shard_map/ppermute | solution.py:230
  23.2 33.6 %collective-permute-start.4 = (bf16[128,2048]{1,0:T(8,128)(2,1)}, bf16[128,2048]{1,0:T(8,128)(2,1)}, u32[]{:S(2)}, u32[]{:S(2)}) collective-permute-start(bf16[128,2048]{1,0:T(8,128)(2,1)} %get-tuple-element.70), channel_id=1, source_target_pairs={{0,3},{1,2},{2,1},{3,0},{4,7},{5,6},{6,5},{7,4}} | collective-permute-start | bytes 1572872 | tf_op jit(solution)/shard_map/ppermute | solution.py:230
  25.1 130.2 %collective-permute-start = (bf16[2048,1024]{1,0:T(8,128)(2,1)}, bf16[2048,1024]{1,0:T(8,128)(2,1)}, u32[]{:S(2)}, u32[]{:S(2)}) collective-permute-start(bf16[2048,1024]{1,0:T(8,128)(2,1)} %shard_map.77.refs_1_.refs_2_), channel_id=1, source_target_pairs={{8,9},{9,8},{10,11},{11,10},{16,17},{17,16},{18,19},{19,18},{12,13... | collective-permute-start | bytes 12582920 | tf_op jit(solution)/shard_map/ppermute | solution.py:230
  33.6 121.7 %collective-permute-start.9 = (bf16[2048,1024]{1,0:T(8,128)(2,1)}, bf16[2048,1024]{1,0:T(8,128)(2,1)}, u32[]{:S(2)}, u32[]{:S(2)}) collective-permute-start(bf16[2048,1024]{1,0:T(8,128)(2,1)} %shard_map.77.refs_1_.refs_2_), channel_id=1, source_target_pairs={{8,10},{9,11},{10,8},{11,9},{16,18},{17,19},{18,16},{19,17},{12,14... | collective-permute-start | bytes 12582920 | tf_op jit(solution)/shard_map/ppermute | solution.py:230
  56.8 21.2 %collective-permute-start.5 = (bf16[1,8192]{1,0:T(2,128)(2,1)S(1)}, bf16[1,8192]{1,0:T(2,128)(2,1)S(1)}, u32[]{:S(2)}, u32[]{:S(2)}) collective-permute-start(bf16[1,8192]{1,0:T(2,128)(2,1)S(1)} %copy-done.5), channel_id=1, source_target_pairs={{0,4},{4,0},{8,12},{12,8},{16,20},{20,16},{24,28},{28,24},{1,5},{5... | collective-permute-start | bytes 49160 | tf_op jit(solution)/shard_map/ppermute | solution.py:230
  78.0 26.4 %copy-start.4 = (f32[512,1024]{1,0:T(8,128)S(1)}, f32[512,1024]{1,0:T(8,128)}, u32[]{:S(2)}) copy-start(f32[512,1024]{1,0:T(8,128)} %shard_map.78) | copy-start | bytes 6291460
  78.0 84.8 %collective-permute-start.14 = (bf16[2048,1024]{1,0:T(8,128)(2,1)}, bf16[2048,1024]{1,0:T(8,128)(2,1)}, u32[]{:S(2)}, u32[]{:S(2)}) collective-permute-start(bf16[2048,1024]{1,0:T(8,128)(2,1)} %shard_map.79.refs_1_), channel_id=1, source_target_pairs={{8,12},{12,8},{16,20},{20,16},{9,13},{13,9},{17,21},{21,17},{10,14... | collective-permute-start | bytes 12582920 | tf_op jit(solution)/shard_map/ppermute | solution.py:230
  82.5 21.9 %collective-permute-start.6 = (bf16[512,1024]{1,0:T(8,128)(2,1)S(1)}, bf16[512,1024]{1,0:T(8,128)(2,1)S(1)}, u32[]{:S(2)}, u32[]{:S(2)}) collective-permute-start(bf16[512,1024]{1,0:T(8,128)(2,1)S(1)} %convert_element_type.92), channel_id=1, source_target_pairs={{0,4},{4,0},{1,5},{5,1},{2,6},{6,2},{3,7},{7,3}} | collective-permute-start | bytes 3145736 | tf_op jit(solution)/shard_map/ppermute | solution.py:230
  105.1 21.3 %collective-permute-start.7 = (bf16[2,128,1024]{2,1,0:T(8,128)(2,1)S(1)}, bf16[2,128,1024]{2,1,0:T(8,128)(2,1)S(1)}, u32[]{:S(2)}, u32[]{:S(2)}) collective-permute-start(bf16[2,128,1024]{2,1,0:T(8,128)(2,1)S(1)} %pad_maximum_fusion.1), channel_id=1, source_target_pairs={{0,1},{1,0},{2,3},{3,2},{4,5},{5,4},{6,7},{7,6}} | collective-permute-start | bytes 1572872 | tf_op jit(solution)/shard_map/ppermute | solution.py:230
  107.5 23.6 %copy-start.6 = (s32[1,128]{1,0:T(1,128)S(1)}, s32[1,128]{1,0:T(1,128)}, u32[]{:S(2)}) copy-start(s32[1,128]{1,0:T(1,128)} %param.11) | copy-start | bytes 1540
  127.3 14.3 %collective-permute-start.8 = (bf16[1,128,1024]{2,1,0:T(8,128)(2,1)}, bf16[1,128,1024]{2,1,0:T(8,128)(2,1)S(1)}, u32[]{:S(2)}, u32[]{:S(2)}) collective-permute-start(bf16[1,128,1024]{2,1,0:T(8,128)(2,1)} %slice.65), channel_id=1, source_target_pairs={{0,2},{1,3},{2,0},{3,1},{4,6},{5,7},{6,4},{7,5}} | collective-permute-start | bytes 786440 | tf_op jit(solution)/shard_map/ppermute | solution.py:230
  155.3 28.2 %collective-permute-start.11 = (bf16[128,8192]{1,0:T(8,128)(2,1)}, bf16[128,8192]{1,0:T(8,128)(2,1)}, u32[]{:S(2)}, u32[]{:S(2)}) collective-permute-start(bf16[128,8192]{1,0:T(8,128)(2,1)} %shard_map.81.held_ref), channel_id=1, source_target_pairs={{0,4},{4,0},{1,5},{5,1},{2,6},{6,2},{3,7},{7,3}} | collective-permute-start | bytes 6291464 | tf_op jit(solution)/shard_map/ppermute | solution.py:230
  158.7 27.5 %collective-permute-start.10 = (bf16[128,8192]{1,0:T(8,128)(2,1)}, bf16[128,8192]{1,0:T(8,128)(2,1)S(1)}, u32[]{:S(2)}, u32[]{:S(2)}) collective-permute-start(bf16[128,8192]{1,0:T(8,128)(2,1)} %shard_map.81.held_ref), channel_id=1, source_target_pairs={{0,8},{4,12},{1,9},{5,13},{2,10},{6,14},{3,11},{7,15}} | collective-permute-start | bytes 6291464 | tf_op jit(solution)/shard_map/ppermute | solution.py:230
  160.2 32.8 %collective-permute-start.13 = (bf16[2048,1024]{1,0:T(8,128)(2,1)}, bf16[2048,1024]{1,0:T(8,128)(2,1)}, u32[]{:S(2)}, u32[]{:S(2)}) collective-permute-start(bf16[2048,1024]{1,0:T(8,128)(2,1)} %collective-permute-done.9.refs_4_), channel_id=1, source_target_pairs={{8,9},{9,8},{10,11},{11,10},{16,17},{17,16},{18,19},{19,18},{12,13... | collective-permute-start | bytes 12582920 | tf_op jit(solution)/shard_map/ppermute | solution.py:230
  162.8 30.2 %collective-permute-start.16 = (bf16[2048,1024]{1,0:T(8,128)(2,1)}, bf16[2048,1024]{1,0:T(8,128)(2,1)}, u32[]{:S(2)}, u32[]{:S(2)}) collective-permute-start(bf16[2048,1024]{1,0:T(8,128)(2,1)} %collective-permute-done.14.refs_6_), channel_id=1, source_target_pairs={{8,10},{9,11},{10,8},{11,9},{16,18},{17,19},{18,16},{19,17},{12,14... | collective-permute-start | bytes 12582920 | tf_op jit(solution)/shard_map/ppermute | solution.py:230
  165.4 27.7 %collective-permute-start.15 = (bf16[2048,1024]{1,0:T(8,128)(2,1)}, bf16[2048,1024]{1,0:T(8,128)(2,1)}, u32[]{:S(2)}, u32[]{:S(2)}) collective-permute-start(bf16[2048,1024]{1,0:T(8,128)(2,1)} %collective-permute-done.14.refs_6_), channel_id=1, source_target_pairs={{8,9},{9,8},{10,11},{11,10},{16,17},{17,16},{18,19},{19,18},{12,13... | collective-permute-start | bytes 12582920 | tf_op jit(solution)/shard_map/ppermute | solution.py:230
  183.5 7.4 %collective-permute-start.12 = (bf16[128,8192]{1,0:T(8,128)(2,1)}, bf16[128,8192]{1,0:T(8,128)(2,1)}, u32[]{:S(2)}, u32[]{:S(2)}) collective-permute-start(bf16[128,8192]{1,0:T(8,128)(2,1)} %collective-permute-done.11), channel_id=1, source_target_pairs={{0,8},{4,12},{1,9},{5,13},{2,10},{6,14},{3,11},{7,15}} | collective-permute-start | bytes 6291464 | tf_op jit(solution)/shard_map/ppermute | solution.py:230
  186.2 14.1 %copy-start.1 = (bf16[128,8192]{1,0:T(8,128)(2,1)}, bf16[128,8192]{1,0:T(8,128)(2,1)S(1)}, u32[]{:S(2)}) copy-start(bf16[128,8192]{1,0:T(8,128)(2,1)S(1)} %collective-permute-done.10.x_ref) | copy-start | bytes 6291460
  186.2 50.7 %collective-permute-start.18 = (bf16[2048,1024]{1,0:T(8,128)(2,1)}, bf16[2048,1024]{1,0:T(8,128)(2,1)}, u32[]{:S(2)}, u32[]{:S(2)}) collective-permute-start(bf16[2048,1024]{1,0:T(8,128)(2,1)} %shard_map.79.refs_1_), channel_id=1, source_target_pairs={{0,4},{4,0},{24,28},{28,24},{1,5},{5,1},{25,29},{29,25},{2,6},{6,2... | collective-permute-start | bytes 12582920 | tf_op jit(solution)/shard_map/ppermute | solution.py:230
  193.0 133.2 %collective-permute-start.19 = (bf16[2048,1024]{1,0:T(8,128)(2,1)}, bf16[2048,1024]{1,0:T(8,128)(2,1)}, u32[]{:S(2)}, u32[]{:S(2)}) collective-permute-start(bf16[2048,1024]{1,0:T(8,128)(2,1)} %collective-permute-done.16.refs_8_), channel_id=1, source_target_pairs={{8,9},{9,8},{10,11},{11,10},{16,17},{17,16},{18,19},{19,18},{12,13... | collective-permute-start | bytes 12582920 | tf_op jit(solution)/shard_map/ppermute | solution.py:230
  207.9 110.9 %collective-permute-start.17 = (bf16[16,128]{1,0:T(8,128)(2,1)S(1)}, bf16[16,128]{1,0:T(8,128)(2,1)S(1)}, u32[]{:S(2)}, u32[]{:S(2)}) collective-permute-start(bf16[16,128]{1,0:T(8,128)(2,1)S(1)} %slice.49), channel_id=1, source_target_pairs={{8,0},{9,1},{10,2},{11,3},{16,24},{17,25},{18,26},{19,27},{12,4},{... | collective-permute-start | bytes 12296 | tf_op jit(solution)/shard_map/ppermute | solution.py:230
  318.8 186.6 %collective-permute-start.23 = (bf16[4096,1024]{1,0:T(8,128)(2,1)}, bf16[4096,1024]{1,0:T(8,128)(2,1)}, u32[]{:S(2)}, u32[]{:S(2)}) collective-permute-start(bf16[4096,1024]{1,0:T(8,128)(2,1)} %pad_maximum_fusion.refs_2_), channel_id=1, source_target_pairs={{0,2},{1,3},{2,0},{3,1},{24,26},{25,27},{26,24},{27,25},{4,6},{5,7... | collective-permute-start | bytes 25165832 | tf_op jit(solution)/shard_map/ppermute | solution.py:230
  323.4 192.0 %collective-permute-start.22 = (bf16[4096,1024]{1,0:T(8,128)(2,1)}, bf16[4096,1024]{1,0:T(8,128)(2,1)}, u32[]{:S(2)}, u32[]{:S(2)}) collective-permute-start(bf16[4096,1024]{1,0:T(8,128)(2,1)} %pad_maximum_fusion.refs_2_), channel_id=1, source_target_pairs={{0,1},{1,0},{2,3},{3,2},{24,25},{25,24},{26,27},{27,26},{4,5},{5,4... | collective-permute-start | bytes 25165832 | tf_op jit(solution)/shard_map/ppermute | solution.py:230
  334.2 0.8 collective-permute-start.20
  335.0 10.1 %copy-start.3 = (bf16[128,8192]{1,0:T(8,128)(2,1)}, bf16[128,8192]{1,0:T(8,128)(2,1)S(1)}, u32[]{:S(2)}) copy-start(bf16[128,8192]{1,0:T(8,128)(2,1)S(1)} %collective-permute-done.20.x_ref) | copy-start | bytes 6291460
  335.0 3.2 collective-permute-start.21
  515.4 95.6 %collective-permute-start.26 = (bf16[4096,1024]{1,0:T(8,128)(2,1)}, bf16[4096,1024]{1,0:T(8,128)(2,1)}, u32[]{:S(2)}, u32[]{:S(2)}) collective-permute-start(bf16[4096,1024]{1,0:T(8,128)(2,1)} %collective-permute-done.23.refs_4_), channel_id=1, source_target_pairs={{0,1},{1,0},{2,3},{3,2},{24,25},{25,24},{26,27},{27,26},{4,5},{5,4... | collective-permute-start | bytes 25165832 | tf_op jit(solution)/shard_map/ppermute | solution.py:230
  517.7 0.8 collective-permute-start.24
  518.5 12.7 %copy-start.2 = (bf16[128,8192]{1,0:T(8,128)(2,1)}, bf16[128,8192]{1,0:T(8,128)(2,1)S(1)}, u32[]{:S(2)}) copy-start(bf16[128,8192]{1,0:T(8,128)(2,1)S(1)} %collective-permute-done.24.x_ref) | copy-start | bytes 6291460
  518.5 5.9 collective-permute-start.25

commit v7 on v6

--- a/solution.py
+++ b/solution.py
@@ -295,7 +295,7 @@
         squares = squares + over_tensor(squares, (0,), j)
     (normed,) = normed_of([hidden], lax.rsqrt(squares / D + epsilon), [norm_gain])
     first = [feature_block(normed, b) for b in range(dps)]
-    weight, first = together(weight, first)
+    weight, first, later = together(weight, first, first_kept[0])
     kept = first_kept + requantize(weight, [tensor ^ j for j in range(1, tensors)], own_width, served)
     first[1:] = [over_dp(first[b], (0,), flipped(b)) for b in range(1, dps)]
     first, gain = together(first, norm_gain)
@@ -306,7 +306,6 @@
         return received[0] if len(received) == 1 else jnp.concatenate(received, axis=0)
 
     own = {0: kept[0], 1: over_dp(kept[0], early, flipped(1))}
-    later, kept[1:] = together(kept[0], kept[1:])
     own[2] = over_dp(later, early, flipped(2))
 
     lhs = [jnp.concatenate(first, axis=0)]

time: 626 us -> 624 us (level)
  transfers between devices with their start and end apart: 27 -> 27, of which waited for: 13 -> 12; matrix products, arithmetic and copies ran while one was open for 8% -> 8% of each run, Pallas kernels for 12% -> 12%
where the time goes in v7:
time: 624 us; the launch traced here: 622 us
  waiting for transfers between devices  403 us (65%)
  Pallas kernels  96.8 us (16%)
  starting transfers between devices  70 us (11%)
  other arithmetic  36.2 us (6%)
  local copies, waits for them, and re-layouts  14 us (2%)
    ppermute x27, waiting for transfers between devices, over(): return lax.ppermute(value, ('section', axis), pairs)  403 us
    ppermute x27, starting transfers between devices, over(): return lax.ppermute(value, ('section', axis), pairs)  70 us
    pallas_call x7, Pallas kernels, project(): pl.pallas_call(functools.partial(project_kernel, layout, len(lhs), bool(a...  64.6 us
    pallas_call x4, Pallas kernels, attend(): pl.pallas_call(functools.partial(attend_kernel, share), out_shape=jax.Sha...  21.6 us
    convert_element_type x4, other arithmetic, normed_of(): (part.astype(jnp.float32) * inverse[:, None] * gain.astype(jnp.float32))....  14.8 us
  transfers between devices with their start and end apart: 27, of which 12 were waited for; matrix products, arithmetic and copies ran while one was open for 8% of the time, Pallas kernels for 12%

profile of v7, /device:TPU:0, one launch (start us, length us, event | category | flops | bytes accessed | tf_op | source)
XLA Modules:
  0.0 622.2 jit_solution(8667566084626481853)
XLA Ops:
  0.7 5.4 shard_map.77.refs_1_.refs_2_
  6.5 4.9 collective-permute-start.1
  11.5 1.4 collective-permute-done.1
  13.5 1.2 constant_dynamic-slice_fusion
  14.7 4.0 collective-permute-start.2
  18.7 4.5 collective-permute-start.3
  23.2 1.9 collective-permute-start.4
  25.1 2.6 collective-permute-start
  28.4 2.7 collective-permute-start.9
  31.1 5.2 shard_map.79.refs_1_
  36.3 12.9 %collective-permute-done.2 = bf16[128,2048]{1,0:T(8,128)(2,1)S(1)} collective-permute-done((bf16[128,2048]{1,0:T(8,128)(2,1)}, bf16[128,2048]{1,0:T(8,128)(2,1)S(1)}, u32[]{:S(2)}, u32[]{:S(2)}) %collective-permute-start.2) | collective-permute-done | bytes 524320 | tf_op jit(solution)/shard_map/ppermute | solution.py:230
  49.2 7.6 %collective-permute-done.4 = bf16[128,2048]{1,0:T(8,128)(2,1)} collective-permute-done((bf16[128,2048]{1,0:T(8,128)(2,1)}, bf16[128,2048]{1,0:T(8,128)(2,1)}, u32[]{:S(2)}, u32[]{:S(2)}) %collective-permute-start.4) | collective-permute-done | bytes 524320 | tf_op jit(solution)/shard_map/ppermute | solution.py:230
  56.8 1.5 collective-permute-start.5
  58.3 0.8 constant_dynamic-update-slice_fusion.3
  59.9 1.9 constant_dynamic-update-slice_fusion.1
  61.8 1.9 constant_dynamic-update-slice_fusion.refs_0_
  63.7 7.1 %shard_map.78 = f32[512,1024]{1,0:T(8,128)} custom-call(s32[6]{0:T(128)} %pad_add_fusion.where_ref, bf16[512,2048]{1,0:T(8,128)(2,1)} %constant_dynamic-update-slice_fusion.refs_0_, bf16[2048,1024]{1,0:T(8,128)(2,1)} %shard_map.77.refs_1_.refs_2_), custom_call_target="tpu_custom_call" | custom-call | tf_op jit(solution)/shard_map/pallas_call | solution.py:126
  70.8 7.2 %shard_map.80 = f32[512,1024]{1,0:T(8,128)} custom-call(s32[6]{0:T(128)} %pad_add_fusion.where_ref, bf16[512,2048]{1,0:T(8,128)(2,1)} %constant_dynamic-update-slice_fusion.refs_0_, bf16[2048,1024]{1,0:T(8,128)(2,1)} %shard_map.79.refs_1_), custom_call_target="tpu_custom_call" | custom-call | tf_op jit(solution)/shard_map/pallas_call | solution.py:126
  78.0 2.8 collective-permute-start.14
  80.7 1.7 convert_element_type.92
  82.5 2.4 collective-permute-start.6
  84.9 19.5 %collective-permute-done.6 = bf16[512,1024]{1,0:T(8,128)(2,1)S(1)} collective-permute-done((bf16[512,1024]{1,0:T(8,128)(2,1)S(1)}, bf16[512,1024]{1,0:T(8,128)(2,1)S(1)}, u32[]{:S(2)}, u32[]{:S(2)}) %collective-permute-start.6) | collective-permute-done | bytes 1048608 | tf_op jit(solution)/shard_map/ppermute | solution.py:230
  105.1 2.4 collective-permute-start.7
  107.5 19.8 %collective-permute-done.7 = bf16[2,128,1024]{2,1,0:T(8,128)(2,1)S(1)} collective-permute-done((bf16[2,128,1024]{2,1,0:T(8,128)(2,1)S(1)}, bf16[2,128,1024]{2,1,0:T(8,128)(2,1)S(1)}, u32[]{:S(2)}, u32[]{:S(2)}) %collective-permute-start.7) | collective-permute-done | bytes 524320 | tf_op jit(solution)/shard_map/ppermute | solution.py:230
  128.3 1.9 collective-permute-start.8
  130.2 1.3 copy.18.held_ref
  133.6 7.9 %collective-permute-done.8 = bf16[1,128,1024]{2,1,0:T(8,128)(2,1)S(1)} collective-permute-done((bf16[1,128,1024]{2,1,0:T(8,128)(2,1)}, bf16[1,128,1024]{2,1,0:T(8,128)(2,1)S(1)}, u32[]{:S(2)}, u32[]{:S(2)}) %collective-permute-start.8) | collective-permute-done | bytes 262176 | tf_op jit(solution)/shard_map/ppermute | solution.py:230
  141.5 0.9 fusion.21.f_ref
  142.4 12.8 %shard_map.81.held_ref = bf16[128,8192]{1,0:T(8,128)(2,1)} custom-call(s32[1]{0:T(128)} %bitcast.12.active_ref, f32[8,16,256]{2,1,0:T(8,128)} %and_select_fusion.bias_ref, bf16[128,8192]{1,0:T(8,128)(2,1)} %bitcast.58, bf16[128,8192]{1,0:T(8,128)(2,1)} %bitcast.52, bf16[128,16,2048]{2,1,0:T(8,128)(2,1)} %bitcast.47, ...), custom_call_target="tpu_custom_call", output_to_operand_aliasing={{}: (6, {})} | custom-call | tf_op jit(solution)/shard_map/pallas_call | solution.py:191
  155.2 3.4 collective-permute-start.11
  158.6 1.4 collective-permute-start.10
  160.1 2.6 collective-permute-start.13
  162.7 2.6 collective-permute-start.16
  165.3 2.7 collective-permute-start.15
  168.0 15.5 %collective-permute-done.11 = bf16[128,8192]{1,0:T(8,128)(2,1)} collective-permute-done((bf16[128,8192]{1,0:T(8,128)(2,1)}, bf16[128,8192]{1,0:T(8,128)(2,1)}, u32[]{:S(2)}, u32[]{:S(2)}) %collective-permute-start.11) | collective-permute-done | bytes 2097184 | tf_op jit(solution)/shard_map/ppermute | solution.py:230
  183.5 2.7 collective-permute-start.12
  186.1 3.4 collective-permute-start.18
  190.8 2.1 fusion.3
  192.9 2.7 collective-permute-start.19
  195.6 4.7 fusion.8
  200.9 6.9 %shard_map.82 = (f32[128,1024]{1,0:T(8,128)}, bf16[16384,1024]{1,0:T(8,128)(2,1)}) custom-call(s32[18]{0:T(128)} %stack.161.where_ref, bf16[128,8192]{1,0:T(8,128)(2,1)} %get-tuple-element.138.refs_0_, bf16[128,8192]{1,0:T(8,128)(2,1)} %get-tuple-element.139.refs_1_.refs_0_, bf16[2048,1024]{1,0:T(8,128)(2,1)} %shard_map.77.refs_1_.refs_2_, ...), custom_call_target="tpu_custom_call" | custom-call | tf_op jit(solution)/shard_map/pallas_call | solution.py:126
  207.8 1.5 collective-permute-start.17
  209.3 27.6 %collective-permute-done.18 = bf16[2048,1024]{1,0:T(8,128)(2,1)} collective-permute-done((bf16[2048,1024]{1,0:T(8,128)(2,1)}, bf16[2048,1024]{1,0:T(8,128)(2,1)}, u32[]{:S(2)}, u32[]{:S(2)}) %collective-permute-start.18) | collective-permute-done | bytes 4194336 | tf_op jit(solution)/shard_map/ppermute | solution.py:230
  236.8 7.7 %pad_maximum_fusion.refs_2_ = bf16[4096,1024]{1,0:T(8,128)(2,1)} fusion(bf16[2048,1024]{1,0:T(8,128)(2,1)} %collective-permute-done.18, bf16[2048,1024]{1,0:T(8,128)(2,1)} %shard_map.77.refs_1_.refs_2_), kind=kLoop, calls=%fused_computation | loop fusion | flops 16777216 | bytes 16777216 | tf_op jit(solution)/shard_map/concatenate | solution.py:343
  244.5 72.1 %collective-permute-done.17 = bf16[16,128]{1,0:T(8,128)(2,1)S(1)} collective-permute-done((bf16[16,128]{1,0:T(8,128)(2,1)S(1)}, bf16[16,128]{1,0:T(8,128)(2,1)S(1)}, u32[]{:S(2)}, u32[]{:S(2)}) %collective-permute-start.17) | collective-permute-done | bytes 4128 | tf_op jit(solution)/shard_map/ppermute | solution.py:230
  316.7 4.9 collective-permute-start.23
  321.6 2.2 collective-permute-start.22
  324.5 5.0 shard_map.83
  329.5 2.9 shard_map.84.held_ref
  333.2 2.0 collective-permute-start.21
  336.4 2.1 fusion.12
  338.5 4.8 fusion.14
  343.3 7.1 %shard_map.85.f_ref = f32[128,1024]{1,0:T(8,128)} custom-call(s32[20]{0:T(128)} %stack.162.where_ref, bf16[128,8192]{1,0:T(8,128)(2,1)} %get-tuple-element.137.refs_0_, bf16[128,8192]{1,0:T(8,128)(2,1)} %get-tuple-element.136.refs_1_, bf16[2048,1024]{1,0:T(8,128)(2,1)} %shard_map.77.refs_1_.refs_2_, bf16[2048,1024]{1,0:T(8,128)(2,1)} %collective-permute-done.refs_3_, ...), custom_call_target="tpu_custom_call" | custom-call | tf_op jit(solution)/shard_map/pallas_call | solution.py:126
  350.4 2.9 shard_map.86.held_ref
  353.3 150.0 %collective-permute-done.23.refs_4_ = bf16[4096,1024]{1,0:T(8,128)(2,1)} collective-permute-done((bf16[4096,1024]{1,0:T(8,128)(2,1)}, bf16[4096,1024]{1,0:T(8,128)(2,1)}, u32[]{:S(2)}, u32[]{:S(2)}) %collective-permute-start.23) | collective-permute-done | bytes 8388640 | tf_op jit(solution)/shard_map/ppermute | solution.py:230
  503.3 9.6 %collective-permute-done.22.refs_3_ = bf16[4096,1024]{1,0:T(8,128)(2,1)} collective-permute-done((bf16[4096,1024]{1,0:T(8,128)(2,1)}, bf16[4096,1024]{1,0:T(8,128)(2,1)}, u32[]{:S(2)}, u32[]{:S(2)}) %collective-permute-start.22) | collective-permute-done | bytes 8388640 | tf_op jit(solution)/shard_map/ppermute | solution.py:230
  512.9 2.6 collective-permute-start.26
  516.4 2.1 collective-permute-start.25
  522.3 2.1 fusion.18
  524.4 4.7 fusion.20
  529.1 20.7 %shard_map.87 = (f32[128,1024]{1,0:T(8,128)}, bf16[16384,1024]{1,0:T(8,128)(2,1)}) custom-call(s32[16]{0:T(128)} %stack.166.where_ref, bf16[128,8192]{1,0:T(8,128)(2,1)} %get-tuple-element.135.refs_0_, bf16[128,8192]{1,0:T(8,128)(2,1)} %get-tuple-element.134.refs_1_, bf16[4096,1024]{1,0:T(8,128)(2,1)} %pad_maximum_fusion.refs_2_, ...), custom_call_target="tpu_custom_call", output_to_operand_aliasing={{1}: (6, {})} | custom-call | tf_op jit(solution)/shard_map/pallas_call | solution.py:126
  549.8 58.8 %collective-permute-done.26.refs_2_ = bf16[4096,1024]{1,0:T(8,128)(2,1)} collective-permute-done((bf16[4096,1024]{1,0:T(8,128)(2,1)}, bf16[4096,1024]{1,0:T(8,128)(2,1)}, u32[]{:S(2)}, u32[]{:S(2)}) %collective-permute-start.26) | collective-permute-done | bytes 8388640 | tf_op jit(solution)/shard_map/ppermute | solution.py:230
  608.6 10.7 %shard_map.88 = (f32[128,1024]{1,0:T(8,128)}, bf16[16384,1024]{1,0:T(8,128)(2,1)}) custom-call(s32[8]{0:T(128)} %stack.66.where_ref, bf16[128,8192]{1,0:T(8,128)(2,1)} %get-tuple-element.135.refs_0_, bf16[128,8192]{1,0:T(8,128)(2,1)} %get-tuple-element.134.refs_1_, ...), custom_call_target="tpu_custom_call", output_to_operand_aliasing={{1}: (5, {})} | custom-call | tf_op jit(solution)/shard_map/pallas_call | solution.py:126
  619.3 2.9 shard_map.89
  (66 shorter events, 14.0 us)
Async XLA Ops:
  0.6 5.4 copy-start
  0.7 10.8 %copy-start.5 = (bf16[1,8192]{1,0:T(2,128)(2,1)S(1)}, bf16[1,8192]{1,0:T(2,128)(2,1)}, u32[]{:S(2)}) copy-start(bf16[1,8192]{1,0:T(2,128)(2,1)} %param.7) | copy-start | bytes 49156
  6.5 6.4 %collective-permute-start.1 = (f32[128]{0:T(128)S(1)}, f32[128]{0:T(128)S(1)}, u32[]{:S(2)}, u32[]{:S(2)}) collective-permute-start(f32[128]{0:T(128)S(1)} %fusion), channel_id=1, source_target_pairs={{0,4},{4,0},{1,5},{5,1},{2,6},{6,2},{3,7},{7,3}} | collective-permute-start | bytes 1544 | tf_op jit(solution)/shard_map/ppermute | solution.py:230
  14.7 34.5 %collective-permute-start.2 = (bf16[128,2048]{1,0:T(8,128)(2,1)}, bf16[128,2048]{1,0:T(8,128)(2,1)S(1)}, u32[]{:S(2)}, u32[]{:S(2)}) collective-permute-start(bf16[128,2048]{1,0:T(8,128)(2,1)} %get-tuple-element.67), channel_id=1, source_target_pairs={{0,1},{1,0},{2,3},{3,2},{4,5},{5,4},{6,7},{7,6}} | collective-permute-start | bytes 1572872 | tf_op jit(solution)/shard_map/ppermute | solution.py:230
  18.7 30.5 %collective-permute-start.3 = (bf16[128,2048]{1,0:T(8,128)(2,1)}, bf16[128,2048]{1,0:T(8,128)(2,1)}, u32[]{:S(2)}, u32[]{:S(2)}) collective-permute-start(bf16[128,2048]{1,0:T(8,128)(2,1)} %get-tuple-element.68), channel_id=1, source_target_pairs={{0,2},{1,3},{2,0},{3,1},{4,6},{5,7},{6,4},{7,5}} | collective-permute-start | bytes 1572872 | tf_op jit(solution)/shard_map/ppermute | solution.py:230
  23.2 33.6 %collective-permute-start.4 = (bf16[128,2048]{1,0:T(8,128)(2,1)}, bf16[128,2048]{1,0:T(8,128)(2,1)}, u32[]{:S(2)}, u32[]{:S(2)}) collective-permute-start(bf16[128,2048]{1,0:T(8,128)(2,1)} %get-tuple-element.69), channel_id=1, source_target_pairs={{0,3},{1,2},{2,1},{3,0},{4,7},{5,6},{6,5},{7,4}} | collective-permute-start | bytes 1572872 | tf_op jit(solution)/shard_map/ppermute | solution.py:230
  25.1 130.1 %collective-permute-start = (bf16[2048,1024]{1,0:T(8,128)(2,1)}, bf16[2048,1024]{1,0:T(8,128)(2,1)}, u32[]{:S(2)}, u32[]{:S(2)}) collective-permute-start(bf16[2048,1024]{1,0:T(8,128)(2,1)} %shard_map.77.refs_1_.refs_2_), channel_id=1, source_target_pairs={{8,9},{9,8},{10,11},{11,10},{16,17},{17,16},{18,19},{19,18},{12,13... | collective-permute-start | bytes 12582920 | tf_op jit(solution)/shard_map/ppermute | solution.py:230
  28.4 126.8 %collective-permute-start.9 = (bf16[2048,1024]{1,0:T(8,128)(2,1)}, bf16[2048,1024]{1,0:T(8,128)(2,1)}, u32[]{:S(2)}, u32[]{:S(2)}) collective-permute-start(bf16[2048,1024]{1,0:T(8,128)(2,1)} %shard_map.77.refs_1_.refs_2_), channel_id=1, source_target_pairs={{8,10},{9,11},{10,8},{11,9},{16,18},{17,19},{18,16},{19,17},{12,14... | collective-permute-start | bytes 12582920 | tf_op jit(solution)/shard_map/ppermute | solution.py:230
  56.8 21.2 %collective-permute-start.5 = (bf16[1,8192]{1,0:T(2,128)(2,1)S(1)}, bf16[1,8192]{1,0:T(2,128)(2,1)S(1)}, u32[]{:S(2)}, u32[]{:S(2)}) collective-permute-start(bf16[1,8192]{1,0:T(2,128)(2,1)S(1)} %copy-done.5), channel_id=1, source_target_pairs={{0,4},{4,0},{8,12},{12,8},{16,20},{20,16},{24,28},{28,24},{1,5},{5... | collective-permute-start | bytes 49160 | tf_op jit(solution)/shard_map/ppermute | solution.py:230
  78.0 26.4 %copy-start.4 = (f32[512,1024]{1,0:T(8,128)S(1)}, f32[512,1024]{1,0:T(8,128)}, u32[]{:S(2)}) copy-start(f32[512,1024]{1,0:T(8,128)} %shard_map.78) | copy-start | bytes 6291460
  78.0 84.7 %collective-permute-start.14 = (bf16[2048,1024]{1,0:T(8,128)(2,1)}, bf16[2048,1024]{1,0:T(8,128)(2,1)}, u32[]{:S(2)}, u32[]{:S(2)}) collective-permute-start(bf16[2048,1024]{1,0:T(8,128)(2,1)} %shard_map.79.refs_1_), channel_id=1, source_target_pairs={{8,12},{12,8},{16,20},{20,16},{9,13},{13,9},{17,21},{21,17},{10,14... | collective-permute-start | bytes 12582920 | tf_op jit(solution)/shard_map/ppermute | solution.py:230
  82.5 21.9 %collective-permute-start.6 = (bf16[512,1024]{1,0:T(8,128)(2,1)S(1)}, bf16[512,1024]{1,0:T(8,128)(2,1)S(1)}, u32[]{:S(2)}, u32[]{:S(2)}) collective-permute-start(bf16[512,1024]{1,0:T(8,128)(2,1)S(1)} %convert_element_type.92), channel_id=1, source_target_pairs={{0,4},{4,0},{1,5},{5,1},{2,6},{6,2},{3,7},{7,3}} | collective-permute-start | bytes 3145736 | tf_op jit(solution)/shard_map/ppermute | solution.py:230
  105.1 22.3 %collective-permute-start.7 = (bf16[2,128,1024]{2,1,0:T(8,128)(2,1)S(1)}, bf16[2,128,1024]{2,1,0:T(8,128)(2,1)S(1)}, u32[]{:S(2)}, u32[]{:S(2)}) collective-permute-start(bf16[2,128,1024]{2,1,0:T(8,128)(2,1)S(1)} %pad_maximum_fusion.1), channel_id=1, source_target_pairs={{0,1},{1,0},{2,3},{3,2},{4,5},{5,4},{6,7},{7,6}} | collective-permute-start | bytes 1572872 | tf_op jit(solution)/shard_map/ppermute | solution.py:230
  107.5 24.6 %copy-start.6 = (s32[1,128]{1,0:T(1,128)S(1)}, s32[1,128]{1,0:T(1,128)}, u32[]{:S(2)}) copy-start(s32[1,128]{1,0:T(1,128)} %param.11) | copy-start | bytes 1540
  128.3 13.2 %collective-permute-start.8 = (bf16[1,128,1024]{2,1,0:T(8,128)(2,1)}, bf16[1,128,1024]{2,1,0:T(8,128)(2,1)S(1)}, u32[]{:S(2)}, u32[]{:S(2)}) collective-permute-start(bf16[1,128,1024]{2,1,0:T(8,128)(2,1)} %slice.65), channel_id=1, source_target_pairs={{0,2},{1,3},{2,0},{3,1},{4,6},{5,7},{6,4},{7,5}} | collective-permute-start | bytes 786440 | tf_op jit(solution)/shard_map/ppermute | solution.py:230
  155.2 28.2 %collective-permute-start.11 = (bf16[128,8192]{1,0:T(8,128)(2,1)}, bf16[128,8192]{1,0:T(8,128)(2,1)}, u32[]{:S(2)}, u32[]{:S(2)}) collective-permute-start(bf16[128,8192]{1,0:T(8,128)(2,1)} %shard_map.81.held_ref), channel_id=1, source_target_pairs={{0,4},{4,0},{1,5},{5,1},{2,6},{6,2},{3,7},{7,3}} | collective-permute-start | bytes 6291464 | tf_op jit(solution)/shard_map/ppermute | solution.py:230
  158.6 27.5 %collective-permute-start.10 = (bf16[128,8192]{1,0:T(8,128)(2,1)}, bf16[128,8192]{1,0:T(8,128)(2,1)S(1)}, u32[]{:S(2)}, u32[]{:S(2)}) collective-permute-start(bf16[128,8192]{1,0:T(8,128)(2,1)} %shard_map.81.held_ref), channel_id=1, source_target_pairs={{0,8},{4,12},{1,9},{5,13},{2,10},{6,14},{3,11},{7,15}} | collective-permute-start | bytes 6291464 | tf_op jit(solution)/shard_map/ppermute | solution.py:230
  160.1 32.8 %collective-permute-start.13 = (bf16[2048,1024]{1,0:T(8,128)(2,1)}, bf16[2048,1024]{1,0:T(8,128)(2,1)}, u32[]{:S(2)}, u32[]{:S(2)}) collective-permute-start(bf16[2048,1024]{1,0:T(8,128)(2,1)} %collective-permute-done.9.refs_4_), channel_id=1, source_target_pairs={{8,9},{9,8},{10,11},{11,10},{16,17},{17,16},{18,19},{19,18},{12,13... | collective-permute-start | bytes 12582920 | tf_op jit(solution)/shard_map/ppermute | solution.py:230
  162.7 30.2 %collective-permute-start.16 = (bf16[2048,1024]{1,0:T(8,128)(2,1)}, bf16[2048,1024]{1,0:T(8,128)(2,1)}, u32[]{:S(2)}, u32[]{:S(2)}) collective-permute-start(bf16[2048,1024]{1,0:T(8,128)(2,1)} %collective-permute-done.14.refs_6_), channel_id=1, source_target_pairs={{8,10},{9,11},{10,8},{11,9},{16,18},{17,19},{18,16},{19,17},{12,14... | collective-permute-start | bytes 12582920 | tf_op jit(solution)/shard_map/ppermute | solution.py:230
  165.3 27.7 %collective-permute-start.15 = (bf16[2048,1024]{1,0:T(8,128)(2,1)}, bf16[2048,1024]{1,0:T(8,128)(2,1)}, u32[]{:S(2)}, u32[]{:S(2)}) collective-permute-start(bf16[2048,1024]{1,0:T(8,128)(2,1)} %collective-permute-done.14.refs_6_), channel_id=1, source_target_pairs={{8,9},{9,8},{10,11},{11,10},{16,17},{17,16},{18,19},{19,18},{12,13... | collective-permute-start | bytes 12582920 | tf_op jit(solution)/shard_map/ppermute | solution.py:230
  183.5 7.4 %collective-permute-start.12 = (bf16[128,8192]{1,0:T(8,128)(2,1)}, bf16[128,8192]{1,0:T(8,128)(2,1)}, u32[]{:S(2)}, u32[]{:S(2)}) collective-permute-start(bf16[128,8192]{1,0:T(8,128)(2,1)} %collective-permute-done.11), channel_id=1, source_target_pairs={{0,8},{4,12},{1,9},{5,13},{2,10},{6,14},{3,11},{7,15}} | collective-permute-start | bytes 6291464 | tf_op jit(solution)/shard_map/ppermute | solution.py:230
  186.1 14.1 %copy-start.1 = (bf16[128,8192]{1,0:T(8,128)(2,1)}, bf16[128,8192]{1,0:T(8,128)(2,1)S(1)}, u32[]{:S(2)}) copy-start(bf16[128,8192]{1,0:T(8,128)(2,1)S(1)} %collective-permute-done.10.x_ref) | copy-start | bytes 6291460
  186.1 50.7 %collective-permute-start.18 = (bf16[2048,1024]{1,0:T(8,128)(2,1)}, bf16[2048,1024]{1,0:T(8,128)(2,1)}, u32[]{:S(2)}, u32[]{:S(2)}) collective-permute-start(bf16[2048,1024]{1,0:T(8,128)(2,1)} %shard_map.79.refs_1_), channel_id=1, source_target_pairs={{0,4},{4,0},{24,28},{28,24},{1,5},{5,1},{25,29},{29,25},{2,6},{6,2... | collective-permute-start | bytes 12582920 | tf_op jit(solution)/shard_map/ppermute | solution.py:230
  192.9 131.6 %collective-permute-start.19 = (bf16[2048,1024]{1,0:T(8,128)(2,1)}, bf16[2048,1024]{1,0:T(8,128)(2,1)}, u32[]{:S(2)}, u32[]{:S(2)}) collective-permute-start(bf16[2048,1024]{1,0:T(8,128)(2,1)} %collective-permute-done.16.refs_8_), channel_id=1, source_target_pairs={{8,9},{9,8},{10,11},{11,10},{16,17},{17,16},{18,19},{19,18},{12,13... | collective-permute-start | bytes 12582920 | tf_op jit(solution)/shard_map/ppermute | solution.py:230
  207.8 108.8 %collective-permute-start.17 = (bf16[16,128]{1,0:T(8,128)(2,1)S(1)}, bf16[16,128]{1,0:T(8,128)(2,1)S(1)}, u32[]{:S(2)}, u32[]{:S(2)}) collective-permute-start(bf16[16,128]{1,0:T(8,128)(2,1)S(1)} %slice.49), channel_id=1, source_target_pairs={{8,0},{9,1},{10,2},{11,3},{16,24},{17,25},{18,26},{19,27},{12,4},{... | collective-permute-start | bytes 12296 | tf_op jit(solution)/shard_map/ppermute | solution.py:230
  316.7 186.7 %collective-permute-start.23 = (bf16[4096,1024]{1,0:T(8,128)(2,1)}, bf16[4096,1024]{1,0:T(8,128)(2,1)}, u32[]{:S(2)}, u32[]{:S(2)}) collective-permute-start(bf16[4096,1024]{1,0:T(8,128)(2,1)} %pad_maximum_fusion.refs_2_), channel_id=1, source_target_pairs={{0,2},{1,3},{2,0},{3,1},{24,26},{25,27},{26,24},{27,25},{4,6},{5,7... | collective-permute-start | bytes 25165832 | tf_op jit(solution)/shard_map/ppermute | solution.py:230
  321.6 191.3 %collective-permute-start.22 = (bf16[4096,1024]{1,0:T(8,128)(2,1)}, bf16[4096,1024]{1,0:T(8,128)(2,1)}, u32[]{:S(2)}, u32[]{:S(2)}) collective-permute-start(bf16[4096,1024]{1,0:T(8,128)(2,1)} %pad_maximum_fusion.refs_2_), channel_id=1, source_target_pairs={{0,1},{1,0},{2,3},{3,2},{24,25},{25,24},{26,27},{27,26},{4,5},{5,4... | collective-permute-start | bytes 25165832 | tf_op jit(solution)/shard_map/ppermute | solution.py:230
  332.4 0.8 collective-permute-start.20
  333.2 10.1 %copy-start.3 = (bf16[128,8192]{1,0:T(8,128)(2,1)}, bf16[128,8192]{1,0:T(8,128)(2,1)S(1)}, u32[]{:S(2)}) copy-start(bf16[128,8192]{1,0:T(8,128)(2,1)S(1)} %collective-permute-done.20.x_ref) | copy-start | bytes 6291460
  333.2 3.2 collective-permute-start.21
  512.9 95.6 %collective-permute-start.26 = (bf16[4096,1024]{1,0:T(8,128)(2,1)}, bf16[4096,1024]{1,0:T(8,128)(2,1)}, u32[]{:S(2)}, u32[]{:S(2)}) collective-permute-start(bf16[4096,1024]{1,0:T(8,128)(2,1)} %collective-permute-done.23.refs_4_), channel_id=1, source_target_pairs={{0,1},{1,0},{2,3},{3,2},{24,25},{25,24},{26,27},{27,26},{4,5},{5,4... | collective-permute-start | bytes 25165832 | tf_op jit(solution)/shard_map/ppermute | solution.py:230
  515.6 0.8 collective-permute-start.24
  516.4 12.7 %copy-start.2 = (bf16[128,8192]{1,0:T(8,128)(2,1)}, bf16[128,8192]{1,0:T(8,128)(2,1)S(1)}, u32[]{:S(2)}) copy-start(bf16[128,8192]{1,0:T(8,128)(2,1)S(1)} %collective-permute-done.24.x_ref) | copy-start | bytes 6291460
  516.4 5.9 collective-permute-start.25
